TPU v7x, 512 devices: a whole 4x4x16 slice. The times are simulated.
512 devices in a mesh: dp: 16 (over y_hi, x, core), expert: 32 (over y_lo, z).
Axes of the slice: x: 4, y: 4 (y_hi: 2, y_lo: 2; y = y_hi * 2 + y_lo), z: 16, core: 2. Of those that a mesh axis runs over, the one named last changes fastest.
Arguments:
- tokens: bfloat16 [8192, 5120], P(('dp', 'expert')), may hold values from -6 to 6
- out_grad: bfloat16 [8192, 5120], P(('dp', 'expert')), may hold values from -6 to 6
- expert_index: int32 [8192, 2], P(('dp', 'expert')), may hold values from 0 to 3, as said below
- slot: int32 [8192, 2], P(('dp', 'expert')), may hold values from -1 to 9, as said below
- gate: bfloat16 [8192, 2], P(('dp', 'expert')), may hold values from 0.19921875 to 1
- w_gate: bfloat16 [32, 5120, 128], P('expert'), may hold values from -0.078125 to 0.078125
- w_up: bfloat16 [32, 5120, 128], P('expert'), may hold values from -0.078125 to 0.078125
- w_down: bfloat16 [32, 5120, 128], P('expert'), may hold values from -0.1875 to 0.1875
Outputs:
- input_grad: bfloat16 [8192, 5120], P(('dp', 'expert'))
- grad_gate: bfloat16 [32, 5120, 128], P('expert', 'dp')
- grad_up: bfloat16 [32, 5120, 128], P('expert', 'dp')
- grad_down: bfloat16 [32, 5120, 128], P('expert', 'dp')
Inputs may be any that keep to these rules, and one draw needn't show every extreme that they name: `expert_index`: each row names 2 different experts. `slot`: within the 16 tokens of one device, the routes to one expert, taken in order of token and then route, get slots 0, 1, 2 and so on; routes past the capacity get -1. In every draw some expert is full on every device.
All inputs are finite; a program needn't handle non-finite values.
Results may differ from a plain program's by a relative error of at most 0.017.
Values may be sent and summed in bfloat16 or wider, within the bound.
No kernel may reach another device: no remote copies, remote signals or barrier semaphores. Data moves between devices by JAX's collectives and lax.ppermute only.
A program may use at most 64 MiB of HBM per device.

v0:
```python
import jax
import jax.numpy as jnp
from jax import lax
from jax.sharding import PartitionSpec as P

WINDOW_EXPERTS = 4
SLOT_CAPACITY = 10


def slot_tables(expert_index, slot, gate):
    flat = jnp.where(
        slot >= 0, expert_index * SLOT_CAPACITY + slot, WINDOW_EXPERTS * SLOT_CAPACITY
    ).reshape(-1)
    count = WINDOW_EXPERTS * SLOT_CAPACITY
    tok_ids = jnp.repeat(jnp.arange(expert_index.shape[0], dtype=jnp.int32), expert_index.shape[1])
    slot_tok = jnp.zeros((count + 1,), jnp.int32).at[flat].set(tok_ids)[:-1]
    capacity_gate_weight = (
        jnp.zeros((count + 1,), jnp.float32).at[flat].set(gate.reshape(-1).astype(jnp.float32))[:-1]
    )
    live = jnp.zeros((count + 1,), jnp.float32).at[flat].set(1.0)[:-1]
    return (flat, slot_tok, capacity_gate_weight, live)


def reduce_weights(stacked):
    summed = lax.psum_scatter(stacked.astype(jnp.bfloat16), "dp", scatter_dimension=1, tiled=True)
    return summed


def local(tokens, out_grad, expert_index, slot, gate, w_gate, w_up, w_down):
    tok = tokens.shape[0]
    width = tokens.shape[1]
    sources = lax.axis_size("expert")
    split = sources // WINDOW_EXPERTS
    flat, slot_tok, capacity_gate_weight, live = slot_tables(expert_index, slot, gate)
    live_rows = live[:, None].astype(jnp.bfloat16)
    xsend = (tokens[slot_tok] * live_rows).reshape(WINDOW_EXPERTS, SLOT_CAPACITY, width)
    xsend = jnp.repeat(xsend, split, axis=0)
    gsend = (out_grad[slot_tok].astype(jnp.float32) * capacity_gate_weight[:, None]).astype(
        jnp.bfloat16
    )
    gsend = jnp.repeat(gsend.reshape(WINDOW_EXPERTS, SLOT_CAPACITY, width), split, axis=0)
    xrecv, grecv = (
        lax.all_to_all(xsend, "expert", split_axis=0, concat_axis=0, tiled=True),
        lax.all_to_all(gsend, "expert", split_axis=0, concat_axis=0, tiled=True),
    )
    xrecv = xrecv.reshape(sources * SLOT_CAPACITY, width)
    grecv = grecv.reshape(sources * SLOT_CAPACITY, width)
    weight_g = w_gate[0]
    weight_u = w_up[0]
    weight_d = w_down[0]
    act_a = jnp.dot(xrecv, weight_g, preferred_element_type=jnp.float32)
    act_b = jnp.dot(xrecv, weight_u, preferred_element_type=jnp.float32)
    grad_h = jnp.dot(grecv, weight_d, preferred_element_type=jnp.float32)
    sig = jax.nn.sigmoid(act_a)
    silu = act_a * sig
    hidden = (silu * act_b).astype(jnp.bfloat16)
    grad_a = (grad_h * act_b * sig * (1.0 + act_a * (1.0 - sig))).astype(jnp.bfloat16)
    grad_b = (grad_h * silu).astype(jnp.bfloat16)
    contract_rows = (((0,), (0,)), ((), ()))
    stacked = (
        jnp.stack(
            [
                lax.dot_general(xrecv, grad_a, contract_rows, preferred_element_type=jnp.float32),
                lax.dot_general(xrecv, grad_b, contract_rows, preferred_element_type=jnp.float32),
                lax.dot_general(grecv, hidden, contract_rows, preferred_element_type=jnp.float32),
            ]
        )
        .astype(jnp.bfloat16)
        .astype(jnp.float32)
    )
    contract_hidden = (((1,), (1,)), ((), ()))
    partial_rows = lax.dot_general(
        grad_a, weight_g, contract_hidden, preferred_element_type=jnp.float32
    )
    partial_rows = partial_rows + lax.dot_general(
        grad_b, weight_u, contract_hidden, preferred_element_type=jnp.float32
    )
    partial_rows = partial_rows.astype(jnp.bfloat16).reshape(sources, SLOT_CAPACITY, width)
    back = lax.all_to_all(partial_rows, "expert", split_axis=0, concat_axis=0, tiled=True)
    reduced = reduce_weights(stacked)
    summed = jnp.sum(
        back.astype(jnp.float32).reshape(WINDOW_EXPERTS, split, SLOT_CAPACITY, width), axis=1
    )
    summed = jnp.concatenate(
        [summed.reshape(WINDOW_EXPERTS * SLOT_CAPACITY, width), jnp.zeros((1, width), jnp.float32)],
        axis=0,
    )
    input_grad = jnp.sum(summed[flat].reshape(tok, expert_index.shape[1], width), axis=1).astype(
        jnp.bfloat16
    )
    return (input_grad, reduced[0][None], reduced[1][None], reduced[2][None])


def solution(mesh):
    return jax.shard_map(
        local,
        mesh=mesh,
        in_specs=(
            P(("dp", "expert"), None),
            P(("dp", "expert"), None),
            P(("dp", "expert"), None),
            P(("dp", "expert"), None),
            P(("dp", "expert"), None),
            P("expert", None, None),
            P("expert", None, None),
            P("expert", None, None),
        ),
        out_specs=(
            P(("dp", "expert"), None),
            P("expert", "dp", None),
            P("expert", "dp", None),
            P("expert", "dp", None),
        ),
        check_vma=False,
    )
```

profile of v0, /device:TPU:6, one launch (start us, length us, event | category | flops | bytes accessed | tf_op | source)
XLA Modules:
  0.0 776.6 jit_solution(17238559236808101854)
XLA Ops:
  7.2 0.8 compare_select_fusion.2
  8.0 0.1 copy.14
  8.1 0.1 reshape.93
  8.2 0.7 scatter_custom_fusion.2
  8.9 0.1 convert_element_type.47
  9.0 0.1 reshape.136
  9.1 0.7 scatter_custom_fusion
  9.8 2.1 gather_fusion.1
  11.9 0.2 gather.13
  12.1 0.1 broadcast_multiply_fusion
  12.2 2.9 broadcast_in_dim.36
  15.1 16.7 %all-to-all-start.1 = ((bf16[32,10,5120]{2,1,0:T(8,128)(2,1)}), bf16[32,10,5120]{2,1,0:T(8,128)(2,1)}, u32[]{:S(2)}, u32[]{:S(2)}) async-start(bf16[32,10,5120]{2,1,0:T(8,128)(2,1)} %bitcast.43), calls=%async_computation.1 | async-start | bytes 10485760 | tf_op jit(solution)/shard_map/all_to_all | solution.py:43
  31.9 0.1 copy.15
  32.0 0.1 reshape.144
  32.1 0.7 scatter_custom_fusion.1
  32.7 0.1 mul.49
  32.8 0.8 gather_fusion
  33.6 0.1 reshape.104
  33.7 0.1 multiply_convert_fusion
  33.9 227.4 %all-to-all-done.1 = bf16[32,10,5120]{2,1,0:T(8,128)(2,1)} async-done(((bf16[32,10,5120]{2,1,0:T(8,128)(2,1)}), bf16[32,10,5120]{2,1,0:T(8,128)(2,1)}, u32[]{:S(2)}, u32[]{:S(2)}) %all-to-all-start.1) | async-done | bytes 3276832 | tf_op jit(solution)/shard_map/all_to_all | solution.py:43
  261.3 3.0 broadcast_in_dim.34
  264.3 9.7 %all-to-all-start = ((bf16[32,10,5120]{2,1,0:T(8,128)(2,1)}), bf16[32,10,5120]{2,1,0:T(8,128)(2,1)}, u32[]{:S(2)}, u32[]{:S(2)}) async-start(bf16[32,10,5120]{2,1,0:T(8,128)(2,1)} %bitcast.44), calls=%async_computation | async-start | bytes 10485760 | tf_op jit(solution)/shard_map/all_to_all | solution.py:44
  274.0 7.1 reshape.98
  281.1 3.1 fusion.6
  284.2 0.2 copy-done.6
  284.4 1.0 fusion.9
  285.4 217.9 %all-to-all-done = bf16[32,10,5120]{2,1,0:T(8,128)(2,1)} async-done(((bf16[32,10,5120]{2,1,0:T(8,128)(2,1)}), bf16[32,10,5120]{2,1,0:T(8,128)(2,1)}, u32[]{:S(2)}, u32[]{:S(2)}) %all-to-all-start) | async-done | bytes 3276832 | tf_op jit(solution)/shard_map/all_to_all | solution.py:44
  503.3 7.1 reshape.96
  510.4 3.3 multiply_convert_fusion.2
  513.7 1.0 fusion.4
  514.7 2.8 fusion
  517.5 6.9 reshape.99
  524.4 9.7 %all-to-all-start.2 = ((bf16[32,10,5120]{2,1,0:T(8,128)(2,1)}), bf16[32,10,5120]{2,1,0:T(8,128)(2,1)}, u32[]{:S(2)}, u32[]{:S(2)}) async-start(bf16[32,10,5120]{2,1,0:T(8,128)(2,1)} %reshape.99), calls=%async_computation.2 | async-start | bytes 10485760 | tf_op jit(solution)/shard_map/all_to_all | solution.py:79
  534.1 0.2 reduce-scatter.2.cloned.1.call-start
  534.3 3.4 fusion.2
  537.7 1.3 fusion.1
  539.0 0.6 copy-done.5
  539.6 1.3 fusion.3
  540.9 2.2 pad_maximum_fusion
  543.2 103.5 %reduce-scatter.2.cloned.1.call-done = bf16[3,320,128]{2,1,0:T(8,128)(2,1)} async-done(((bf16[3,5120,128]{2,1,0:T(8,128)(2,1)}), bf16[3,320,128]{2,1,0:T(8,128)(2,1)}) %reduce-scatter.2.cloned.1.call-update) | async-done | bytes 245776 | tf_op jit(solution)/shard_map/reduce_scatter | solution.py:25
  646.6 1.7 fusion.23
  648.3 115.0 %all-to-all-done.2 = bf16[32,10,5120]{2,1,0:T(8,128)(2,1)} async-done(((bf16[32,10,5120]{2,1,0:T(8,128)(2,1)}), bf16[32,10,5120]{2,1,0:T(8,128)(2,1)}, u32[]{:S(2)}, u32[]{:S(2)}) %all-to-all-start.2) | async-done | bytes 3276832 | tf_op jit(solution)/shard_map/all_to_all | solution.py:79
  763.3 3.5 convert_reduce_fusion
  766.9 0.1 reshape.102
  767.0 0.1 concatenate.3
  767.1 0.8 gather_fusion.2
  767.8 0.4 reshape.103
  768.2 1.5 reduce_sum.19
  (22 shorter events, 0.1 us)
Async XLA Ops:
  7.2 274.0 %copy-start = (bf16[1,5120,128]{2,1,0:T(8,128)(2,1)S(1)}, bf16[1,5120,128]{2,1,0:T(8,128)(2,1)}, u32[]{:S(2)}) copy-start(bf16[1,5120,128]{2,1,0:T(8,128)(2,1)} %param.13) | copy-start | bytes 3932164
  15.1 16.8 %copy-start.7 = (bf16[16,2]{0,1:T(2,128)(2,1)S(1)}, bf16[16,2]{0,1:T(2,128)(2,1)}, u32[]{:S(2)}) copy-start(bf16[16,2]{0,1:T(2,128)(2,1)} %param.12) | copy-start | bytes 196
  15.1 17.7 %copy-start.4 = (bf16[16,5120]{1,0:T(8,128)(2,1)S(1)}, bf16[16,5120]{1,0:T(8,128)(2,1)}, u32[]{:S(2)}) copy-start(bf16[16,5120]{1,0:T(8,128)(2,1)} %param.9) | copy-start | bytes 491524
  15.1 246.2 %all-to-all-start.1 = ((bf16[32,10,5120]{2,1,0:T(8,128)(2,1)}), bf16[32,10,5120]{2,1,0:T(8,128)(2,1)}, u32[]{:S(2)}, u32[]{:S(2)}) async-start(bf16[32,10,5120]{2,1,0:T(8,128)(2,1)} %bitcast.43), calls=%async_computation.1 | async-start | bytes 10485760 | tf_op jit(solution)/shard_map/all_to_all | solution.py:43
  264.3 239.0 %all-to-all-start = ((bf16[32,10,5120]{2,1,0:T(8,128)(2,1)}), bf16[32,10,5120]{2,1,0:T(8,128)(2,1)}, u32[]{:S(2)}, u32[]{:S(2)}) async-start(bf16[32,10,5120]{2,1,0:T(8,128)(2,1)} %bitcast.44), calls=%async_computation | async-start | bytes 10485760 | tf_op jit(solution)/shard_map/all_to_all | solution.py:44
  281.1 3.1 copy-start.2
  281.1 3.3 copy-start.6
  524.4 238.9 %all-to-all-start.2 = ((bf16[32,10,5120]{2,1,0:T(8,128)(2,1)}), bf16[32,10,5120]{2,1,0:T(8,128)(2,1)}, u32[]{:S(2)}, u32[]{:S(2)}) async-start(bf16[32,10,5120]{2,1,0:T(8,128)(2,1)} %reshape.99), calls=%async_computation.2 | async-start | bytes 10485760 | tf_op jit(solution)/shard_map/all_to_all | solution.py:79
  534.1 112.6 %reduce-scatter.2.cloned.1.call-start = ((), (), s32[]{:S(2)}) async-start(), calls=%async_computation.4 | async-start | bytes 4177920 | tf_op jit(solution)/shard_map/reduce_scatter | solution.py:25
  534.3 3.4 copy-start.3
  537.7 1.9 copy-start.5
  767.0 2.8 copy-start.1
Sparse Core Ops, SparseCore 0:
  543.3 103.3 reduce-scatter.1
where the time goes:
time: 781 us; the launch traced here: 777 us
  waiting for transfers between devices  664 us (85%)
  local copies, waits for them, and re-layouts  36.6 us (5%)
  starting transfers between devices  36.4 us (5%)
  matrix products  17.1 us (2%)
  between operations  14.3 us (2%)
  other arithmetic  8.35 us (1%)
    all_to_all x1, waiting for transfers between devices, local(): lax.all_to_all(xsend, 'expert', split_axis=0, concat_axis=0, tiled=True)  227 us
    all_to_all x1, waiting for transfers between devices, local(): lax.all_to_all(gsend, 'expert', split_axis=0, concat_axis=0, tiled=True)  218 us
    all_to_all x1, waiting for transfers between devices, local(): lax.all_to_all(partial_rows, 'expert', split_axis=0, concat_axis=0, tiled...  115 us
    reduce_scatter x1, waiting for transfers between devices, reduce_weights(): lax.psum_scatter(stacked.astype(jnp.bfloat16), 'dp', scatter_dimension=1,...  103 us
    all_to_all x1, starting transfers between devices, local(): lax.all_to_all(xsend, 'expert', split_axis=0, concat_axis=0, tiled=True)  16.7 us
  transfers between devices with their start and end apart: 4, of which 4 were waited for; matrix products, arithmetic and copies ran while one was open for 3% of the time, Pallas kernels for 0%

commit v1 on v0

v1 whole, which is shorter than its diff:
```python
import jax
import jax.numpy as jnp
from jax import lax
from jax.sharding import Mesh
from jax.sharding import PartitionSpec as P

WINDOW_EXPERTS = 4
SPLIT = 8
PAD = 128


def route_columns(expert_index, slot, gate):
    experts = jnp.arange(PAD, dtype=jnp.int32)
    hit = (expert_index[:, :, None] == experts) & (slot >= 0)[:, :, None]
    live = jnp.sum(hit.astype(jnp.float32), axis=1)
    weight = jnp.sum(jnp.where(hit, gate[:, :, None].astype(jnp.float32), 0.0), axis=1)
    return live.astype(jnp.bfloat16), weight.astype(jnp.bfloat16)


def local(tokens, out_grad, expert_index, slot, gate, w_gate, w_up, w_down):
    tok, width = tokens.shape
    n_yl, n_z = lax.axis_size("yl"), lax.axis_size("z")
    sources = n_yl * n_z
    n_yh, n_x, n_core = lax.axis_size("yh"), lax.axis_size("x"), lax.axis_size("core")
    hidden = w_gate.shape[2]
    expert = (lax.axis_index("yl") * n_z + lax.axis_index("z")) // SPLIT

    weights = jnp.concatenate([w_gate[0], w_up[0], w_down[0]], axis=1)
    weights_pad = jnp.pad(weights, ((0, PAD), (0, 0)))

    live, weight = route_columns(expert_index, slot, gate)
    send = jnp.concatenate(
        [
            jnp.concatenate([tokens, live], axis=1),
            jnp.concatenate([out_grad, weight], axis=1),
        ],
        axis=0,
    )
    rows = lax.all_gather(send, ("yl", "z"), axis=0, tiled=True)

    mine = (jnp.arange(PAD, dtype=jnp.int32) == expert).astype(jnp.float32)
    routes = jnp.sum(rows[:, width:].astype(jnp.float32) * mine, axis=1)
    routes = routes.reshape(sources, 2, tok, 1)
    live_rows, gate_rows = routes[:, 0], routes[:, 1]

    act = jnp.dot(rows, weights_pad, preferred_element_type=jnp.float32)
    act = act.reshape(sources, 2, tok, 3 * hidden)
    act_a = act[:, 0, :, :hidden]
    act_b = act[:, 0, :, hidden : 2 * hidden]
    grad_h = act[:, 1, :, 2 * hidden :] * gate_rows
    sig = jax.nn.sigmoid(act_a)
    silu = act_a * sig
    is_live = live_rows > 0
    hid = jnp.where(is_live, silu * act_b * gate_rows, 0.0).astype(jnp.bfloat16)
    grad_a = jnp.where(is_live, grad_h * act_b * sig * (1.0 + act_a * (1.0 - sig)), 0.0)
    grad_b = jnp.where(is_live, grad_h * silu, 0.0)
    grad_ab = jnp.concatenate([grad_a, grad_b], axis=2).astype(jnp.bfloat16)

    by_z = grad_ab.reshape(n_yl, n_z, tok, 2 * hidden).transpose(1, 0, 2, 3)
    back = lax.dot_general(
        by_z.reshape(sources * tok, 2 * hidden),
        weights[:, : 2 * hidden],
        (((1,), (1,)), ((), ())),
        preferred_element_type=jnp.float32,
    ).astype(jnp.bfloat16)
    back = lax.psum_scatter(back, "z", scatter_dimension=0, tiled=True)
    input_grad = lax.psum_scatter(back, "yl", scatter_dimension=0, tiled=True)

    upper = jnp.concatenate([grad_ab, jnp.zeros_like(hid)], axis=2)
    lower = jnp.concatenate([jnp.zeros_like(grad_ab), hid], axis=2)
    both = jnp.stack([upper, lower], axis=1).reshape(sources * 2 * tok, 3 * hidden)
    grads = lax.dot_general(
        rows[:, :width], both, (((0,), (0,)), ((), ())), preferred_element_type=jnp.float32
    ).astype(jnp.bfloat16)
    grads = grads.reshape(n_yh, n_x, n_core, -1, 3 * hidden).transpose(2, 1, 0, 3, 4)
    grads = grads.reshape(width, 3 * hidden)
    grads = lax.psum_scatter(grads, "core", scatter_dimension=0, tiled=True)
    grads = lax.psum_scatter(grads, "x", scatter_dimension=0, tiled=True)
    grads = lax.psum_scatter(grads, "yh", scatter_dimension=0, tiled=True)
    return (
        input_grad,
        grads[None, :, :hidden],
        grads[None, :, hidden : 2 * hidden],
        grads[None, :, 2 * hidden :],
    )


def solution(mesh):
    fine = Mesh(mesh.devices.reshape(2, 4, 2, 2, 16), ("yh", "x", "core", "yl", "z"))
    every = P(("yh", "x", "core", "yl", "z"), None)
    slices = P(("yl", "z"), None, None)
    grads = P(("yl", "z"), ("yh", "x", "core"), None)
    return jax.shard_map(
        local,
        mesh=fine,
        in_specs=(every, every, every, every, every, slices, slices, slices),
        out_specs=(every, grads, grads, grads),
        check_vma=False,
    )
```

time: 781 us -> 393 us (0.50)
  waiting for transfers between devices: 664 us -> 345 us
  starting transfers between devices: 36.4 us -> 0.24 us
  local copies, waits for them, and re-layouts: 36.6 us -> 5.16 us
    all_to_all x3 -> x0, waiting for transfers between devices: 560 us -> none  [the longest x1 227 us: local(): lax.all_to_all(xsend, 'expert', split_axis=0, concat_axis=0, tiled=True)]
    all_gather x0 -> x1, waiting for transfers between devices: none -> 157 us  [local(): rows = lax.all_gather(send, ('yl', 'z'), axis=0, tiled=True)]
    reduce_scatter x1 -> x5, waiting for transfers between devices: 103 us -> 189 us  [the longest x1 87.2 us: local(): back = lax.psum_scatter(back, 'z', scatter_dimension=0, tiled=True)]
    all_to_all x3 -> x0, starting transfers between devices: 36.2 us -> none  [the longest x1 16.7 us: local(): lax.all_to_all(xsend, 'expert', split_axis=0, concat_axis=0, tiled=True)]
    reshape x7 -> x1, local copies, waits for them, and re-layouts: 21.7 us -> 0.1 us  [local(): routes = routes.reshape(sources, 2, tok, 1)]
    dot_general x8 -> x3, matrix products: 17.1 us -> 20.8 us  [the longest x1 11 us: local(): act = jnp.dot(rows, weights_pad, preferred_element_type=jnp.float32)]
  transfers between devices with their start and end apart: 4 -> 6, of which waited for: 4 -> 6; matrix products, arithmetic and copies ran while one was open for 3% -> 2% of each run, Pallas kernels for 0% -> 0%
where the time goes in v1:
time: 393 us; the launch traced here: 391 us
  waiting for transfers between devices  345 us (88%)
  matrix products  20.8 us (5%)
  between operations  14.3 us (4%)
  other arithmetic  5.7 us (1%)
  local copies, waits for them, and re-layouts  5.16 us (1%)
    all_gather x1, waiting for transfers between devices, local(): rows = lax.all_gather(send, ('yl', 'z'), axis=0, tiled=True)  157 us
    reduce_scatter x1, waiting for transfers between devices, local(): back = lax.psum_scatter(back, 'z', scatter_dimension=0, tiled=True)  87.2 us
    reduce_scatter x1, waiting for transfers between devices, local(): grads = lax.psum_scatter(grads, 'x', scatter_dimension=0, tiled=True)  33.5 us
    reduce_scatter x1, waiting for transfers between devices, local(): grads = lax.psum_scatter(grads, 'yh', scatter_dimension=0, tiled=True)  27.5 us
    reduce_scatter x1, waiting for transfers between devices, local(): input_grad = lax.psum_scatter(back, 'yl', scatter_dimension=0, tiled=True)  23.9 us
    reduce_scatter x1, waiting for transfers between devices, local(): grads = lax.psum_scatter(grads, 'core', scatter_dimension=0, tiled=True)  16.4 us
    dot_general x1, matrix products, local(): act = jnp.dot(rows, weights_pad, preferred_element_type=jnp.float32)  11 us
  transfers between devices with their start and end apart: 6, of which 6 were waited for; matrix products, arithmetic and copies ran while one was open for 2% of the time, Pallas kernels for 0%

profile of v1, /device:TPU:6, one launch (start us, length us, event | category | flops | bytes accessed | tf_op | source)
XLA Modules:
  0.0 391.4 jit_solution(2568015357559826655)
XLA Ops:
  7.2 0.0 all-gather.2.cloned.1.call-start
  7.2 0.7 broadcast_compare_fusion
  7.9 0.7 convert_element_type.38
  8.6 0.8 convert_reduce_fusion
  9.3 1.7 maximum_maximum_fusion
  11.1 0.0 all-gather.2.cloned.1.call-update
  11.1 0.0 reduce-scatter.10.cloned.1.call-start
  11.2 156.5 %all-gather.2.cloned.1.call-done = bf16[1024,5248]{1,0:T(8,128)(2,1)} async-done(((bf16[32,5248]{1,0:T(8,128)(2,1)}), bf16[1024,5248]{1,0:T(8,128)(2,1)}) %all-gather.2.cloned.1.call-update) | async-done | bytes 10747920 | tf_op jit(solution)/shard_map/all_gather | solution.py:39
  167.7 1.2 multiply_reduce_fusion
  168.9 0.1 reshape.62
  169.1 0.0 slice-start
  169.1 0.0 slice-start.1
  169.1 0.0 slice-start.2
  169.1 11.0 %fusion.10 = f32[1024,384]{1,0:T(8,128)S(1)} fusion(bf16[1024,5248]{1,0:T(8,128)(2,1)} %all-gather.2.cloned.1.call-done, bf16[5120,128]{1,0:T(8,128)(2,1)} %bitcast.148, bf16[5120,128]{1,0:T(8,128)(2,1)} %bitcast.133, bf16[5120,128]{1,0:T(8,128)(2,1)} %bitcast.135), kind=kOutput, calls=%fused_computation.10 | convolution fusion | flops 4147347456 | bytes 16252928 | tf_op jit(solution)/shard_map/dot_general | solution.py:46
  180.1 0.2 fusion.32
  180.3 0.1 fusion.25
  180.4 0.1 pad_maximum_fusion
  180.5 0.1 copy.45
  180.6 0.0 slice-done
  180.6 0.0 slice-done.1
  180.6 0.0 slice-done.2
  180.6 6.0 %fusion.5 = bf16[5120,384]{1,0:T(8,128)(2,1)S(1)} fusion(bf16[1024,384]{1,0:T(8,128)(2,1)S(1)} %bitcast.141, bf16[1024,5248]{1,0:T(8,128)(2,1)S(1)} %bitcast.147), kind=kOutput, calls=%fused_computation.7 | convolution fusion | flops 4028497920 | bytes 15204352 | tf_op jit(solution)/shard_map/dot_general | solution.py:72
  186.6 2.3 copy.46
  188.9 0.0 copy-start
  188.9 0.0 reduce-scatter.10.cloned.1.call-update
  188.9 0.0 reduce-scatter.12.cloned.1.call-start
  188.9 16.4 %reduce-scatter.10.cloned.1.call-done = bf16[2560,384]{1,0:T(8,128)(2,1)} async-done(((bf16[5120,384]{1,0:T(8,128)(2,1)}), bf16[2560,384]{1,0:T(8,128)(2,1)}) %reduce-scatter.10.cloned.1.call-update) | async-done | bytes 1966096 | tf_op jit(solution)/shard_map/reduce_scatter | solution.py:77
  205.4 0.0 reduce-scatter.12.cloned.1.call-update
  205.4 0.0 reduce-scatter.6.cloned.1.call-start
  205.5 0.0 copy-start.1
  205.5 0.1 fusion.53
  205.5 0.2 fusion.43
  205.8 0.0 copy-done
  205.9 0.9 copy-done.1
  206.8 3.9 convolution_convert_fusion
  210.7 0.0 reduce-scatter.6.cloned.1.call-update
  210.7 0.0 reduce-scatter.14.cloned.1.call-start
  210.8 33.5 %reduce-scatter.12.cloned.1.call-done = bf16[640,384]{1,0:T(8,128)(2,1)} async-done(((bf16[2560,384]{1,0:T(8,128)(2,1)}), bf16[640,384]{1,0:T(8,128)(2,1)}) %reduce-scatter.12.cloned.1.call-update) | async-done | bytes 491536 | tf_op jit(solution)/shard_map/reduce_scatter | solution.py:78
  244.3 0.0 reduce-scatter.14.cloned.1.call-update
  244.3 0.0 reduce-scatter.8.cloned.1.call-start
  244.4 87.2 %reduce-scatter.6.cloned.1.call-done = bf16[32,5120]{1,0:T(8,128)(2,1)} async-done(((bf16[512,5120]{1,0:T(8,128)(2,1)}), bf16[32,5120]{1,0:T(8,128)(2,1)}) %reduce-scatter.6.cloned.1.call-update) | async-done | bytes 327696 | tf_op jit(solution)/shard_map/reduce_scatter | solution.py:66
  331.5 0.0 reduce-scatter.8.cloned.1.call-update
  331.6 27.5 %reduce-scatter.14.cloned.1.call-done = bf16[320,384]{1,0:T(8,128)(2,1)} async-done(((bf16[640,384]{1,0:T(8,128)(2,1)}), bf16[320,384]{1,0:T(8,128)(2,1)}) %reduce-scatter.14.cloned.1.call-update) | async-done | bytes 245776 | tf_op jit(solution)/shard_map/reduce_scatter | solution.py:79
  359.0 1.7 slice_bitcast_fusion
  360.7 23.9 %reduce-scatter.8.cloned.1.call-done = bf16[16,5120]{1,0:T(8,128)(2,1)} async-done(((bf16[32,5120]{1,0:T(8,128)(2,1)}), bf16[16,5120]{1,0:T(8,128)(2,1)}) %reduce-scatter.8.cloned.1.call-update) | async-done | bytes 163856 | tf_op jit(solution)/shard_map/reduce_scatter | solution.py:67
  (8 shorter events, 0.1 us)
Async XLA Ops:
  7.2 160.5 %all-gather.2.cloned.1.call-start = ((), (), s32[]{:S(2)}) async-start(), calls=%async_computation.5 | async-start | bytes 11083776 | tf_op jit(solution)/shard_map/all_gather | solution.py:39
  11.1 194.3 %reduce-scatter.10.cloned.1.call-start = ((), (), s32[]{:S(2)}) async-start(), calls=%async_computation.8 | async-start | bytes 5898240 | tf_op jit(solution)/shard_map/reduce_scatter | solution.py:77
  169.1 11.5 %slice-start = ((s8[10747904]{0:T(1024)(128)(4,1)}), s8[4194304]{0:T(1024)(128)(4,1)S(1)}, s32[]{:S(2)}) async-start(s8[10747904]{0:T(1024)(128)(4,1)} %bitcast.146), calls=%async_computation.11 | async-start | bytes 8388608
  169.1 11.5 %slice-start.1 = ((s8[10747904]{0:T(1024)(128)(4,1)}), s8[4194304]{0:T(1024)(128)(4,1)S(1)}, s32[]{:S(2)}) async-start(s8[10747904]{0:T(1024)(128)(4,1)} %bitcast.146), calls=%async_computation.12 | async-start | bytes 8388608
  169.1 11.5 %slice-start.2 = ((s8[10747904]{0:T(1024)(128)(4,1)}), s8[2359296]{0:T(1024)(128)(4,1)S(1)}, s32[]{:S(2)}) async-start(s8[10747904]{0:T(1024)(128)(4,1)} %bitcast.146), calls=%async_computation.13 | async-start | bytes 4718592
  188.9 17.0 %copy-start = (bf16[1,5120,128]{2,1,0:T(8,128)(2,1)S(1)}, bf16[1,5120,128]{2,1,0:T(8,128)(2,1)}, u32[]{:S(2)}) copy-start(bf16[1,5120,128]{2,1,0:T(8,128)(2,1)} %param.14) | copy-start | bytes 3932164
  188.9 55.4 %reduce-scatter.12.cloned.1.call-start = ((), (), s32[]{:S(2)}) async-start(), calls=%async_computation.9 | async-start | bytes 2457600 | tf_op jit(solution)/shard_map/reduce_scatter | solution.py:78
  205.4 126.1 %reduce-scatter.6.cloned.1.call-start = ((), (), s32[]{:S(2)}) async-start(), calls=%async_computation.6 | async-start | bytes 5570560 | tf_op jit(solution)/shard_map/reduce_scatter | solution.py:66
  205.5 1.3 copy-start.1
  210.7 148.3 %reduce-scatter.14.cloned.1.call-start = ((), (), s32[]{:S(2)}) async-start(), calls=%async_computation.10 | async-start | bytes 737280 | tf_op jit(solution)/shard_map/reduce_scatter | solution.py:79
  244.3 140.3 %reduce-scatter.8.cloned.1.call-start = ((), (), s32[]{:S(2)}) async-start(), calls=%async_computation.7 | async-start | bytes 491520 | tf_op jit(solution)/shard_map/reduce_scatter | solution.py:67
Sparse Core Ops, SparseCore 0:
  11.2 156.4 all-gather.1
  189.0 16.3 reduce-scatter.9
  208.5 35.7 reduce-scatter.11
  247.2 84.2 reduce-scatter.5
  334.4 24.5 reduce-scatter.13
  362.5 22.0 reduce-scatter.7

commit v2 on v1

--- a/solution.py
+++ b/solution.py
@@ -7,6 +7,7 @@
 WINDOW_EXPERTS = 4
 SPLIT = 8
 PAD = 128
+SWAP = [(0, 1), (1, 0)]
 
 
 def route_columns(expert_index, slot, gate):
@@ -17,16 +18,49 @@
     return live.astype(jnp.bfloat16), weight.astype(jnp.bfloat16)
 
 
+def add(*terms):
+    return sum(t.astype(jnp.float32) for t in terms).astype(jnp.bfloat16)
+
+
+def take(array, index, axis):
+    return lax.dynamic_index_in_dim(array, index, axis, keepdims=False)
+
+
+def reduce_weights(grads):
+    n_yh, n_x, n_core = lax.axis_size("yh"), lax.axis_size("x"), lax.axis_size("core")
+    yh, x, core = lax.axis_index("yh"), lax.axis_index("x"), lax.axis_index("core")
+    grads = grads.reshape(n_yh * n_x, n_core, -1, grads.shape[1])
+    other = lax.ppermute(take(grads, 1 - core, 1), "core", SWAP)
+    grads = add(take(grads, core, 1), other)
+
+    grads = grads.reshape(n_yh, n_x, *grads.shape[1:])
+    right = [(i, (i + 1) % n_x) for i in range(n_x)]
+    left = [(i, (i - 1) % n_x) for i in range(n_x)]
+    after = take(grads, (x + 1) % n_x, 1)
+    before = take(grads, (x + n_x - 1) % n_x, 1)
+    across = take(grads, (x + 2) % n_x, 1)
+    own = take(grads, x, 1)
+    from_left = lax.ppermute(jnp.stack([across[0], after[1]]), "x", right)
+    from_right = lax.ppermute(jnp.stack([across[1], before[0]]), "x", left)
+    last_left = lax.ppermute(add(after[0], from_left[0]), "x", right)
+    last_right = lax.ppermute(add(before[1], from_right[0]), "x", left)
+    low = add(own[0], last_left, from_right[1])
+    high = add(own[1], last_right, from_left[1])
+
+    is_low = yh == 0
+    other = lax.ppermute(jnp.where(is_low, high, low), "yh", SWAP)
+    return add(jnp.where(is_low, low, high), other)
+
+
 def local(tokens, out_grad, expert_index, slot, gate, w_gate, w_up, w_down):
     tok, width = tokens.shape
     n_yl, n_z = lax.axis_size("yl"), lax.axis_size("z")
     sources = n_yl * n_z
-    n_yh, n_x, n_core = lax.axis_size("yh"), lax.axis_size("x"), lax.axis_size("core")
     hidden = w_gate.shape[2]
     expert = (lax.axis_index("yl") * n_z + lax.axis_index("z")) // SPLIT
 
     weights = jnp.concatenate([w_gate[0], w_up[0], w_down[0]], axis=1)
-    weights_pad = jnp.pad(weights, ((0, PAD), (0, 0)))
+    weights_pad = lax.optimization_barrier(jnp.pad(weights, ((0, PAD), (0, 0))))
 
     live, weight = route_columns(expert_index, slot, gate)
     send = jnp.concatenate(
@@ -36,7 +70,8 @@
         ],
         axis=0,
     )
-    rows = lax.all_gather(send, ("yl", "z"), axis=0, tiled=True)
+    partner = lax.ppermute(send, "yl", SWAP)
+    rows = lax.all_gather(jnp.concatenate([send, partner], axis=0), "z", axis=0, tiled=True)
 
     mine = (jnp.arange(PAD, dtype=jnp.int32) == expert).astype(jnp.float32)
     routes = jnp.sum(rows[:, width:].astype(jnp.float32) * mine, axis=1)
@@ -56,27 +91,24 @@
     grad_b = jnp.where(is_live, grad_h * silu, 0.0)
     grad_ab = jnp.concatenate([grad_a, grad_b], axis=2).astype(jnp.bfloat16)
 
-    by_z = grad_ab.reshape(n_yl, n_z, tok, 2 * hidden).transpose(1, 0, 2, 3)
     back = lax.dot_general(
-        by_z.reshape(sources * tok, 2 * hidden),
+        grad_ab.reshape(sources * tok, 2 * hidden),
         weights[:, : 2 * hidden],
         (((1,), (1,)), ((), ())),
         preferred_element_type=jnp.float32,
     ).astype(jnp.bfloat16)
-    back = lax.psum_scatter(back, "z", scatter_dimension=0, tiled=True)
-    input_grad = lax.psum_scatter(back, "yl", scatter_dimension=0, tiled=True)
 
     upper = jnp.concatenate([grad_ab, jnp.zeros_like(hid)], axis=2)
     lower = jnp.concatenate([jnp.zeros_like(grad_ab), hid], axis=2)
     both = jnp.stack([upper, lower], axis=1).reshape(sources * 2 * tok, 3 * hidden)
+    back, both = lax.optimization_barrier((back, both))
     grads = lax.dot_general(
         rows[:, :width], both, (((0,), (0,)), ((), ())), preferred_element_type=jnp.float32
     ).astype(jnp.bfloat16)
-    grads = grads.reshape(n_yh, n_x, n_core, -1, 3 * hidden).transpose(2, 1, 0, 3, 4)
-    grads = grads.reshape(width, 3 * hidden)
-    grads = lax.psum_scatter(grads, "core", scatter_dimension=0, tiled=True)
-    grads = lax.psum_scatter(grads, "x", scatter_dimension=0, tiled=True)
-    grads = lax.psum_scatter(grads, "yh", scatter_dimension=0, tiled=True)
+    grads = reduce_weights(grads)
+
+    back = lax.psum_scatter(back, "z", scatter_dimension=0, tiled=True)
+    input_grad = add(back[:tok], lax.ppermute(back[tok:], "yl", SWAP))
     return (
         input_grad,
         grads[None, :, :hidden],

time: 393 us -> 274 us (0.70)
  waiting for transfers between devices: 345 us -> 184 us
  starting transfers between devices: 0.24 us -> 28.6 us
  other arithmetic: 5.7 us -> 19 us
    reduce_scatter x4 -> x0, waiting for transfers between devices: 101 us -> none  [the longest x1 33.5 us: local(): grads = lax.psum_scatter(grads, 'x', scatter_dimension=0, tiled=True)]
    reduce_scatter x1, waiting for transfers between devices: 87.2 us -> 17.2 us  [local(): back = lax.psum_scatter(back, 'z', scatter_dimension=0, tiled=True)]
    ppermute x0 -> x8, waiting for transfers between devices: none -> 38.1 us  [the longest x1 9.23 us: reduce_weights(): from_right = lax.ppermute(jnp.stack([across[1], before[0]]), 'x', left)]
    ppermute x0 -> x8, starting transfers between devices: none -> 28.5 us  [the longest x1 5.5 us: reduce_weights(): last_left = lax.ppermute(add(after[0], from_left[0]), 'x', right)]
    all_gather x1, waiting for transfers between devices: 157 us -> 129 us  [local(): lax.all_gather(jnp.concatenate([send, partner], axis=0), 'z', axis=0, til...]
    concatenate x0 -> x2, other arithmetic: none -> 7.04 us  [the longest x1 5.16 us: local(): weights = jnp.concatenate([w_gate[0], w_up[0], w_down[0]], axis=1)]
    convert_element_type x0 -> x4, other arithmetic: none -> 4.48 us  [add(): return sum((t.astype(jnp.float32) for t in terms)).astype(jnp.bfloat16)]
  transfers between devices with their start and end apart: 6 -> 10, of which waited for: 6 -> 10; matrix products, arithmetic and copies ran while one was open for 2% -> 7% of each run, Pallas kernels for 0% -> 0%
where the time goes in v2:
time: 274 us
  waiting for transfers between devices  184 us (67%)
  starting transfers between devices  28.6 us (10%)
  matrix products  22.1 us (8%)
  other arithmetic  19 us (7%)
  between operations  14.4 us (5%)
  local copies, waits for them, and re-layouts  5.33 us (2%)
    all_gather x1, waiting for transfers between devices, local(): lax.all_gather(jnp.concatenate([send, partner], axis=0), 'z', axis=0, til...  129 us
    reduce_scatter x1, waiting for transfers between devices, local(): back = lax.psum_scatter(back, 'z', scatter_dimension=0, tiled=True)  17.2 us
    dot_general x1, matrix products, local(): act = jnp.dot(rows, weights_pad, preferred_element_type=jnp.float32)  9.82 us
    ppermute x1, waiting for transfers between devices, reduce_weights(): from_right = lax.ppermute(jnp.stack([across[1], before[0]]), 'x', left)  9.23 us
    dot_general x1, matrix products, local(): lax.dot_general(rows[:, :width], both, (((0,), (0,)), ((), ())), preferre...  8.37 us
    ppermute x1, waiting for transfers between devices, local(): partner = lax.ppermute(send, 'yl', SWAP)  8.03 us
    ppermute x1, starting transfers between devices, reduce_weights(): last_left = lax.ppermute(add(after[0], from_left[0]), 'x', right)  5.5 us
  transfers between devices with their start and end apart: 10, of which 10 were waited for; matrix products, arithmetic and copies ran while one was open for 7% of the time, Pallas kernels for 0%

profile of v2, /device:TPU:6, one launch (start us, length us, event | category | flops | bytes accessed | tf_op | source)
XLA Modules:
  0.0 273.6 jit_solution(3165858685775061145)
XLA Ops:
  7.2 0.7 broadcast_compare_fusion
  7.9 0.7 convert_element_type.134
  8.6 0.8 convert_reduce_fusion
  9.3 1.0 maximum_maximum_fusion
  10.3 3.5 %collective-permute-start = (bf16[32,5248]{1,0:T(8,128)(2,1)S(1)}, bf16[32,5248]{1,0:T(8,128)(2,1)S(1)}, u32[]{:S(2)}, u32[]{:S(2)}) collective-permute-start(bf16[32,5248]{1,0:T(8,128)(2,1)S(1)} %maximum_maximum_fusion), channel_id=1, source_target_pairs={{0,16},{16,0},{1,17},{17,1},{2,18},{18,2},{3,19},{19,3},{4,20},{20... | collective-permute-start | bytes 1007624 | tf_op jit(solution)/shard_map/ppermute | solution.py:73
  13.8 8.0 %collective-permute-done = bf16[32,5248]{1,0:T(8,128)(2,1)S(1)} collective-permute-done((bf16[32,5248]{1,0:T(8,128)(2,1)S(1)}, bf16[32,5248]{1,0:T(8,128)(2,1)S(1)}, u32[]{:S(2)}, u32[]{:S(2)}) %collective-permute-start) | collective-permute-done | bytes 335904 | tf_op jit(solution)/shard_map/ppermute | solution.py:73
  21.9 1.9 pad_maximum_fusion.1
  23.8 5.2 %fusion.9 = bf16[5248,384]{1,0:T(8,128)(2,1)} fusion(bf16[5120,128]{1,0:T(8,128)(2,1)} %bitcast.189, bf16[5120,128]{1,0:T(8,128)(2,1)} %bitcast.181, bf16[5120,128]{1,0:T(8,128)(2,1)} %bitcast.183), kind=kLoop, calls=%fused_computation.9 | loop fusion | flops 20152320 | bytes 7962624 | tf_op jit(solution)/shard_map/concatenate | solution.py:62
  29.0 129.0 %all-gather.2.cloned.1.call-done = bf16[1024,5248]{1,0:T(8,128)(2,1)} async-done(((bf16[64,5248]{1,0:T(8,128)(2,1)}), bf16[1024,5248]{1,0:T(8,128)(2,1)}) %all-gather.2.cloned.1.call-update) | async-done | bytes 10747920 | tf_op jit(solution)/shard_map/all_gather | solution.py:74
  158.0 1.2 multiply_reduce_fusion
  159.1 0.1 reshape.89
  159.3 0.1 fusion.51
  159.4 9.8 %fusion.54 = f32[1024,384]{1,0:T(8,128)S(1)} fusion(bf16[1024,5248]{1,0:T(8,128)(2,1)} %all-gather.2.cloned.1.call-done, bf16[5248,384]{1,0:T(8,128)(2,1)} %fusion.9), kind=kOutput, calls=%fused_computation.106 | convolution fusion | flops 4127195136 | bytes 16351232 | tf_op jit(solution)/shard_map/dot_general | solution.py:81
  169.2 1.1 copy-done.3
  170.4 0.1 mul.77
  170.5 0.1 gt.20
  170.6 0.2 fusion.42
  170.8 3.9 %convolution_convert_fusion = bf16[512,5120]{1,0:T(8,128)(2,1)} fusion(bf16[5120,128]{1,0:T(8,128)(2,1)S(1)} %bitcast.182, bf16[5120,128]{1,0:T(8,128)(2,1)S(1)} %bitcast.184, bf16[512,128]{1,0:T(8,128)(2,1)S(1)} %get-tuple-element.28, bf16[512,128]{1,0:T(8,128)(2,1)S(1)} %get-tuple-element.27), kind=kOutput, calls=%fused_computation.6 | convolution fusion | flops 1350565888 | bytes 8126464 | tf_op jit(solution)/shard_map/dot_general | solution.py:94
  174.7 1.4 fusion.31
  176.1 0.1 fusion.21
  176.2 0.1 pad_maximum_fusion
  176.3 8.4 %fusion.5 = bf16[5120,384]{1,0:T(8,128)(2,1)S(1)} fusion(bf16[1024,384]{1,0:T(8,128)(2,1)S(1)} %bitcast.190, bf16[1024,5248]{1,0:T(8,128)(2,1)} %all-gather.2.cloned.1.call-done), kind=kOutput, calls=%fused_computation.7 | convolution fusion | flops 4028497920 | bytes 15204352 | tf_op jit(solution)/shard_map/dot_general | solution.py:105
  184.7 1.9 copy-done.2
  186.6 0.2 dynamic-slice_bitcast_fusion
  186.8 1.9 collective-permute-start.2
  188.8 4.0 %collective-permute-done.2 = bf16[8,320,384]{2,1,0:T(8,128)(2,1)} collective-permute-done((bf16[8,320,384]{2,1,0:T(8,128)(2,1)S(1)}, bf16[8,320,384]{2,1,0:T(8,128)(2,1)}, u32[]{:S(2)}, u32[]{:S(2)}) %collective-permute-start.2) | collective-permute-done | bytes 1966112 | tf_op jit(solution)/shard_map/ppermute | solution.py:33
  192.8 2.6 fusion.10
  195.4 0.1 dynamic-slice_bitcast_fusion.6
  195.6 2.8 %collective-permute-start.5 = (bf16[2,320,384]{2,1,0:T(8,128)(2,1)S(1)}, bf16[2,320,384]{2,1,0:T(8,128)(2,1)S(1)}, u32[]{:S(2)}, u32[]{:S(2)}) collective-permute-start(bf16[2,320,384]{2,1,0:T(8,128)(2,1)S(1)} %pad_maximum_fusion.3), channel_id=1, source_target_pairs={{0,192},{64,0},{128,64},{192,128},{1,193},{65,1},{129,65},{193,129... | collective-permute-start | bytes 1474568 | tf_op jit(solution)/shard_map/ppermute | solution.py:44
  198.4 0.1 pad_maximum_fusion.2
  198.4 4.3 %collective-permute-start.3 = (bf16[2,320,384]{2,1,0:T(8,128)(2,1)S(1)}, bf16[2,320,384]{2,1,0:T(8,128)(2,1)S(1)}, u32[]{:S(2)}, u32[]{:S(2)}) collective-permute-start(bf16[2,320,384]{2,1,0:T(8,128)(2,1)S(1)} %pad_maximum_fusion.2), channel_id=1, source_target_pairs={{0,64},{64,128},{128,192},{192,0},{1,65},{65,129},{129,193},{193,1... | collective-permute-start | bytes 1474568 | tf_op jit(solution)/shard_map/ppermute | solution.py:43
  202.7 9.2 %collective-permute-done.5 = bf16[2,320,384]{2,1,0:T(8,128)(2,1)S(1)} collective-permute-done((bf16[2,320,384]{2,1,0:T(8,128)(2,1)S(1)}, bf16[2,320,384]{2,1,0:T(8,128)(2,1)S(1)}, u32[]{:S(2)}, u32[]{:S(2)}) %collective-permute-start.5) | collective-permute-done | bytes 491552 | tf_op jit(solution)/shard_map/ppermute | solution.py:44
  212.0 1.3 collective-permute-done.3
  213.3 0.1 fusion.17
  213.5 5.5 %collective-permute-start.4 = (bf16[320,384]{1,0:T(8,128)(2,1)S(1)}, bf16[320,384]{1,0:T(8,128)(2,1)}, u32[]{:S(2)}, u32[]{:S(2)}) collective-permute-start(bf16[320,384]{1,0:T(8,128)(2,1)S(1)} %get-tuple-element.16), channel_id=1, source_target_pairs={{0,64},{64,128},{128,192},{192,0},{1,65},{65,129},{129,193},{193,1... | collective-permute-start | bytes 737288 | tf_op jit(solution)/shard_map/ppermute | solution.py:45
  219.0 1.9 collective-permute-start.6
  220.9 2.5 collective-permute-done.4
  223.4 5.4 %collective-permute-done.6 = bf16[320,384]{1,0:T(8,128)(2,1)} collective-permute-done((bf16[320,384]{1,0:T(8,128)(2,1)S(1)}, bf16[320,384]{1,0:T(8,128)(2,1)}, u32[]{:S(2)}, u32[]{:S(2)}) %collective-permute-start.6) | collective-permute-done | bytes 245792 | tf_op jit(solution)/shard_map/ppermute | solution.py:46
  228.8 1.3 broadcast_select_fusion
  230.1 4.9 %collective-permute-start.7 = (bf16[320,384]{1,0:T(8,128)(2,1)S(1)}, bf16[320,384]{1,0:T(8,128)(2,1)S(1)}, u32[]{:S(2)}, u32[]{:S(2)}) collective-permute-start(bf16[320,384]{1,0:T(8,128)(2,1)S(1)} %get-tuple-element.10), channel_id=1, source_target_pairs={{0,256},{256,0},{1,257},{257,1},{2,258},{258,2},{3,259},{259,3},{4... | collective-permute-start | bytes 737288 | tf_op jit(solution)/shard_map/ppermute | solution.py:51
  235.1 4.7 %collective-permute-done.7 = bf16[320,384]{1,0:T(8,128)(2,1)S(1)} collective-permute-done((bf16[320,384]{1,0:T(8,128)(2,1)S(1)}, bf16[320,384]{1,0:T(8,128)(2,1)S(1)}, u32[]{:S(2)}, u32[]{:S(2)}) %collective-permute-start.7) | collective-permute-done | bytes 245792 | tf_op jit(solution)/shard_map/ppermute | solution.py:51
  239.7 0.1 add_convert_fusion
  239.8 17.2 %reduce-scatter.2.cloned.1.call-done = bf16[32,5120]{1,0:T(8,128)(2,1)} async-done(((bf16[512,5120]{1,0:T(8,128)(2,1)}), bf16[32,5120]{1,0:T(8,128)(2,1)}) %reduce-scatter.2.cloned.1.call-update) | async-done | bytes 327696 | tf_op jit(solution)/shard_map/reduce_scatter | solution.py:110
  257.0 0.9 slice.125
  258.0 3.7 %collective-permute-start.1 = (bf16[16,5120]{1,0:T(8,128)(2,1)S(1)}, bf16[16,5120]{1,0:T(8,128)(2,1)S(1)}, u32[]{:S(2)}, u32[]{:S(2)}) collective-permute-start(bf16[16,5120]{1,0:T(8,128)(2,1)S(1)} %slice.125), channel_id=1, source_target_pairs={{0,16},{16,0},{1,17},{17,1},{2,18},{18,2},{3,19},{19,3},{4,20},{20... | collective-permute-start | bytes 491528 | tf_op jit(solution)/shard_map/ppermute | solution.py:111
  261.6 0.7 slice_bitcast_fusion.4
  262.3 2.8 %collective-permute-done.1 = bf16[16,5120]{1,0:T(8,128)(2,1)S(1)} collective-permute-done((bf16[16,5120]{1,0:T(8,128)(2,1)S(1)}, bf16[16,5120]{1,0:T(8,128)(2,1)S(1)}, u32[]{:S(2)}, u32[]{:S(2)}) %collective-permute-start.1) | collective-permute-done | bytes 163872 | tf_op jit(solution)/shard_map/ppermute | solution.py:111
  265.2 1.6 add_convert_fusion.1
  (15 shorter events, 0.3 us)
Async XLA Ops:
  7.2 150.8 %all-gather.2.cloned.1.call-start = ((), (), s32[]{:S(2)}) async-start(), calls=%async_computation.1 | async-start | bytes 11419648 | tf_op jit(solution)/shard_map/all_gather | solution.py:74
  10.3 11.5 %collective-permute-start = (bf16[32,5248]{1,0:T(8,128)(2,1)S(1)}, bf16[32,5248]{1,0:T(8,128)(2,1)S(1)}, u32[]{:S(2)}, u32[]{:S(2)}) collective-permute-start(bf16[32,5248]{1,0:T(8,128)(2,1)S(1)} %maximum_maximum_fusion), channel_id=1, source_target_pairs={{0,16},{16,0},{1,17},{17,1},{2,18},{18,2},{3,19},{19,3},{4,20},{20... | collective-permute-start | bytes 1007624 | tf_op jit(solution)/shard_map/ppermute | solution.py:73
  23.8 233.3 %reduce-scatter.2.cloned.1.call-start = ((), (), s32[]{:S(2)}) async-start(), calls=%async_computation.2 | async-start | bytes 5570560 | tf_op jit(solution)/shard_map/reduce_scatter | solution.py:110
  159.4 11.4 %copy-start = (bf16[1,5120,128]{2,1,0:T(8,128)(2,1)S(1)}, bf16[1,5120,128]{2,1,0:T(8,128)(2,1)}, u32[]{:S(2)}) copy-start(bf16[1,5120,128]{2,1,0:T(8,128)(2,1)} %param.14) | copy-start | bytes 3932164
  159.4 11.4 %copy-start.1 = (bf16[1,5120,128]{2,1,0:T(8,128)(2,1)S(1)}, bf16[1,5120,128]{2,1,0:T(8,128)(2,1)}, u32[]{:S(2)}) copy-start(bf16[1,5120,128]{2,1,0:T(8,128)(2,1)} %param.13) | copy-start | bytes 3932164
  169.2 1.1 copy-start.3
  184.7 1.9 copy-start.2
  186.8 6.0 %collective-permute-start.2 = (bf16[8,320,384]{2,1,0:T(8,128)(2,1)S(1)}, bf16[8,320,384]{2,1,0:T(8,128)(2,1)}, u32[]{:S(2)}, u32[]{:S(2)}) collective-permute-start(bf16[8,320,384]{2,1,0:T(8,128)(2,1)S(1)} %dynamic-slice_bitcast_fusion), channel_id=1, source_target_pairs={{0,32},{32,0},{1,33},{33,1},{2,34},{34,2},{3,35},{35,3},{4,36},{36... | collective-permute-start | bytes 5898248 | tf_op jit(solution)/shard_map/ppermute | solution.py:33
  195.6 16.4 %collective-permute-start.5 = (bf16[2,320,384]{2,1,0:T(8,128)(2,1)S(1)}, bf16[2,320,384]{2,1,0:T(8,128)(2,1)S(1)}, u32[]{:S(2)}, u32[]{:S(2)}) collective-permute-start(bf16[2,320,384]{2,1,0:T(8,128)(2,1)S(1)} %pad_maximum_fusion.3), channel_id=1, source_target_pairs={{0,192},{64,0},{128,64},{192,128},{1,193},{65,1},{129,65},{193,129... | collective-permute-start | bytes 1474568 | tf_op jit(solution)/shard_map/ppermute | solution.py:44
  198.4 14.9 %collective-permute-start.3 = (bf16[2,320,384]{2,1,0:T(8,128)(2,1)S(1)}, bf16[2,320,384]{2,1,0:T(8,128)(2,1)S(1)}, u32[]{:S(2)}, u32[]{:S(2)}) collective-permute-start(bf16[2,320,384]{2,1,0:T(8,128)(2,1)S(1)} %pad_maximum_fusion.2), channel_id=1, source_target_pairs={{0,64},{64,128},{128,192},{192,0},{1,65},{65,129},{129,193},{193,1... | collective-permute-start | bytes 1474568 | tf_op jit(solution)/shard_map/ppermute | solution.py:43
  213.5 10.0 %collective-permute-start.4 = (bf16[320,384]{1,0:T(8,128)(2,1)S(1)}, bf16[320,384]{1,0:T(8,128)(2,1)}, u32[]{:S(2)}, u32[]{:S(2)}) collective-permute-start(bf16[320,384]{1,0:T(8,128)(2,1)S(1)} %get-tuple-element.16), channel_id=1, source_target_pairs={{0,64},{64,128},{128,192},{192,0},{1,65},{65,129},{129,193},{193,1... | collective-permute-start | bytes 737288 | tf_op jit(solution)/shard_map/ppermute | solution.py:45
  219.0 9.9 %collective-permute-start.6 = (bf16[320,384]{1,0:T(8,128)(2,1)S(1)}, bf16[320,384]{1,0:T(8,128)(2,1)}, u32[]{:S(2)}, u32[]{:S(2)}) collective-permute-start(bf16[320,384]{1,0:T(8,128)(2,1)S(1)} %get-tuple-element.15), channel_id=1, source_target_pairs={{0,192},{64,0},{128,64},{192,128},{1,193},{65,1},{129,65},{193,129... | collective-permute-start | bytes 737288 | tf_op jit(solution)/shard_map/ppermute | solution.py:46
  230.1 9.6 %collective-permute-start.7 = (bf16[320,384]{1,0:T(8,128)(2,1)S(1)}, bf16[320,384]{1,0:T(8,128)(2,1)S(1)}, u32[]{:S(2)}, u32[]{:S(2)}) collective-permute-start(bf16[320,384]{1,0:T(8,128)(2,1)S(1)} %get-tuple-element.10), channel_id=1, source_target_pairs={{0,256},{256,0},{1,257},{257,1},{2,258},{258,2},{3,259},{259,3},{4... | collective-permute-start | bytes 737288 | tf_op jit(solution)/shard_map/ppermute | solution.py:51
  258.0 7.2 %collective-permute-start.1 = (bf16[16,5120]{1,0:T(8,128)(2,1)S(1)}, bf16[16,5120]{1,0:T(8,128)(2,1)S(1)}, u32[]{:S(2)}, u32[]{:S(2)}) collective-permute-start(bf16[16,5120]{1,0:T(8,128)(2,1)S(1)} %slice.125), channel_id=1, source_target_pairs={{0,16},{16,0},{1,17},{17,1},{2,18},{18,2},{3,19},{19,3},{4,20},{20... | collective-permute-start | bytes 491528 | tf_op jit(solution)/shard_map/ppermute | solution.py:111
Sparse Core Ops, SparseCore 0:
  23.9 134.0 all-gather.1
  176.5 80.5 reduce-scatter.1

commit v3 on v2

v3 whole, which is shorter than its diff:
```python
import jax
import jax.numpy as jnp
from jax import lax
from jax.sharding import Mesh
from jax.sharding import PartitionSpec as P

WINDOW_EXPERTS = 4
SPLIT = 8
PAD = 128
SWAP = [(0, 1), (1, 0)]


def route_columns(expert_index, slot, gate):
    experts = jnp.arange(PAD, dtype=jnp.int32)
    hit = (expert_index[:, :, None] == experts) & (slot >= 0)[:, :, None]
    live = jnp.sum(hit.astype(jnp.float32), axis=1)
    weight = jnp.sum(jnp.where(hit, gate[:, :, None].astype(jnp.float32), 0.0), axis=1)
    return live.astype(jnp.bfloat16), weight.astype(jnp.bfloat16)


def add(*terms):
    return sum(t.astype(jnp.float32) for t in terms).astype(jnp.bfloat16)


def take(array, index, axis):
    return lax.dynamic_index_in_dim(array, index, axis, keepdims=False)


def pair_steps(place):
    return [
        [
            (place(p, c), place(p ^ 1 if (c + step) % 2 == 0 else 3 - p, c))
            for p in range(4)
            for c in range(2)
        ]
        for step in range(2)
    ]


X_RING = ("x", "core"), pair_steps(lambda p, c: p * 2 + c)
Y_RING = ("yh", "core", "yl"), pair_steps(lambda p, c: (p // 2 * 2 + c) * 2 + p % 2)


def pair_sum(ring, own, first, second, across):
    axes, (step1, step2) = ring
    got = lax.ppermute(jnp.stack([first, across]), axes, step1)
    last = lax.ppermute(add(second, got[1]), axes, step2)
    return add(own, got[0], last)


def x_blocks(blocks, axis):
    x, core = lax.axis_index("x"), lax.axis_index("core")
    up = (x + core) % 2 == 0
    after, before = (x + 1) % 4, (x + 3) % 4
    first, second = jnp.where(up, after, before), jnp.where(up, before, after)
    return [take(blocks, at, axis) for at in (x, first, second, (x + 2) % 4)]


def y_blocks(blocks):
    yh, even = lax.axis_index("yh"), lax.axis_index("core") == 0
    cols = blocks.shape[-1] // 2
    here, there = take(blocks, yh, 0), take(blocks, 1 - yh, 0)
    near, far = here[..., cols:], there[..., cols:]
    first, second = jnp.where(even, near, far), jnp.where(even, far, near)
    return [here[..., :cols], first, second, there[..., :cols]]


def reduce_weights(grads):
    n_yh, n_x, n_core = lax.axis_size("yh"), lax.axis_size("x"), lax.axis_size("core")
    core = lax.axis_index("core")
    grads = grads.reshape(n_yh * n_x, n_core, -1, grads.shape[1])
    other = lax.ppermute(take(grads, 1 - core, 1), "core", SWAP)
    grads = add(take(grads, core, 1), other)

    cut = grads.shape[1] // 2
    upper = grads[:, :cut].reshape(n_yh, n_x, cut, -1)
    lower = grads[:, cut:].reshape(n_yh, n_x, cut, -1)
    upper = pair_sum(X_RING, *x_blocks(upper, 1))
    lower = pair_sum(Y_RING, *y_blocks(lower))
    upper = pair_sum(Y_RING, *y_blocks(upper))
    lower = pair_sum(X_RING, *x_blocks(lower, 0))
    return jnp.concatenate([upper, lower], axis=0)


def partner_weights(weights):
    core = lax.axis_index("core")
    half = take(weights.reshape(2, -1, weights.shape[1]), core, 0)
    mine = lax.ppermute(half, "yl", SWAP)
    other = lax.ppermute(mine, "core", SWAP)
    first = core == 0
    return jnp.concatenate([jnp.where(first, mine, other), jnp.where(first, other, mine)], axis=0)


def local(tokens, out_grad, expert_index, slot, gate, w_gate, w_up, w_down):
    tok, width = tokens.shape
    n_yl, n_z = lax.axis_size("yl"), lax.axis_size("z")
    hidden = w_gate.shape[2]
    yl, z = lax.axis_index("yl"), lax.axis_index("z")
    experts = [(row * n_z + z) // SPLIT for row in (yl, 1 - yl)]

    live, weight = route_columns(expert_index, slot, gate)
    send = jnp.concatenate(
        [
            jnp.concatenate([tokens, live], axis=1),
            jnp.concatenate([out_grad, weight], axis=1),
        ],
        axis=0,
    )
    rows = lax.all_gather(send, "z", axis=0, tiled=True)

    own = jnp.concatenate([w_gate[0], w_up[0], w_down[0]], axis=1)
    partner = partner_weights(own)
    weights = jnp.concatenate(
        [w[:, i * hidden : (i + 1) * hidden] for i in range(3) for w in (own, partner)], axis=1
    )
    weights = lax.optimization_barrier(jnp.pad(weights, ((0, PAD), (0, 0))))

    columns = jnp.arange(PAD, dtype=jnp.int32)
    routes = rows[:, width:].astype(jnp.float32)
    routes = jnp.concatenate(
        [
            jnp.broadcast_to(
                jnp.sum(jnp.where(columns == e, routes, 0.0), axis=1, keepdims=True),
                (n_z * 2 * tok, hidden),
            )
            for e in experts
        ],
        axis=1,
    ).reshape(n_z, 2, tok, 2 * hidden)
    live_rows, gate_rows = routes[:, 0], routes[:, 1]

    act = jnp.dot(rows, weights, preferred_element_type=jnp.float32)
    act = act.reshape(n_z, 2, tok, 6 * hidden)
    act_a = act[:, 0, :, : 2 * hidden]
    act_b = act[:, 0, :, 2 * hidden : 4 * hidden]
    grad_h = act[:, 1, :, 4 * hidden :] * gate_rows
    sig = jax.nn.sigmoid(act_a)
    silu = act_a * sig
    is_live = live_rows > 0
    hid = jnp.where(is_live, silu * act_b * gate_rows, 0.0).astype(jnp.bfloat16)
    grad_a = jnp.where(is_live, grad_h * act_b * sig * (1.0 + act_a * (1.0 - sig)), 0.0)
    grad_a = grad_a.astype(jnp.bfloat16)
    grad_b = jnp.where(is_live, grad_h * silu, 0.0).astype(jnp.bfloat16)

    zero = jnp.zeros((n_z, tok, hidden), jnp.bfloat16)
    upper, lower = [], []
    for i in range(2):
        cut = slice(i * hidden, (i + 1) * hidden)
        upper += [grad_a[:, :, cut], grad_b[:, :, cut], zero]
        lower += [zero, zero, hid[:, :, cut]]
    both = jnp.stack([jnp.concatenate(upper, axis=2), jnp.concatenate(lower, axis=2)], axis=1)
    both = both.reshape(n_z * 2 * tok, 6 * hidden)
    back = lax.dot_general(
        jnp.concatenate([grad_a, grad_b], axis=2).reshape(n_z * tok, 4 * hidden),
        weights[:width, : 4 * hidden],
        (((1,), (1,)), ((), ())),
        preferred_element_type=jnp.float32,
    ).astype(jnp.bfloat16)
    back, both = lax.optimization_barrier((back, both))
    grads = lax.dot_general(
        rows[:, :width], both, (((0,), (0,)), ((), ())), preferred_element_type=jnp.float32
    ).astype(jnp.bfloat16)
    grads = reduce_weights(grads)
    input_grad = lax.psum_scatter(back, "z", scatter_dimension=0, tiled=True)
    return (
        input_grad,
        grads[None, :, :hidden],
        grads[None, :, hidden : 2 * hidden],
        grads[None, :, 2 * hidden :],
    )


def solution(mesh):
    fine = Mesh(mesh.devices.reshape(2, 4, 2, 2, 16), ("yh", "x", "core", "yl", "z"))
    every = P(("yh", "x", "core", "yl", "z"), None)
    slices = P(("yl", "z"), None, None)
    grads = P(("yl", "z"), ("yh", "x", "core"), None)
    return jax.shard_map(
        local,
        mesh=fine,
        in_specs=(every, every, every, every, every, slices, slices, slices),
        out_specs=(every, grads, grads, grads),
        check_vma=False,
    )
```

time: 274 us -> 204 us (0.74)
  waiting for transfers between devices: 184 us -> 101 us
  local copies, waits for them, and re-layouts: 5.33 us -> 13.9 us
  other arithmetic: 19 us -> 23.3 us
  matrix products: 22.1 us -> 19.2 us
    all_gather x1, waiting for transfers between devices: 129 us -> 22.2 us  [local(): rows = lax.all_gather(send, 'z', axis=0, tiled=True)]
    ppermute x7 -> x10, waiting for transfers between devices: 34 us -> 68.7 us  [the longest x1 43.1 us: partner_weights(): mine = lax.ppermute(half, 'yl', SWAP)]
    reduce_scatter x1, waiting for transfers between devices: 17.2 us -> 3.17 us  [local(): input_grad = lax.psum_scatter(back, 'z', scatter_dimension=0, tiled=True)]
    concatenate x2, other arithmetic: 7.04 us -> 0.35 us  [the longest x1 0.31 us: local(): jnp.concatenate([w[:, i * hidden:(i + 1) * hidden] for i in range(3) for...]
    convert_element_type x4 -> x9, other arithmetic: 4.48 us -> 9.43 us  [add(): return sum((t.astype(jnp.float32) for t in terms)).astype(jnp.bfloat16)]
    unnamed x8 -> x22, local copies, waits for them, and re-layouts: 3 us -> 6.77 us
    pad x0 -> x1, local copies, waits for them, and re-layouts: none -> 3.66 us  [local(): weights = lax.optimization_barrier(jnp.pad(weights, ((0, PAD), (0, 0))))]
    ppermute x1, waiting for transfers between devices: 4.02 us -> 7.06 us  [reduce_weights(): other = lax.ppermute(take(grads, 1 - core, 1), 'core', SWAP)]
  transfers between devices with their start and end apart: 10 -> 13, of which waited for: 10 -> 10; matrix products, arithmetic and copies ran while one was open for 7% -> 12% of each run, Pallas kernels for 0% -> 0%
where the time goes in v3:
time: 204 us; the launch traced here: 203 us
  waiting for transfers between devices  101 us (50%)
  starting transfers between devices  31 us (15%)
  other arithmetic  23.3 us (11%)
  matrix products  19.2 us (9%)
  between operations  14.6 us (7%)
  local copies, waits for them, and re-layouts  13.9 us (7%)
    ppermute x1, waiting for transfers between devices, partner_weights(): mine = lax.ppermute(half, 'yl', SWAP)  43.1 us
    all_gather x1, waiting for transfers between devices, local(): rows = lax.all_gather(send, 'z', axis=0, tiled=True)  22.2 us
    ppermute x4, starting transfers between devices, pair_sum(): last = lax.ppermute(add(second, got[1]), axes, step2)  12.7 us
    ppermute x4, waiting for transfers between devices, pair_sum(): got = lax.ppermute(jnp.stack([first, across]), axes, step1)  12.2 us
    ppermute x4, starting transfers between devices, pair_sum(): got = lax.ppermute(jnp.stack([first, across]), axes, step1)  10.9 us
    ppermute x4, waiting for transfers between devices, pair_sum(): last = lax.ppermute(add(second, got[1]), axes, step2)  10.8 us
    convert_element_type x9, other arithmetic, add(): return sum((t.astype(jnp.float32) for t in terms)).astype(jnp.bfloat16)  9.43 us
    dot_general x1, matrix products, local(): act = jnp.dot(rows, weights, preferred_element_type=jnp.float32)  8.83 us
  transfers between devices with their start and end apart: 13, of which 10 were waited for; matrix products, arithmetic and copies ran while one was open for 12% of the time, Pallas kernels for 0%

profile of v3, /device:TPU:6, one launch (start us, length us, event | category | flops | bytes accessed | tf_op | source)
XLA Modules:
  0.0 203.1 jit_solution(15764921526248741394)
XLA Ops:
  7.2 0.7 convert_element_type.168
  7.9 0.7 broadcast_compare_fusion
  8.6 0.8 convert_reduce_fusion
  9.3 1.7 maximum_maximum_fusion
  11.1 1.7 fusion.5
  12.9 3.5 %collective-permute-start = (bf16[2560,384]{1,0:T(8,128)(2,1)S(1)}, bf16[2560,384]{1,0:T(8,128)(2,1)}, u32[]{:S(2)}, u32[]{:S(2)}) collective-permute-start(bf16[2560,384]{1,0:T(8,128)(2,1)S(1)} %fusion.5), channel_id=1, source_target_pairs={{0,16},{16,0},{1,17},{17,1},{2,18},{18,2},{3,19},{19,3},{4,20},{20... | collective-permute-start | bytes 5898248 | tf_op jit(solution)/shard_map/ppermute | solution.py:88
  16.4 43.1 %collective-permute-done = bf16[2560,384]{1,0:T(8,128)(2,1)} collective-permute-done((bf16[2560,384]{1,0:T(8,128)(2,1)S(1)}, bf16[2560,384]{1,0:T(8,128)(2,1)}, u32[]{:S(2)}, u32[]{:S(2)}) %collective-permute-start) | collective-permute-done | bytes 1966112 | tf_op jit(solution)/shard_map/ppermute | solution.py:88
  59.4 1.9 collective-permute-start.1
  61.4 1.5 bitcast_dynamic-update-slice_fusion.2
  63.0 2.7 %collective-permute-done.1 = bf16[2560,384]{1,0:T(8,128)(2,1)} collective-permute-done((bf16[2560,384]{1,0:T(8,128)(2,1)}, bf16[2560,384]{1,0:T(8,128)(2,1)}, u32[]{:S(2)}, u32[]{:S(2)}) %collective-permute-start.1) | collective-permute-done | bytes 1966112 | tf_op jit(solution)/shard_map/ppermute | solution.py:89
  65.6 2.5 %broadcast_select_fusion = (bf16[2560,384]{1,0:T(8,128)(2,1)S(1)}, bf16[2560,384]{1,0:T(8,128)(2,1)S(1)}) fusion(bf16[2560,384]{1,0:T(8,128)(2,1)} %collective-permute-done.1, bf16[2560,384]{1,0:T(8,128)(2,1)} %collective-permute-done, pred[]{:T(512)S(6)} %eq.50), kind=kLoop, calls=%fused_computation.17 | loop fusion | flops 1966080 | bytes 7864321 | tf_op jit(solution)/shard_map/jit(_where)/select_n | solution.py:91
  68.2 0.3 fusion.9
  68.5 1.0 copy-done.3
  69.8 0.3 fusion.7
  70.1 0.7 copy-done.4
  71.5 3.7 %pad.4 = bf16[5248,768]{1,0:T(8,128)(2,1)} pad(bf16[5120,768]{1,0:T(8,128)(2,1)S(1)} %fusion.10, bf16[]{:T(256)} %constant.135.clone.1), padding=0_128x0_0 | pad | bytes 15925250 | tf_op jit(solution)/shard_map/jit(_pad)/pad | solution.py:116
  75.1 22.2 %all-gather.2.cloned.1.call-done = bf16[512,5248]{1,0:T(8,128)(2,1)} async-done(((bf16[32,5248]{1,0:T(8,128)(2,1)}), bf16[512,5248]{1,0:T(8,128)(2,1)}) %all-gather.2.cloned.1.call-update) | async-done | bytes 5373968 | tf_op jit(solution)/shard_map/all_gather | solution.py:109
  97.3 1.1 fusion.17
  98.7 8.8 %fusion.61 = f32[512,768]{1,0:T(8,128)S(1)} fusion(bf16[512,5248]{1,0:T(8,128)(2,1)} %all-gather.2.cloned.1.call-done, bf16[5248,768]{1,0:T(8,128)(2,1)} %pad.4), kind=kOutput, calls=%fused_computation.143 | convolution fusion | flops 4127195136 | bytes 15007744 | tf_op jit(solution)/shard_map/dot_general | solution.py:132
  108.7 3.1 %convolution_convert_fusion.1 = bf16[256,5120]{1,0:T(8,128)(2,1)} fusion(bf16[5248,768]{1,0:T(8,128)(2,1)S(1)} %bitcast.213, bf16[256,256]{1,0:T(8,128)(2,1)S(1)} %get-tuple-element.29, bf16[256,256]{1,0:T(8,128)(2,1)S(1)} %get-tuple-element.28), kind=kOutput, calls=%fused_computation.3 | convolution fusion | flops 1344012288 | bytes 8126464 | tf_op jit(solution)/shard_map/dot_general | solution.py:153
  111.7 7.3 %convolution_convert_fusion = bf16[5120,768]{1,0:T(8,128)(2,1)S(1)} fusion(bf16[512,768]{1,0:T(8,128)(2,1)S(1)} %bitcast.230, bf16[512,5248]{1,0:T(8,128)(2,1)} %all-gather.2.cloned.1.call-done), kind=kOutput, calls=%fused_computation | convolution fusion | flops 4030464000 | bytes 13893632 | tf_op jit(solution)/shard_map/dot_general | solution.py:160
  119.0 2.4 %dynamic-slice_bitcast_fusion = bf16[8,320,768]{2,1,0:T(8,128)(2,1)} fusion(bf16[8,2,320,768]{3,2,1,0:T(8,128)(2,1)S(1)} %bitcast.214, s32[]{:T(128)S(6)} %select_n.156), kind=kLoop, calls=%fused_computation.13 | loop fusion | bytes 7864324 | tf_op jit(solution)/shard_map/jit(dynamic_index_in_dim)/squeeze | solution.py:26
  121.5 1.8 copy-done
  123.3 1.9 collective-permute-start.2
  125.2 7.1 %collective-permute-done.2 = bf16[8,320,768]{2,1,0:T(8,128)(2,1)} collective-permute-done((bf16[8,320,768]{2,1,0:T(8,128)(2,1)}, bf16[8,320,768]{2,1,0:T(8,128)(2,1)}, u32[]{:S(2)}, u32[]{:S(2)}) %collective-permute-start.2) | collective-permute-done | bytes 3932192 | tf_op jit(solution)/shard_map/ppermute | solution.py:72
  132.3 4.3 %fusion = bf16[8,320,768]{2,1,0:T(8,128)(2,1)S(1)} fusion(bf16[8,320,768]{2,1,0:T(8,128)(2,1)} %collective-permute-done.2, bf16[8,2,320,768]{3,2,1,0:T(8,128)(2,1)} %bitcast.215, s32[]{:T(128)S(6)} %select_n.148), kind=kLoop, calls=%fused_computation.2 | loop fusion | flops 7864320 | bytes 11796484 | tf_op jit(solution)/shard_map/convert_element_type | solution.py:22
  137.0 1.0 copy-done.1
  138.0 1.1 pad_maximum_fusion.2
  139.1 3.4 %collective-permute-start.7 = (bf16[2,4,160,384]{3,2,1,0:T(8,128)(2,1)}, bf16[2,4,160,384]{3,2,1,0:T(8,128)(2,1)}, u32[]{:S(2)}, u32[]{:S(2)}) collective-permute-start(bf16[2,4,160,384]{3,2,1,0:T(8,128)(2,1)} %pad_maximum_fusion.2), channel_id=1, source_target_pairs={{0,16},{32,304},{16,0},{48,288},{256,272},{288,48},{272,256},{304,... | collective-permute-start | bytes 2949128 | tf_op jit(solution)/shard_map/ppermute | solution.py:46
  142.7 1.0 pad_maximum_fusion.1
  143.7 2.9 %collective-permute-start.3 = (bf16[2,2,160,768]{3,2,1,0:T(8,128)(2,1)}, bf16[2,2,160,768]{3,2,1,0:T(8,128)(2,1)}, u32[]{:S(2)}, u32[]{:S(2)}) collective-permute-start(bf16[2,2,160,768]{3,2,1,0:T(8,128)(2,1)} %pad_maximum_fusion.1), channel_id=1, source_target_pairs={{0,64},{32,224},{64,0},{96,160},{128,192},{160,96},{192,128},{224,... | collective-permute-start | bytes 2949128 | tf_op jit(solution)/shard_map/ppermute | solution.py:46
  146.6 8.9 %collective-permute-done.7 = bf16[2,4,160,384]{3,2,1,0:T(8,128)(2,1)} collective-permute-done((bf16[2,4,160,384]{3,2,1,0:T(8,128)(2,1)}, bf16[2,4,160,384]{3,2,1,0:T(8,128)(2,1)}, u32[]{:S(2)}, u32[]{:S(2)}) %collective-permute-start.7) | collective-permute-done | bytes 983072 | tf_op jit(solution)/shard_map/ppermute | solution.py:46
  155.4 1.2 fusion.11
  156.7 4.6 %collective-permute-start.8 = (bf16[4,160,384]{2,1,0:T(8,128)(2,1)S(1)}, bf16[4,160,384]{2,1,0:T(8,128)(2,1)S(1)}, u32[]{:S(2)}, u32[]{:S(2)}) collective-permute-start(bf16[4,160,384]{2,1,0:T(8,128)(2,1)S(1)} %fusion.11), channel_id=1, source_target_pairs={{0,272},{32,48},{16,256},{48,32},{256,16},{288,304},{272,0},{304,2... | collective-permute-start | bytes 1474568 | tf_op jit(solution)/shard_map/ppermute | solution.py:47
  161.3 1.2 fusion.14
  162.5 2.6 %collective-permute-start.4 = (bf16[2,160,768]{2,1,0:T(8,128)(2,1)S(1)}, bf16[2,160,768]{2,1,0:T(8,128)(2,1)S(1)}, u32[]{:S(2)}, u32[]{:S(2)}) collective-permute-start(bf16[2,160,768]{2,1,0:T(8,128)(2,1)S(1)} %fusion.14), channel_id=1, source_target_pairs={{0,192},{32,96},{64,128},{96,32},{128,64},{160,224},{192,0},{224,1... | collective-permute-start | bytes 1474568 | tf_op jit(solution)/shard_map/ppermute | solution.py:47
  165.1 3.5 %collective-permute-done.8 = bf16[4,160,384]{2,1,0:T(8,128)(2,1)S(1)} collective-permute-done((bf16[4,160,384]{2,1,0:T(8,128)(2,1)S(1)}, bf16[4,160,384]{2,1,0:T(8,128)(2,1)S(1)}, u32[]{:S(2)}, u32[]{:S(2)}) %collective-permute-start.8) | collective-permute-done | bytes 491552 | tf_op jit(solution)/shard_map/ppermute | solution.py:47
  168.6 1.4 fusion.13
  170.0 2.8 %collective-permute-start.9 = (bf16[2,160,384]{2,1,0:T(8,128)(2,1)S(1)}, bf16[2,160,384]{2,1,0:T(8,128)(2,1)S(1)}, u32[]{:S(2)}, u32[]{:S(2)}) collective-permute-start(bf16[2,160,384]{2,1,0:T(8,128)(2,1)S(1)} %pad_maximum_fusion.6), channel_id=1, source_target_pairs={{0,64},{32,224},{64,0},{96,160},{128,192},{160,96},{192,128},{224,... | collective-permute-start | bytes 737288 | tf_op jit(solution)/shard_map/ppermute | solution.py:46
  172.8 2.1 %collective-permute-done.4 = bf16[2,160,768]{2,1,0:T(8,128)(2,1)S(1)} collective-permute-done((bf16[2,160,768]{2,1,0:T(8,128)(2,1)S(1)}, bf16[2,160,768]{2,1,0:T(8,128)(2,1)S(1)}, u32[]{:S(2)}, u32[]{:S(2)}) %collective-permute-start.4) | collective-permute-done | bytes 491552 | tf_op jit(solution)/shard_map/ppermute | solution.py:47
  174.9 1.2 fusion.16
  176.2 1.9 collective-permute-start.5
  178.2 2.8 %collective-permute-start.10 = (bf16[160,384]{1,0:T(8,128)(2,1)S(1)}, bf16[160,384]{1,0:T(8,128)(2,1)S(1)}, u32[]{:S(2)}, u32[]{:S(2)}) collective-permute-start(bf16[160,384]{1,0:T(8,128)(2,1)S(1)} %fusion.49), channel_id=1, source_target_pairs={{0,192},{32,96},{64,128},{96,32},{128,64},{160,224},{192,0},{224,1... | collective-permute-start | bytes 368648 | tf_op jit(solution)/shard_map/ppermute | solution.py:47
  181.0 3.3 %collective-permute-done.5 = bf16[2,160,384]{2,1,0:T(8,128)(2,1)S(1)} collective-permute-done((bf16[2,160,384]{2,1,0:T(8,128)(2,1)S(1)}, bf16[2,160,384]{2,1,0:T(8,128)(2,1)S(1)}, u32[]{:S(2)}, u32[]{:S(2)}) %collective-permute-start.5) | collective-permute-done | bytes 245792 | tf_op jit(solution)/shard_map/ppermute | solution.py:46
  184.4 2.6 %collective-permute-start.6 = (bf16[160,384]{1,0:T(8,128)(2,1)S(1)}, bf16[160,384]{1,0:T(8,128)(2,1)S(1)}, u32[]{:S(2)}, u32[]{:S(2)}) collective-permute-start(bf16[160,384]{1,0:T(8,128)(2,1)S(1)} %fusion.45), channel_id=1, source_target_pairs={{0,272},{32,48},{16,256},{48,32},{256,16},{288,304},{272,0},{304,2... | collective-permute-start | bytes 368648 | tf_op jit(solution)/shard_map/ppermute | solution.py:47
  187.1 5.3 %collective-permute-done.6 = bf16[160,384]{1,0:T(8,128)(2,1)S(1)} collective-permute-done((bf16[160,384]{1,0:T(8,128)(2,1)S(1)}, bf16[160,384]{1,0:T(8,128)(2,1)S(1)}, u32[]{:S(2)}, u32[]{:S(2)}) %collective-permute-start.6) | collective-permute-done | bytes 122912 | tf_op jit(solution)/shard_map/ppermute | solution.py:47
  192.4 0.7 fusion.54
  193.1 3.2 %reduce-scatter.2.cloned.1.call-done = bf16[16,5120]{1,0:T(8,128)(2,1)} async-done(((bf16[256,5120]{1,0:T(8,128)(2,1)}), bf16[16,5120]{1,0:T(8,128)(2,1)}) %reduce-scatter.2.cloned.1.call-update) | async-done | bytes 163856 | tf_op jit(solution)/shard_map/reduce_scatter | solution.py:164
  (54 shorter events, 3.3 us)
Async XLA Ops:
  7.2 90.2 %all-gather.2.cloned.1.call-start = ((), (), s32[]{:S(2)}) async-start(), calls=%async_computation.1 | async-start | bytes 5709824 | tf_op jit(solution)/shard_map/all_gather | solution.py:109
  11.1 185.2 %reduce-scatter.2.cloned.1.call-start = ((), (), s32[]{:S(2)}) async-start(), calls=%async_computation.2 | async-start | bytes 2785280 | tf_op jit(solution)/shard_map/reduce_scatter | solution.py:164
  12.9 46.6 %collective-permute-start = (bf16[2560,384]{1,0:T(8,128)(2,1)S(1)}, bf16[2560,384]{1,0:T(8,128)(2,1)}, u32[]{:S(2)}, u32[]{:S(2)}) collective-permute-start(bf16[2560,384]{1,0:T(8,128)(2,1)S(1)} %fusion.5), channel_id=1, source_target_pairs={{0,16},{16,0},{1,17},{17,1},{2,18},{18,2},{3,19},{19,3},{4,20},{20... | collective-permute-start | bytes 5898248 | tf_op jit(solution)/shard_map/ppermute | solution.py:88
  59.4 6.2 %collective-permute-start.1 = (bf16[2560,384]{1,0:T(8,128)(2,1)}, bf16[2560,384]{1,0:T(8,128)(2,1)}, u32[]{:S(2)}, u32[]{:S(2)}) collective-permute-start(bf16[2560,384]{1,0:T(8,128)(2,1)} %collective-permute-done), channel_id=1, source_target_pairs={{0,32},{32,0},{1,33},{33,1},{2,34},{34,2},{3,35},{35,3},{4,36},{36... | collective-permute-start | bytes 5898248 | tf_op jit(solution)/shard_map/ppermute | solution.py:89
  68.2 1.3 copy-start.3
  69.5 1.3 copy-start.4
  98.7 10.0 %slice-start = ((s8[8060928]{0:T(1024)(128)(4,1)}), s8[4194304]{0:T(1024)(128)(4,1)S(1)}, s32[]{:S(2)}) async-start(s8[8060928]{0:T(1024)(128)(4,1)} %bitcast.212), calls=%async_computation.3 | async-start | bytes 8388608
  98.7 10.0 %slice-start.1 = ((s8[8060928]{0:T(1024)(128)(4,1)}), s8[3866624]{0:T(1024)(128)(4,1)S(1)}, s32[]{:S(2)}) async-start(s8[8060928]{0:T(1024)(128)(4,1)} %bitcast.212), calls=%async_computation.4 | async-start | bytes 7733248
  119.0 4.2 %copy-start = (bf16[5120,768]{1,0:T(8,128)(2,1)}, bf16[5120,768]{1,0:T(8,128)(2,1)S(1)}, u32[]{:S(2)}) copy-start(bf16[5120,768]{1,0:T(8,128)(2,1)S(1)} %convolution_convert_fusion) | copy-start | bytes 23592964
  123.3 9.0 %collective-permute-start.2 = (bf16[8,320,768]{2,1,0:T(8,128)(2,1)}, bf16[8,320,768]{2,1,0:T(8,128)(2,1)}, u32[]{:S(2)}, u32[]{:S(2)}) collective-permute-start(bf16[8,320,768]{2,1,0:T(8,128)(2,1)} %dynamic-slice_bitcast_fusion), channel_id=1, source_target_pairs={{0,32},{32,0},{1,33},{33,1},{2,34},{34,2},{3,35},{35,3},{4,36},{36... | collective-permute-start | bytes 11796488 | tf_op jit(solution)/shard_map/ppermute | solution.py:72
  137.0 1.0 copy-start.1
  139.1 16.3 %collective-permute-start.7 = (bf16[2,4,160,384]{3,2,1,0:T(8,128)(2,1)}, bf16[2,4,160,384]{3,2,1,0:T(8,128)(2,1)}, u32[]{:S(2)}, u32[]{:S(2)}) collective-permute-start(bf16[2,4,160,384]{3,2,1,0:T(8,128)(2,1)} %pad_maximum_fusion.2), channel_id=1, source_target_pairs={{0,16},{32,304},{16,0},{48,288},{256,272},{288,48},{272,256},{304,... | collective-permute-start | bytes 2949128 | tf_op jit(solution)/shard_map/ppermute | solution.py:46
  142.6 12.9 %copy-start.2 = (bf16[4,160,768]{2,1,0:T(8,128)(2,1)S(1)}, bf16[4,160,768]{2,1,0:T(8,128)(2,1)}, u32[]{:S(2)}) copy-start(bf16[4,160,768]{2,1,0:T(8,128)(2,1)} %copy-done.1) | copy-start | bytes 2949124
  143.7 17.6 %collective-permute-start.3 = (bf16[2,2,160,768]{3,2,1,0:T(8,128)(2,1)}, bf16[2,2,160,768]{3,2,1,0:T(8,128)(2,1)}, u32[]{:S(2)}, u32[]{:S(2)}) collective-permute-start(bf16[2,2,160,768]{3,2,1,0:T(8,128)(2,1)} %pad_maximum_fusion.1), channel_id=1, source_target_pairs={{0,64},{32,224},{64,0},{96,160},{128,192},{160,96},{192,128},{224,... | collective-permute-start | bytes 2949128 | tf_op jit(solution)/shard_map/ppermute | solution.py:46
  156.7 11.9 %collective-permute-start.8 = (bf16[4,160,384]{2,1,0:T(8,128)(2,1)S(1)}, bf16[4,160,384]{2,1,0:T(8,128)(2,1)S(1)}, u32[]{:S(2)}, u32[]{:S(2)}) collective-permute-start(bf16[4,160,384]{2,1,0:T(8,128)(2,1)S(1)} %fusion.11), channel_id=1, source_target_pairs={{0,272},{32,48},{16,256},{48,32},{256,16},{288,304},{272,0},{304,2... | collective-permute-start | bytes 1474568 | tf_op jit(solution)/shard_map/ppermute | solution.py:47
  162.5 12.4 %collective-permute-start.4 = (bf16[2,160,768]{2,1,0:T(8,128)(2,1)S(1)}, bf16[2,160,768]{2,1,0:T(8,128)(2,1)S(1)}, u32[]{:S(2)}, u32[]{:S(2)}) collective-permute-start(bf16[2,160,768]{2,1,0:T(8,128)(2,1)S(1)} %fusion.14), channel_id=1, source_target_pairs={{0,192},{32,96},{64,128},{96,32},{128,64},{160,224},{192,0},{224,1... | collective-permute-start | bytes 1474568 | tf_op jit(solution)/shard_map/ppermute | solution.py:47
  170.0 8.1 %collective-permute-start.9 = (bf16[2,160,384]{2,1,0:T(8,128)(2,1)S(1)}, bf16[2,160,384]{2,1,0:T(8,128)(2,1)S(1)}, u32[]{:S(2)}, u32[]{:S(2)}) collective-permute-start(bf16[2,160,384]{2,1,0:T(8,128)(2,1)S(1)} %pad_maximum_fusion.6), channel_id=1, source_target_pairs={{0,64},{32,224},{64,0},{96,160},{128,192},{160,96},{192,128},{224,... | collective-permute-start | bytes 737288 | tf_op jit(solution)/shard_map/ppermute | solution.py:46
  176.2 8.1 %collective-permute-start.5 = (bf16[2,160,384]{2,1,0:T(8,128)(2,1)S(1)}, bf16[2,160,384]{2,1,0:T(8,128)(2,1)S(1)}, u32[]{:S(2)}, u32[]{:S(2)}) collective-permute-start(bf16[2,160,384]{2,1,0:T(8,128)(2,1)S(1)} %pad_maximum_fusion.5), channel_id=1, source_target_pairs={{0,16},{32,304},{16,0},{48,288},{256,272},{288,48},{272,256},{304,... | collective-permute-start | bytes 737288 | tf_op jit(solution)/shard_map/ppermute | solution.py:46
  178.2 8.8 %collective-permute-start.10 = (bf16[160,384]{1,0:T(8,128)(2,1)S(1)}, bf16[160,384]{1,0:T(8,128)(2,1)S(1)}, u32[]{:S(2)}, u32[]{:S(2)}) collective-permute-start(bf16[160,384]{1,0:T(8,128)(2,1)S(1)} %fusion.49), channel_id=1, source_target_pairs={{0,192},{32,96},{64,128},{96,32},{128,64},{160,224},{192,0},{224,1... | collective-permute-start | bytes 368648 | tf_op jit(solution)/shard_map/ppermute | solution.py:47
  184.4 8.0 %collective-permute-start.6 = (bf16[160,384]{1,0:T(8,128)(2,1)S(1)}, bf16[160,384]{1,0:T(8,128)(2,1)S(1)}, u32[]{:S(2)}, u32[]{:S(2)}) collective-permute-start(bf16[160,384]{1,0:T(8,128)(2,1)S(1)} %fusion.45), channel_id=1, source_target_pairs={{0,272},{32,48},{16,256},{48,32},{256,16},{288,304},{272,0},{304,2... | collective-permute-start | bytes 368648 | tf_op jit(solution)/shard_map/ppermute | solution.py:47
Sparse Core Ops, SparseCore 0:
  11.2 86.0 all-gather.1
  125.3 70.8 reduce-scatter.1

commit v4 on v3

v4 whole, which is shorter than its diff:
```python
import jax
import jax.numpy as jnp
from jax import lax
from jax.experimental import pallas as pl
from jax.experimental.pallas import tpu as pltpu
from jax.sharding import Mesh
from jax.sharding import PartitionSpec as P

WINDOW_EXPERTS = 4
SPLIT = 8
PAD = 128
CHUNKS = 5
VMEM_LIMIT = 60 * 1024 * 1024
SWAP = [(0, 1), (1, 0)]


def flat(block):
    return block.reshape(-1, block.shape[-1])


def forward_kernel(experts, rows, weights, back, dab, hid, rows_v, routes_v, w_v, back_v, total, sems):
    n_z, both, chunk = rows_v.shape[1:]
    tok = both // 2
    hidden = hid.shape[1] // 2

    def row_copy(k):
        return pltpu.make_async_copy(
            rows.at[:, :, pl.ds(pl.multiple_of(k * chunk, 128), chunk)], rows_v.at[k], sems.at[0, k]
        )

    def weight_copy(k):
        return pltpu.make_async_copy(
            weights.at[pl.ds(pl.multiple_of(k * chunk, 128), chunk), :], w_v.at[k], sems.at[1, k]
        )

    def back_copy(k):
        return pltpu.make_async_copy(
            back_v.at[k], back.at[:, pl.ds(pl.multiple_of(k * chunk, 128), chunk)], sems.at[2, k]
        )

    route_copy = pltpu.make_async_copy(
        rows.at[:, :, CHUNKS * chunk : CHUNKS * chunk + PAD], routes_v, sems.at[3, 0]
    )

    def start(k, carry):
        row_copy(k).start()
        weight_copy(k).start()
        return carry

    lax.fori_loop(0, CHUNKS, start, 0)
    route_copy.start()
    total[...] = jnp.zeros_like(total)

    def accumulate(k, carry):
        row_copy(k).wait()
        weight_copy(k).wait()
        x_rows = flat(rows_v[k, :, :tok, :])
        g_rows = flat(rows_v[k, :, tok:, :])
        w = w_v[k]
        total[:, : 4 * hidden] += jnp.dot(
            x_rows, w[:, : 4 * hidden], preferred_element_type=jnp.float32
        )
        total[:, 4 * hidden :] += jnp.dot(
            g_rows, w[:, 4 * hidden :], preferred_element_type=jnp.float32
        )
        return carry

    lax.fori_loop(0, CHUNKS, accumulate, 0)
    route_copy.wait()

    live_rows = flat(routes_v[:, :tok, :]).astype(jnp.float32)
    gate_rows = flat(routes_v[:, tok:, :]).astype(jnp.float32)
    lanes = lax.broadcasted_iota(jnp.int32, live_rows.shape, 1)
    for i in range(2):
        mine = lanes == experts[i]
        live = jnp.sum(jnp.where(mine, live_rows, 0.0), axis=1, keepdims=True) > 0
        gate = jnp.sum(jnp.where(mine, gate_rows, 0.0), axis=1, keepdims=True)
        at = 2 * i * hidden
        act_a = total[:, at : at + hidden]
        act_b = total[:, at + hidden : at + 2 * hidden]
        grad_h = total[:, (4 + i) * hidden : (5 + i) * hidden] * gate
        sig = 1.0 / (1.0 + jnp.exp(-act_a))
        silu = act_a * sig
        grad_a = grad_h * act_b * sig * (1.0 + act_a * (1.0 - sig))
        dab[:, at : at + hidden] = jnp.where(live, grad_a, 0.0).astype(dab.dtype)
        dab[:, at + hidden : at + 2 * hidden] = jnp.where(live, grad_h * silu, 0.0).astype(dab.dtype)
        hid[:, i * hidden : (i + 1) * hidden] = jnp.where(live, silu * act_b * gate, 0.0).astype(
            hid.dtype
        )

    def produce(k, carry):
        back_v[k] = lax.dot_general(
            dab[...],
            w_v[k, :, : 4 * hidden],
            (((1,), (1,)), ((), ())),
            preferred_element_type=jnp.float32,
        ).astype(back_v.dtype)
        back_copy(k).start()
        return carry

    lax.fori_loop(0, CHUNKS, produce, 0)

    def finish(k, carry):
        back_copy(k).wait()
        return carry

    lax.fori_loop(0, CHUNKS, finish, 0)


def forward(experts, rows, weights):
    n_z, both, padded = rows.shape
    width, cols = weights.shape
    hidden, chunk, count = cols // 6, width // CHUNKS, n_z * both // 2
    bf16 = jnp.bfloat16
    vmem = pl.BlockSpec(memory_space=pltpu.VMEM)
    hbm = pl.BlockSpec(memory_space=pl.ANY)
    return pl.pallas_call(
        forward_kernel,
        out_shape=(
            jax.ShapeDtypeStruct((count, width), bf16),
            jax.ShapeDtypeStruct((count, 4 * hidden), bf16),
            jax.ShapeDtypeStruct((count, 2 * hidden), bf16),
        ),
        in_specs=[pl.BlockSpec(memory_space=pltpu.SMEM), hbm, hbm],
        out_specs=(hbm, vmem, vmem),
        scratch_shapes=[
            pltpu.VMEM((CHUNKS, n_z, both, chunk), bf16),
            pltpu.VMEM((n_z, both, PAD), bf16),
            pltpu.VMEM((CHUNKS, chunk, cols), bf16),
            pltpu.VMEM((CHUNKS, count, chunk), bf16),
            pltpu.VMEM((count, cols), jnp.float32),
            pltpu.SemaphoreType.DMA((4, CHUNKS)),
        ],
        compiler_params=pltpu.CompilerParams(vmem_limit_bytes=VMEM_LIMIT),
        cost_estimate=pl.CostEstimate(
            flops=2 * count * width * 10 * hidden, bytes_accessed=16_000_000, transcendentals=0
        ),
    )(experts, rows, weights)


def grads_kernel(part, rows, dab, hid, out):
    tok = rows.shape[1] // 2
    hidden = hid.shape[1] // 2
    count, height, _ = out.shape
    reach = -(-height // 128) * 128

    def product(block, left):
        return lax.dot_general(
            flat(block), left, (((0,), (0,)), ((), ())), preferred_element_type=jnp.float32
        ).astype(out.dtype)

    def write(start, skip):
        for n in range(count):
            at = 2 * height * n + start
            from_x = product(rows[:, :tok, at : at + reach], dab[...])
            from_g = product(rows[:, tok:, at : at + reach], hid[...])
            for i in range(2):
                col = 3 * i * hidden
                out[n, :, col : col + 2 * hidden] = from_x[
                    skip : skip + height, 2 * i * hidden : 2 * (i + 1) * hidden
                ]
                out[n, :, col + 2 * hidden : col + 3 * hidden] = from_g[
                    skip : skip + height, i * hidden : (i + 1) * hidden
                ]

    @pl.when(part[0] == 0)
    def _():
        write(0, 0)

    @pl.when(part[0] == 1)
    def _():
        write(2 * height - reach, reach - height)


def weight_grads(part, rows, dab, hid, steps=4, per_step=2):
    n_z, both, padded = rows.shape
    height = (padded - PAD) // (2 * steps * per_step)
    count, cols = dab.shape[0], dab.shape[1] + hid.shape[1]
    return pl.pallas_call(
        grads_kernel,
        grid_spec=pltpu.PrefetchScalarGridSpec(
            num_scalar_prefetch=1,
            grid=(steps,),
            in_specs=[
                pl.BlockSpec((n_z, both, 2 * height * per_step), lambda i, part: (0, 0, i)),
                pl.BlockSpec(dab.shape, lambda i, part: (0, 0)),
                pl.BlockSpec(hid.shape, lambda i, part: (0, 0)),
            ],
            out_specs=pl.BlockSpec((per_step, height, cols), lambda i, part: (i, 0, 0)),
        ),
        out_shape=jax.ShapeDtypeStruct((steps * per_step, height, cols), jnp.bfloat16),
        compiler_params=pltpu.CompilerParams(vmem_limit_bytes=VMEM_LIMIT),
        cost_estimate=pl.CostEstimate(
            flops=count * (padded - PAD) * cols, bytes_accessed=9_000_000, transcendentals=0
        ),
    )(jnp.reshape(part, (1,)).astype(jnp.int32), rows, dab, hid)


def split_kernel(place, keep_a, got_a, keep_b, got_b, out_a, out_b):
    out_a[...] = add(keep_a[...], got_a[...])[None]
    out_b[...] = add(keep_b[...], got_b[...])[None]


def core_sum(keep, got, slots):
    x, core, yh = lax.axis_index("x"), lax.axis_index("core"), lax.axis_index("yh")
    blocks, part, cols = keep.shape
    n_x, half, cut = blocks // 2, cols // 2, part // 2
    up = (x + core) % 2 == 0
    after, before = (x + 1) % 4, (x + 3) % 4
    a_slots = [x, jnp.where(up, after, before), jnp.where(up, before, after), (x + 2) % 4]
    far = jnp.where(core == 0, 1 - yh, yh)
    b_slots = [(yh, 0), (1 - far, 1), (far, 1), (1 - yh, 0)]
    place = [h * n_x + a_slots[s] for s in slots for h in range(2)]
    place += [h * 2 + m for h, _ in [b_slots[s] for s in slots] for m in range(2)]
    place += [c for _, c in [b_slots[s] for s in slots] for m in range(2)]
    place = jnp.stack([jnp.asarray(v, jnp.int32) for v in place])

    in_a = pl.BlockSpec((1, cut, cols), lambda j, p: (p[j], 0, 0))
    in_b = pl.BlockSpec((2, cut, half), lambda j, p: (p[4 + j], 1, p[8 + j]))

    def out(j, p):
        return (j // 2, j % 2, 0, 0)

    return pl.pallas_call(
        split_kernel,
        grid_spec=pltpu.PrefetchScalarGridSpec(
            num_scalar_prefetch=1,
            grid=(4,),
            in_specs=[in_a, in_a, in_b, in_b],
            out_specs=[
                pl.BlockSpec((1, 1, cut, cols), out),
                pl.BlockSpec((1, 2, cut, half), out),
            ],
        ),
        out_shape=[
            jax.ShapeDtypeStruct((2, 2, cut, cols), keep.dtype),
            jax.ShapeDtypeStruct((2, n_x, cut, half), keep.dtype),
        ],
        compiler_params=pltpu.CompilerParams(vmem_limit_bytes=VMEM_LIMIT),
        cost_estimate=pl.CostEstimate(flops=0, bytes_accessed=6_000_000, transcendentals=0),
    )(place, keep, got, keep, got)


def route_columns(expert_index, slot, gate):
    experts = jnp.arange(PAD, dtype=jnp.int32)
    hit = (expert_index[:, :, None] == experts) & (slot >= 0)[:, :, None]
    live = jnp.sum(hit.astype(jnp.float32), axis=1)
    weight = jnp.sum(jnp.where(hit, gate[:, :, None].astype(jnp.float32), 0.0), axis=1)
    return live.astype(jnp.bfloat16), weight.astype(jnp.bfloat16)


def add(*terms):
    return sum(t.astype(jnp.float32) for t in terms).astype(jnp.bfloat16)


def take(array, index, axis):
    return lax.dynamic_index_in_dim(array, index, axis, keepdims=False)


def pair_steps(place):
    return [
        [
            (place(p, c), place(p ^ 1 if (c + step) % 2 == 0 else 3 - p, c))
            for p in range(4)
            for c in range(2)
        ]
        for step in range(2)
    ]


X_RING = ("x", "core"), pair_steps(lambda p, c: p * 2 + c)
Y_RING = ("yh", "core", "yl"), pair_steps(lambda p, c: (p // 2 * 2 + c) * 2 + p % 2)


def pair_sum(ring, own, second, send):
    axes, (step1, step2) = ring
    got = lax.ppermute(send, axes, step1)
    last = lax.ppermute(add(second, got[1]), axes, step2)
    return add(own, got[0], last)


def x_blocks(blocks, axis):
    x, core = lax.axis_index("x"), lax.axis_index("core")
    up = (x + core) % 2 == 0
    after, before = (x + 1) % 4, (x + 3) % 4
    first, second = jnp.where(up, after, before), jnp.where(up, before, after)
    own, first, second, across = [take(blocks, at, axis) for at in (x, first, second, (x + 2) % 4)]
    return own, second, jnp.stack([first, across])


def y_blocks(blocks):
    yh, even = lax.axis_index("yh"), lax.axis_index("core") == 0
    cols = blocks.shape[-1] // 2
    here, there = take(blocks, yh, 0), take(blocks, 1 - yh, 0)
    near, far = here[..., cols:], there[..., cols:]
    first, second = jnp.where(even, near, far), jnp.where(even, far, near)
    return here[..., :cols], second, jnp.stack([first, there[..., :cols]])


def reduce_weights(rows, dab, hid):
    core = lax.axis_index("core")
    got = lax.ppermute(weight_grads(1 - core, rows, dab, hid), "core", SWAP)
    keep = weight_grads(core, rows, dab, hid)
    send_a, send_b = core_sum(keep, got, (1, 3))
    own_a, own_b = core_sum(keep, got, (0, 2))
    upper = pair_sum(X_RING, own_a[0], own_a[1], send_a)
    lower = pair_sum(Y_RING, own_b[0], own_b[1], send_b)
    upper = pair_sum(Y_RING, *y_blocks(upper))
    lower = pair_sum(X_RING, *x_blocks(lower, 0))
    return jnp.concatenate([upper, lower], axis=0)


def partner_weights(weights):
    core = lax.axis_index("core")
    half = take(weights.reshape(2, -1, weights.shape[1]), core, 0)
    mine = lax.ppermute(half, "yl", SWAP)
    other = lax.ppermute(mine, "core", SWAP)
    first = core == 0
    return jnp.concatenate([jnp.where(first, mine, other), jnp.where(first, other, mine)], axis=0)


def local(tokens, out_grad, expert_index, slot, gate, w_gate, w_up, w_down):
    tok, width = tokens.shape
    n_yl, n_z = lax.axis_size("yl"), lax.axis_size("z")
    hidden = w_gate.shape[2]
    yl, z = lax.axis_index("yl"), lax.axis_index("z")
    experts = [(row * n_z + z) // SPLIT for row in (yl, 1 - yl)]

    live, weight = route_columns(expert_index, slot, gate)
    send = jnp.concatenate(
        [
            jnp.concatenate([tokens, live], axis=1),
            jnp.concatenate([out_grad, weight], axis=1),
        ],
        axis=0,
    )
    rows = lax.all_gather(send, "z", axis=0, tiled=True)

    own = jnp.concatenate([w_gate[0], w_up[0], w_down[0]], axis=1)
    partner = partner_weights(own)
    pairs = 2 * hidden
    weights = jnp.concatenate(
        [own[:, :pairs], partner[:, :pairs], own[:, pairs:], partner[:, pairs:]], axis=1
    )

    rows = rows.reshape(n_z, 2 * tok, width + PAD)
    back, dab, hid = forward(jnp.stack(experts).astype(jnp.int32), rows, weights)
    grads = reduce_weights(rows, dab, hid)
    input_grad = lax.psum_scatter(back, "z", scatter_dimension=0, tiled=True)
    return (
        input_grad,
        grads[None, :, :hidden],
        grads[None, :, hidden : 2 * hidden],
        grads[None, :, 2 * hidden :],
    )


def solution(mesh):
    fine = Mesh(mesh.devices.reshape(2, 4, 2, 2, 16), ("yh", "x", "core", "yl", "z"))
    every = P(("yh", "x", "core", "yl", "z"), None)
    slices = P(("yl", "z"), None, None)
    grads = P(("yl", "z"), ("yh", "x", "core"), None)
    return jax.shard_map(
        local,
        mesh=fine,
        in_specs=(every, every, every, every, every, slices, slices, slices),
        out_specs=(every, grads, grads, grads),
        check_vma=False,
    )
```

time: 204 us -> 194 us (0.951)
  Pallas kernels: 0 us -> 32.4 us
  matrix products: 19.2 us -> 0 us
  local copies, waits for them, and re-layouts: 13.9 us -> 5.24 us
  waiting for transfers between devices: 101 us -> 92.4 us
  other arithmetic: 23.3 us -> 17.4 us
    pallas_call x0 -> x5, Pallas kernels: none -> 32.4 us  [the longest x2 11.9 us: weight_grads(): pl.pallas_call(grads_kernel, grid_spec=pltpu.PrefetchScalarGridSpec(num_s...]
    dot_general x3 -> x0, matrix products: 19.2 us -> none  [the longest x1 8.83 us: local(): act = jnp.dot(rows, weights, preferred_element_type=jnp.float32)]
    ppermute x5, waiting for transfers between devices: 19.2 us -> 8.33 us  [the longest x4 7.94 us: pair_sum(): got = lax.ppermute(send, axes, step1)]
    convert_element_type x9 -> x8, other arithmetic: 9.43 us -> 4.15 us  [add(): return sum((t.astype(jnp.float32) for t in terms)).astype(jnp.bfloat16)]
    pad x1 -> x0, local copies, waits for them, and re-layouts: 3.66 us -> none  [local(): weights = lax.optimization_barrier(jnp.pad(weights, ((0, PAD), (0, 0))))]
    reduce_scatter x1, waiting for transfers between devices: 3.17 us -> 6.14 us  [local(): input_grad = lax.psum_scatter(back, 'z', scatter_dimension=0, tiled=True)]
    unnamed x22 -> x11, local copies, waits for them, and re-layouts: 6.77 us -> 3.88 us
    squeeze x3 -> x1, local copies, waits for them, and re-layouts: 2.6 us -> 0.04 us  [take(): return lax.dynamic_index_in_dim(array, index, axis, keepdims=False)]
  transfers between devices with their start and end apart: 13 -> 13, of which waited for: 10 -> 12; matrix products, arithmetic and copies ran while one was open for 12% -> 10% of each run, Pallas kernels for 0% -> 8%
where the time goes in v4:
time: 194 us; the launch traced here: 193 us
  waiting for transfers between devices  92.4 us (48%)
  Pallas kernels  32.4 us (17%)
  starting transfers between devices  31.4 us (16%)
  other arithmetic  17.4 us (9%)
  between operations  14.4 us (7%)
  local copies, waits for them, and re-layouts  5.24 us (3%)
    ppermute x1, waiting for transfers between devices, partner_weights(): mine = lax.ppermute(half, 'yl', SWAP)  42.7 us
    all_gather x1, waiting for transfers between devices, local(): rows = lax.all_gather(send, 'z', axis=0, tiled=True)  23.8 us
    ppermute x4, starting transfers between devices, pair_sum(): last = lax.ppermute(add(second, got[1]), axes, step2)  12.9 us
    pallas_call x2, Pallas kernels, weight_grads(): pl.pallas_call(grads_kernel, grid_spec=pltpu.PrefetchScalarGridSpec(num_s...  11.9 us
    ppermute x4, starting transfers between devices, pair_sum(): got = lax.ppermute(send, axes, step1)  10.9 us
    pallas_call x1, Pallas kernels, forward(): pl.pallas_call(forward_kernel, out_shape=(jax.ShapeDtypeStruct((count, wi...  10.5 us
    pallas_call x2, Pallas kernels, core_sum(): pl.pallas_call(split_kernel, grid_spec=pltpu.PrefetchScalarGridSpec(num_s...  10.1 us
    ppermute x4, waiting for transfers between devices, pair_sum(): last = lax.ppermute(add(second, got[1]), axes, step2)  9.79 us
  transfers between devices with their start and end apart: 13, of which 12 were waited for; matrix products, arithmetic and copies ran while one was open for 10% of the time, Pallas kernels for 8%

profile of v4, /device:TPU:6, one launch (start us, length us, event | category | flops | bytes accessed | tf_op | source)
XLA Modules:
  0.0 193.2 jit_solution(9087699350376802614)
XLA Ops:
  7.2 0.7 convert_element_type.126
  7.9 0.7 broadcast_compare_fusion
  8.6 0.8 convert_reduce_fusion
  9.3 1.8 maximum_maximum_fusion
  11.2 3.1 %fusion.4 = bf16[2560,384]{1,0:T(8,128)(2,1)} fusion(s32[]{:T(128)S(6)} %select_n.108, bf16[2,2560,128]{2,1,0:T(8,128)(2,1)} %bitcast.77, bf16[2,2560,128]{2,1,0:T(8,128)(2,1)} %bitcast.78, bf16[2,2560,128]{2,1,0:T(8,128)(2,1)} %bitcast.79), kind=kLoop, calls=%fused_computation.9 | loop fusion | flops 5898240 | bytes 5898244 | tf_op jit(solution)/shard_map/jit(dynamic_index_in_dim)/squeeze | solution.py:257
  14.3 3.6 %collective-permute-start = (bf16[2560,384]{1,0:T(8,128)(2,1)}, bf16[2560,384]{1,0:T(8,128)(2,1)}, u32[]{:S(2)}, u32[]{:S(2)}) collective-permute-start(bf16[2560,384]{1,0:T(8,128)(2,1)} %fusion.4), channel_id=1, source_target_pairs={{0,16},{16,0},{1,17},{17,1},{2,18},{18,2},{3,19},{19,3},{4,20},{20... | collective-permute-start | bytes 5898248 | tf_op jit(solution)/shard_map/ppermute | solution.py:316
  17.9 0.6 pad_add_fusion.experts
  18.5 42.7 %collective-permute-done = bf16[2560,384]{1,0:T(8,128)(2,1)} collective-permute-done((bf16[2560,384]{1,0:T(8,128)(2,1)}, bf16[2560,384]{1,0:T(8,128)(2,1)}, u32[]{:S(2)}, u32[]{:S(2)}) %collective-permute-start) | collective-permute-done | bytes 1966112 | tf_op jit(solution)/shard_map/ppermute | solution.py:316
  61.2 1.9 collective-permute-start.1
  63.1 1.2 bitcast_dynamic-update-slice_fusion.2
  64.3 1.3 bitcast_dynamic-update-slice_fusion.1
  65.6 1.6 collective-permute-done.1
  67.2 1.9 %broadcast_select_fusion = (bf16[2560,384]{1,0:T(8,128)(2,1)S(1)}, bf16[2560,384]{1,0:T(8,128)(2,1)S(1)}) fusion(bf16[2560,384]{1,0:T(8,128)(2,1)S(1)} %collective-permute-done.1, bf16[2560,384]{1,0:T(8,128)(2,1)} %collective-permute-done, pred[]{:T(512)S(6)} %eq.39), kind=kLoop, calls=%fused_computation.10 | loop fusion | flops 1966080 | bytes 7864321 | tf_op jit(solution)/shard_map/jit(_where)/select_n | solution.py:319
  69.2 1.8 fusion.1
  71.0 0.1 copy-done.2
  71.0 1.3 bitcast_dynamic-update-slice_fusion
  72.3 1.2 fusion.5.weights
  73.6 23.8 %all-gather.2.cloned.1.call-done = bf16[512,5248]{1,0:T(8,128)(2,1)} async-done(((bf16[32,5248]{1,0:T(8,128)(2,1)}), bf16[512,5248]{1,0:T(8,128)(2,1)}) %all-gather.2.cloned.1.call-update) | async-done | bytes 5373968 | tf_op jit(solution)/shard_map/all_gather | solution.py:337
  97.3 10.5 %shard_map.111 = (bf16[256,5120]{1,0:T(8,128)(2,1)}, bf16[256,512]{1,0:T(8,128)(2,1)}, bf16[256,256]{1,0:T(8,128)(2,1)}) custom-call(s32[2]{0:T(128)} %pad_add_fusion.experts, bf16[16,32,5248]{2,1,0:T(8,128)(2,1)} %bitcast.74, bf16[5120,768]{1,0:T(8,128)(2,1)} %fusion.5.weights), custom_call_target="tpu_custom_call" | custom-call | flops 3355443200 | bytes 16000000 | tf_op jit(solution)/shard_map/pallas_call | solution.py:117
  107.8 6.0 %shard_map.113 = bf16[8,320,768]{2,1,0:T(8,128)(2,1)} custom-call(s32[1]{0:T(128)} %bitcast.19.part, bf16[16,32,5248]{2,1,0:T(8,128)(2,1)} %bitcast.75, bf16[256,512]{1,0:T(8,128)(2,1)} %get-tuple-element.12.dab, bf16[256,256]{1,0:T(8,128)(2,1)} %get-tuple-element.13.hid), custom_call_target="tpu_custom_call" | custom-call | flops 1006632960 | bytes 9000000 | tf_op jit(solution)/shard_map/pallas_call | solution.py:179
  113.8 1.9 collective-permute-start.2
  115.8 0.7 stack.97.place
  116.5 5.9 %shard_map.112.keep_a.keep_b = bf16[8,320,768]{2,1,0:T(8,128)(2,1)} custom-call(s32[1]{0:T(128)} %bitcast.18.part, bf16[16,32,5248]{2,1,0:T(8,128)(2,1)} %bitcast.76, bf16[256,512]{1,0:T(8,128)(2,1)} %get-tuple-element.12.dab, bf16[256,256]{1,0:T(8,128)(2,1)} %get-tuple-element.13.hid), custom_call_target="tpu_custom_call" | custom-call | flops 1006632960 | bytes 9000000 | tf_op jit(solution)/shard_map/pallas_call | solution.py:179
  122.4 0.4 collective-permute-done.2.got_a.got_b
  122.8 5.1 %shard_map.115 = (bf16[2,2,160,768]{3,2,1,0:T(8,128)(2,1)}, bf16[2,4,160,384]{3,2,1,0:T(8,128)(2,1)}) custom-call(s32[12]{0:T(128)} %stack.97.place, bf16[8,320,768]{2,1,0:T(8,128)(2,1)} %shard_map.112.keep_a.keep_b, bf16[8,320,768]{2,1,0:T(8,128)(2,1)} %collective-permute-done.2.got_a.got_b, bf16[8,320,768]{2,1,0:T(8,128)(2,1)} %shard_map.112.keep_a.keep_b, ...), custom_call_target="tpu_custom_call" | custom-call | bytes 6000000 | tf_op jit(solution)/shard_map/pallas_call | solution.py:224
  127.8 3.4 %collective-permute-start.7 = (bf16[2,4,160,384]{3,2,1,0:T(8,128)(2,1)}, bf16[2,4,160,384]{3,2,1,0:T(8,128)(2,1)S(1)}, u32[]{:S(2)}, u32[]{:S(2)}) collective-permute-start(bf16[2,4,160,384]{3,2,1,0:T(8,128)(2,1)} %get-tuple-element.17), channel_id=1, source_target_pairs={{0,16},{32,304},{16,0},{48,288},{256,272},{288,48},{272,256},{304,... | collective-permute-start | bytes 2949128 | tf_op jit(solution)/shard_map/ppermute | solution.py:277
  131.2 2.9 %collective-permute-start.3 = (bf16[2,2,160,768]{3,2,1,0:T(8,128)(2,1)}, bf16[2,2,160,768]{3,2,1,0:T(8,128)(2,1)S(1)}, u32[]{:S(2)}, u32[]{:S(2)}) collective-permute-start(bf16[2,2,160,768]{3,2,1,0:T(8,128)(2,1)} %get-tuple-element.15), channel_id=1, source_target_pairs={{0,64},{32,224},{64,0},{96,160},{128,192},{160,96},{192,128},{224,... | collective-permute-start | bytes 2949128 | tf_op jit(solution)/shard_map/ppermute | solution.py:277
  134.1 0.6 stack.88.place
  134.7 5.0 %shard_map.114 = (bf16[2,2,160,768]{3,2,1,0:T(8,128)(2,1)}, bf16[2,4,160,384]{3,2,1,0:T(8,128)(2,1)}) custom-call(s32[12]{0:T(128)} %stack.88.place, bf16[8,320,768]{2,1,0:T(8,128)(2,1)} %shard_map.112.keep_a.keep_b, bf16[8,320,768]{2,1,0:T(8,128)(2,1)} %collective-permute-done.2.got_a.got_b, bf16[8,320,768]{2,1,0:T(8,128)(2,1)} %shard_map.112.keep_a.keep_b, ...), custom_call_target="tpu_custom_call" | custom-call | bytes 6000000 | tf_op jit(solution)/shard_map/pallas_call | solution.py:224
  139.7 4.3 %collective-permute-done.7 = bf16[2,4,160,384]{3,2,1,0:T(8,128)(2,1)S(1)} collective-permute-done((bf16[2,4,160,384]{3,2,1,0:T(8,128)(2,1)}, bf16[2,4,160,384]{3,2,1,0:T(8,128)(2,1)S(1)}, u32[]{:S(2)}, u32[]{:S(2)}) %collective-permute-start.7) | collective-permute-done | bytes 983072 | tf_op jit(solution)/shard_map/ppermute | solution.py:277
  144.0 1.2 fusion.9
  145.3 4.6 %collective-permute-start.8 = (bf16[4,160,384]{2,1,0:T(8,128)(2,1)S(1)}, bf16[4,160,384]{2,1,0:T(8,128)(2,1)}, u32[]{:S(2)}, u32[]{:S(2)}) collective-permute-start(bf16[4,160,384]{2,1,0:T(8,128)(2,1)S(1)} %fusion.9), channel_id=1, source_target_pairs={{0,272},{32,48},{16,256},{48,32},{256,16},{288,304},{272,0},{304,2... | collective-permute-start | bytes 1474568 | tf_op jit(solution)/shard_map/ppermute | solution.py:278
  150.0 1.2 fusion.8
  151.1 2.6 %collective-permute-start.4 = (bf16[2,160,768]{2,1,0:T(8,128)(2,1)S(1)}, bf16[2,160,768]{2,1,0:T(8,128)(2,1)S(1)}, u32[]{:S(2)}, u32[]{:S(2)}) collective-permute-start(bf16[2,160,768]{2,1,0:T(8,128)(2,1)S(1)} %fusion.8), channel_id=1, source_target_pairs={{0,192},{32,96},{64,128},{96,32},{128,64},{160,224},{192,0},{224,1... | collective-permute-start | bytes 1474568 | tf_op jit(solution)/shard_map/ppermute | solution.py:278
  153.8 3.6 %collective-permute-done.8 = bf16[4,160,384]{2,1,0:T(8,128)(2,1)} collective-permute-done((bf16[4,160,384]{2,1,0:T(8,128)(2,1)S(1)}, bf16[4,160,384]{2,1,0:T(8,128)(2,1)}, u32[]{:S(2)}, u32[]{:S(2)}) %collective-permute-start.8) | collective-permute-done | bytes 491552 | tf_op jit(solution)/shard_map/ppermute | solution.py:278
  157.3 1.4 fusion.6
  158.8 2.8 %collective-permute-start.9 = (bf16[2,160,384]{2,1,0:T(8,128)(2,1)S(1)}, bf16[2,160,384]{2,1,0:T(8,128)(2,1)S(1)}, u32[]{:S(2)}, u32[]{:S(2)}) collective-permute-start(bf16[2,160,384]{2,1,0:T(8,128)(2,1)S(1)} %pad_maximum_fusion.2), channel_id=1, source_target_pairs={{0,64},{32,224},{64,0},{96,160},{128,192},{160,96},{192,128},{224,... | collective-permute-start | bytes 737288 | tf_op jit(solution)/shard_map/ppermute | solution.py:277
  161.5 1.5 collective-permute-done.4
  163.0 0.2 fusion.7
  163.4 1.9 collective-permute-start.5
  165.3 1.6 collective-permute-done.9
  166.9 2.5 %collective-permute-start.10 = (bf16[160,384]{1,0:T(8,128)(2,1)S(1)}, bf16[160,384]{1,0:T(8,128)(2,1)S(1)}, u32[]{:S(2)}, u32[]{:S(2)}) collective-permute-start(bf16[160,384]{1,0:T(8,128)(2,1)S(1)} %fusion.14), channel_id=1, source_target_pairs={{0,192},{32,96},{64,128},{96,32},{128,64},{160,224},{192,0},{224,1... | collective-permute-start | bytes 368648 | tf_op jit(solution)/shard_map/ppermute | solution.py:278
  169.4 2.1 %collective-permute-done.5 = bf16[2,160,384]{2,1,0:T(8,128)(2,1)S(1)} collective-permute-done((bf16[2,160,384]{2,1,0:T(8,128)(2,1)S(1)}, bf16[2,160,384]{2,1,0:T(8,128)(2,1)S(1)}, u32[]{:S(2)}, u32[]{:S(2)}) %collective-permute-start.5) | collective-permute-done | bytes 245792 | tf_op jit(solution)/shard_map/ppermute | solution.py:277
  171.5 3.2 %collective-permute-start.6 = (bf16[160,384]{1,0:T(8,128)(2,1)S(1)}, bf16[160,384]{1,0:T(8,128)(2,1)S(1)}, u32[]{:S(2)}, u32[]{:S(2)}) collective-permute-start(bf16[160,384]{1,0:T(8,128)(2,1)S(1)} %fusion.10), channel_id=1, source_target_pairs={{0,272},{32,48},{16,256},{48,32},{256,16},{288,304},{272,0},{304,2... | collective-permute-start | bytes 368648 | tf_op jit(solution)/shard_map/ppermute | solution.py:278
  174.7 0.2 collective-permute-done.10
  175.0 4.5 %collective-permute-done.6 = bf16[160,384]{1,0:T(8,128)(2,1)S(1)} collective-permute-done((bf16[160,384]{1,0:T(8,128)(2,1)S(1)}, bf16[160,384]{1,0:T(8,128)(2,1)S(1)}, u32[]{:S(2)}, u32[]{:S(2)}) %collective-permute-start.6) | collective-permute-done | bytes 122912 | tf_op jit(solution)/shard_map/ppermute | solution.py:278
  179.5 0.7 fusion.19
  180.2 6.1 %reduce-scatter.2.cloned.1.call-done = bf16[16,5120]{1,0:T(8,128)(2,1)} async-done(((bf16[256,5120]{1,0:T(8,128)(2,1)}), bf16[16,5120]{1,0:T(8,128)(2,1)}) %reduce-scatter.2.cloned.1.call-update) | async-done | bytes 163856 | tf_op jit(solution)/shard_map/reduce_scatter | solution.py:349
  (23 shorter events, 0.5 us)
Async XLA Ops:
  7.2 90.2 %all-gather.2.cloned.1.call-start = ((), (), s32[]{:S(2)}) async-start(), calls=%async_computation.1 | async-start | bytes 5709824 | tf_op jit(solution)/shard_map/all_gather | solution.py:337
  11.1 175.3 %reduce-scatter.2.cloned.1.call-start = ((), (), s32[]{:S(2)}) async-start(), calls=%async_computation.2 | async-start | bytes 2785280 | tf_op jit(solution)/shard_map/reduce_scatter | solution.py:349
  11.1 52.0 %copy-start = (bf16[1,5120,128]{2,1,0:T(8,128)(2,1)S(1)}, bf16[1,5120,128]{2,1,0:T(8,128)(2,1)}, u32[]{:S(2)}) copy-start(bf16[1,5120,128]{2,1,0:T(8,128)(2,1)} %param.13) | copy-start | bytes 3932164
  14.3 50.1 %copy-start.1 = (bf16[1,5120,128]{2,1,0:T(8,128)(2,1)S(1)}, bf16[1,5120,128]{2,1,0:T(8,128)(2,1)}, u32[]{:S(2)}) copy-start(bf16[1,5120,128]{2,1,0:T(8,128)(2,1)} %param.14) | copy-start | bytes 3932164
  14.3 46.9 %collective-permute-start = (bf16[2560,384]{1,0:T(8,128)(2,1)}, bf16[2560,384]{1,0:T(8,128)(2,1)}, u32[]{:S(2)}, u32[]{:S(2)}) collective-permute-start(bf16[2560,384]{1,0:T(8,128)(2,1)} %fusion.4), channel_id=1, source_target_pairs={{0,16},{16,0},{1,17},{17,1},{2,18},{18,2},{3,19},{19,3},{4,20},{20... | collective-permute-start | bytes 5898248 | tf_op jit(solution)/shard_map/ppermute | solution.py:316
  61.2 6.1 %collective-permute-start.1 = (bf16[2560,384]{1,0:T(8,128)(2,1)}, bf16[2560,384]{1,0:T(8,128)(2,1)S(1)}, u32[]{:S(2)}, u32[]{:S(2)}) collective-permute-start(bf16[2560,384]{1,0:T(8,128)(2,1)} %collective-permute-done), channel_id=1, source_target_pairs={{0,32},{32,0},{1,33},{33,1},{2,34},{34,2},{3,35},{35,3},{4,36},{36... | collective-permute-start | bytes 5898248 | tf_op jit(solution)/shard_map/ppermute | solution.py:317
  69.2 1.9 copy-start.2
  113.8 9.0 %collective-permute-start.2 = (bf16[8,320,768]{2,1,0:T(8,128)(2,1)}, bf16[8,320,768]{2,1,0:T(8,128)(2,1)}, u32[]{:S(2)}, u32[]{:S(2)}) collective-permute-start(bf16[8,320,768]{2,1,0:T(8,128)(2,1)} %shard_map.113), channel_id=1, source_target_pairs={{0,32},{32,0},{1,33},{33,1},{2,34},{34,2},{3,35},{35,3},{4,36},{36... | collective-permute-start | bytes 11796488 | tf_op jit(solution)/shard_map/ppermute | solution.py:302
  127.8 16.2 %collective-permute-start.7 = (bf16[2,4,160,384]{3,2,1,0:T(8,128)(2,1)}, bf16[2,4,160,384]{3,2,1,0:T(8,128)(2,1)S(1)}, u32[]{:S(2)}, u32[]{:S(2)}) collective-permute-start(bf16[2,4,160,384]{3,2,1,0:T(8,128)(2,1)} %get-tuple-element.17), channel_id=1, source_target_pairs={{0,16},{32,304},{16,0},{48,288},{256,272},{288,48},{272,256},{304,... | collective-permute-start | bytes 2949128 | tf_op jit(solution)/shard_map/ppermute | solution.py:277
  131.2 18.7 %collective-permute-start.3 = (bf16[2,2,160,768]{3,2,1,0:T(8,128)(2,1)}, bf16[2,2,160,768]{3,2,1,0:T(8,128)(2,1)S(1)}, u32[]{:S(2)}, u32[]{:S(2)}) collective-permute-start(bf16[2,2,160,768]{3,2,1,0:T(8,128)(2,1)} %get-tuple-element.15), channel_id=1, source_target_pairs={{0,64},{32,224},{64,0},{96,160},{128,192},{160,96},{192,128},{224,... | collective-permute-start | bytes 2949128 | tf_op jit(solution)/shard_map/ppermute | solution.py:277
  144.0 19.0 %copy-start.3 = (bf16[2,2,160,768]{3,2,1,0:T(8,128)(2,1)S(1)}, bf16[2,2,160,768]{3,2,1,0:T(8,128)(2,1)}, u32[]{:S(2)}) copy-start(bf16[2,2,160,768]{3,2,1,0:T(8,128)(2,1)} %get-tuple-element.14) | copy-start | bytes 2949124
  145.3 12.0 %collective-permute-start.8 = (bf16[4,160,384]{2,1,0:T(8,128)(2,1)S(1)}, bf16[4,160,384]{2,1,0:T(8,128)(2,1)}, u32[]{:S(2)}, u32[]{:S(2)}) collective-permute-start(bf16[4,160,384]{2,1,0:T(8,128)(2,1)S(1)} %fusion.9), channel_id=1, source_target_pairs={{0,272},{32,48},{16,256},{48,32},{256,16},{288,304},{272,0},{304,2... | collective-permute-start | bytes 1474568 | tf_op jit(solution)/shard_map/ppermute | solution.py:278
  151.1 11.9 %collective-permute-start.4 = (bf16[2,160,768]{2,1,0:T(8,128)(2,1)S(1)}, bf16[2,160,768]{2,1,0:T(8,128)(2,1)S(1)}, u32[]{:S(2)}, u32[]{:S(2)}) collective-permute-start(bf16[2,160,768]{2,1,0:T(8,128)(2,1)S(1)} %fusion.8), channel_id=1, source_target_pairs={{0,192},{32,96},{64,128},{96,32},{128,64},{160,224},{192,0},{224,1... | collective-permute-start | bytes 1474568 | tf_op jit(solution)/shard_map/ppermute | solution.py:278
  158.8 8.1 %collective-permute-start.9 = (bf16[2,160,384]{2,1,0:T(8,128)(2,1)S(1)}, bf16[2,160,384]{2,1,0:T(8,128)(2,1)S(1)}, u32[]{:S(2)}, u32[]{:S(2)}) collective-permute-start(bf16[2,160,384]{2,1,0:T(8,128)(2,1)S(1)} %pad_maximum_fusion.2), channel_id=1, source_target_pairs={{0,64},{32,224},{64,0},{96,160},{128,192},{160,96},{192,128},{224,... | collective-permute-start | bytes 737288 | tf_op jit(solution)/shard_map/ppermute | solution.py:277
  163.4 8.1 %collective-permute-start.5 = (bf16[2,160,384]{2,1,0:T(8,128)(2,1)S(1)}, bf16[2,160,384]{2,1,0:T(8,128)(2,1)S(1)}, u32[]{:S(2)}, u32[]{:S(2)}) collective-permute-start(bf16[2,160,384]{2,1,0:T(8,128)(2,1)S(1)} %pad_maximum_fusion.1), channel_id=1, source_target_pairs={{0,16},{32,304},{16,0},{48,288},{256,272},{288,48},{272,256},{304,... | collective-permute-start | bytes 737288 | tf_op jit(solution)/shard_map/ppermute | solution.py:277
  166.9 8.0 %collective-permute-start.10 = (bf16[160,384]{1,0:T(8,128)(2,1)S(1)}, bf16[160,384]{1,0:T(8,128)(2,1)S(1)}, u32[]{:S(2)}, u32[]{:S(2)}) collective-permute-start(bf16[160,384]{1,0:T(8,128)(2,1)S(1)} %fusion.14), channel_id=1, source_target_pairs={{0,192},{32,96},{64,128},{96,32},{128,64},{160,224},{192,0},{224,1... | collective-permute-start | bytes 368648 | tf_op jit(solution)/shard_map/ppermute | solution.py:278
  171.5 8.0 %collective-permute-start.6 = (bf16[160,384]{1,0:T(8,128)(2,1)S(1)}, bf16[160,384]{1,0:T(8,128)(2,1)S(1)}, u32[]{:S(2)}, u32[]{:S(2)}) collective-permute-start(bf16[160,384]{1,0:T(8,128)(2,1)S(1)} %fusion.10), channel_id=1, source_target_pairs={{0,272},{32,48},{16,256},{48,32},{256,16},{288,304},{272,0},{304,2... | collective-permute-start | bytes 368648 | tf_op jit(solution)/shard_map/ppermute | solution.py:278
Sparse Core Ops, SparseCore 0:
  11.2 86.0 all-gather.1
  115.8 70.5 reduce-scatter.1

commit v5 on v4

--- a/solution.py
+++ b/solution.py
@@ -10,6 +10,7 @@
 SPLIT = 8
 PAD = 128
 CHUNKS = 5
+BLOCKS = 8
 VMEM_LIMIT = 60 * 1024 * 1024
 SWAP = [(0, 1), (1, 0)]
 
@@ -18,61 +19,101 @@
     return block.reshape(-1, block.shape[-1])
 
 
-def forward_kernel(experts, rows, weights, back, dab, hid, rows_v, routes_v, w_v, back_v, total, sems):
-    n_z, both, chunk = rows_v.shape[1:]
+def dot_rows(block, other):
+    return lax.dot_general(
+        flat(block), other, (((0,), (0,)), ((), ())), preferred_element_type=jnp.float32
+    ).astype(jnp.bfloat16)
+
+
+def put_grads(out, rows, at, skip, dab, hid):
+    height, tok, hidden = out.shape[0], rows.shape[1] // 2, hid.shape[1] // 2
+    reach = -(-height // 128) * 128
+    columns = pl.ds(at, reach)
+    from_x = dot_rows(rows[:, :tok, columns], dab[...])
+    from_g = dot_rows(rows[:, tok:, columns], hid[...])
+    fill_grads(out, from_x, from_g, skip, hidden)
+
+
+def fill_grads(out, from_x, from_g, skip, hidden):
+    height = out.shape[0]
+    for i in range(2):
+        col = 3 * i * hidden
+        out[:, col : col + 2 * hidden] = from_x[
+            skip : skip + height, 2 * i * hidden : 2 * (i + 1) * hidden
+        ]
+        out[:, col + 2 * hidden : col + 3 * hidden] = from_g[
+            skip : skip + height, i * hidden : (i + 1) * hidden
+        ]
+
+
+def each_half(part, height, body):
+    reach = -(-height // 128) * 128
+
+    @pl.when(part == 0)
+    def _():
+        body(0, 0)
+
+    @pl.when(part == 1)
+    def _():
+        body(2 * height - reach, reach - height)
+
+
+def forward_kernel(
+    scalars, rows, weights, back, dab, hid, send, rows_v, turned, w_v, back_v, send_v, total, sems
+):
+    n_z, both, _ = rows_v.shape
+    chunk = w_v.shape[1]
     tok = both // 2
-    hidden = hid.shape[1] // 2
+    hidden, bf16 = hid.shape[1] // 2, jnp.bfloat16
+    width = CHUNKS * chunk
+    blocks, height, _ = send_v.shape
+
+    def columns(k):
+        return pl.ds(pl.multiple_of(k * chunk, 128), chunk)
 
     def row_copy(k):
-        return pltpu.make_async_copy(
-            rows.at[:, :, pl.ds(pl.multiple_of(k * chunk, 128), chunk)], rows_v.at[k], sems.at[0, k]
-        )
+        at = columns(k)
+        return pltpu.make_async_copy(rows.at[:, :, at], rows_v.at[:, :, at], sems.at[0, k])
 
     def weight_copy(k):
-        return pltpu.make_async_copy(
-            weights.at[pl.ds(pl.multiple_of(k * chunk, 128), chunk), :], w_v.at[k], sems.at[1, k]
-        )
+        return pltpu.make_async_copy(weights.at[columns(k), :], w_v.at[k], sems.at[1, k])
 
     def back_copy(k):
-        return pltpu.make_async_copy(
-            back_v.at[k], back.at[:, pl.ds(pl.multiple_of(k * chunk, 128), chunk)], sems.at[2, k]
-        )
-
-    route_copy = pltpu.make_async_copy(
-        rows.at[:, :, CHUNKS * chunk : CHUNKS * chunk + PAD], routes_v, sems.at[3, 0]
-    )
-
-    def start(k, carry):
+        return pltpu.make_async_copy(back_v.at[k], back.at[:, columns(k)], sems.at[2, k])
+
+    def send_copy(n):
+        return pltpu.make_async_copy(send_v.at[n], send.at[n], sems.at[3, n])
+
+    last = pl.ds(width, PAD)
+    route_copy = pltpu.make_async_copy(rows.at[:, :, last], rows_v.at[:, :, last], sems.at[4, 0])
+
+    for k in range(CHUNKS):
         row_copy(k).start()
         weight_copy(k).start()
-        return carry
-
-    lax.fori_loop(0, CHUNKS, start, 0)
     route_copy.start()
-    total[...] = jnp.zeros_like(total)
-
-    def accumulate(k, carry):
+
+    for k in range(CHUNKS):
         row_copy(k).wait()
         weight_copy(k).wait()
-        x_rows = flat(rows_v[k, :, :tok, :])
-        g_rows = flat(rows_v[k, :, tok:, :])
-        w = w_v[k]
-        total[:, : 4 * hidden] += jnp.dot(
-            x_rows, w[:, : 4 * hidden], preferred_element_type=jnp.float32
-        )
-        total[:, 4 * hidden :] += jnp.dot(
-            g_rows, w[:, 4 * hidden :], preferred_element_type=jnp.float32
-        )
-        return carry
-
-    lax.fori_loop(0, CHUNKS, accumulate, 0)
+        at = slice(k * chunk, (k + 1) * chunk)
+        x_rows, g_rows = flat(rows_v[:, :tok, at]), flat(rows_v[:, tok:, at])
+        turned[0, at, :] = x_rows.T
+        turned[1, at, :] = g_rows.T
+        from_x = jnp.dot(x_rows, w_v[k, :, : 4 * hidden], preferred_element_type=jnp.float32)
+        from_g = jnp.dot(g_rows, w_v[k, :, 4 * hidden :], preferred_element_type=jnp.float32)
+        if k == 0:
+            total[:, : 4 * hidden] = from_x
+            total[:, 4 * hidden :] = from_g
+        else:
+            total[:, : 4 * hidden] += from_x
+            total[:, 4 * hidden :] += from_g
     route_copy.wait()
 
-    live_rows = flat(routes_v[:, :tok, :]).astype(jnp.float32)
-    gate_rows = flat(routes_v[:, tok:, :]).astype(jnp.float32)
+    live_rows = flat(rows_v[:, :tok, width:]).astype(jnp.float32)
+    gate_rows = flat(rows_v[:, tok:, width:]).astype(jnp.float32)
     lanes = lax.broadcasted_iota(jnp.int32, live_rows.shape, 1)
     for i in range(2):
-        mine = lanes == experts[i]
+        mine = lanes == scalars[i]
         live = jnp.sum(jnp.where(mine, live_rows, 0.0), axis=1, keepdims=True) > 0
         gate = jnp.sum(jnp.where(mine, gate_rows, 0.0), axis=1, keepdims=True)
         at = 2 * i * hidden
@@ -88,7 +129,7 @@
             hid.dtype
         )
 
-    def produce(k, carry):
+    for k in range(CHUNKS):
         back_v[k] = lax.dot_general(
             dab[...],
             w_v[k, :, : 4 * hidden],
@@ -96,21 +137,24 @@
             preferred_element_type=jnp.float32,
         ).astype(back_v.dtype)
         back_copy(k).start()
-        return carry
-
-    lax.fori_loop(0, CHUNKS, produce, 0)
-
-    def finish(k, carry):
+
+    for n in range(blocks):
+        at = pl.ds(pl.multiple_of((2 * n + scalars[2]) * height, 64), height)
+        from_x = jnp.dot(turned[0, at, :], dab[...], preferred_element_type=jnp.float32)
+        from_g = jnp.dot(turned[1, at, :], hid[...], preferred_element_type=jnp.float32)
+        fill_grads(send_v.at[n], from_x.astype(bf16), from_g.astype(bf16), 0, hidden)
+        send_copy(n).start()
+    for k in range(CHUNKS):
         back_copy(k).wait()
-        return carry
-
-    lax.fori_loop(0, CHUNKS, finish, 0)
-
-
-def forward(experts, rows, weights):
+    for n in range(blocks):
+        send_copy(n).wait()
+
+
+def forward(scalars, rows, weights):
     n_z, both, padded = rows.shape
     width, cols = weights.shape
     hidden, chunk, count = cols // 6, width // CHUNKS, n_z * both // 2
+    height = width // (2 * BLOCKS)
     bf16 = jnp.bfloat16
     vmem = pl.BlockSpec(memory_space=pltpu.VMEM)
     hbm = pl.BlockSpec(memory_space=pl.ANY)
@@ -120,67 +164,45 @@
             jax.ShapeDtypeStruct((count, width), bf16),
             jax.ShapeDtypeStruct((count, 4 * hidden), bf16),
             jax.ShapeDtypeStruct((count, 2 * hidden), bf16),
+            jax.ShapeDtypeStruct((BLOCKS, height, cols), bf16),
         ),
         in_specs=[pl.BlockSpec(memory_space=pltpu.SMEM), hbm, hbm],
-        out_specs=(hbm, vmem, vmem),
+        out_specs=(hbm, vmem, vmem, hbm),
         scratch_shapes=[
-            pltpu.VMEM((CHUNKS, n_z, both, chunk), bf16),
-            pltpu.VMEM((n_z, both, PAD), bf16),
+            pltpu.VMEM((n_z, both, padded), bf16),
+            pltpu.VMEM((2, width, count), bf16),
             pltpu.VMEM((CHUNKS, chunk, cols), bf16),
             pltpu.VMEM((CHUNKS, count, chunk), bf16),
+            pltpu.VMEM((BLOCKS, height, cols), bf16),
             pltpu.VMEM((count, cols), jnp.float32),
-            pltpu.SemaphoreType.DMA((4, CHUNKS)),
+            pltpu.SemaphoreType.DMA((5, BLOCKS)),
         ],
         compiler_params=pltpu.CompilerParams(vmem_limit_bytes=VMEM_LIMIT),
         cost_estimate=pl.CostEstimate(
-            flops=2 * count * width * 10 * hidden, bytes_accessed=16_000_000, transcendentals=0
-        ),
-    )(experts, rows, weights)
+            flops=2 * count * width * 14 * hidden, bytes_accessed=20_000_000, transcendentals=0
+        ),
+    )(scalars, rows, weights)
 
 
 def grads_kernel(part, rows, dab, hid, out):
-    tok = rows.shape[1] // 2
-    hidden = hid.shape[1] // 2
     count, height, _ = out.shape
-    reach = -(-height // 128) * 128
-
-    def product(block, left):
-        return lax.dot_general(
-            flat(block), left, (((0,), (0,)), ((), ())), preferred_element_type=jnp.float32
-        ).astype(out.dtype)
-
-    def write(start, skip):
+
+    def half(start, skip):
         for n in range(count):
-            at = 2 * height * n + start
-            from_x = product(rows[:, :tok, at : at + reach], dab[...])
-            from_g = product(rows[:, tok:, at : at + reach], hid[...])
-            for i in range(2):
-                col = 3 * i * hidden
-                out[n, :, col : col + 2 * hidden] = from_x[
-                    skip : skip + height, 2 * i * hidden : 2 * (i + 1) * hidden
-                ]
-                out[n, :, col + 2 * hidden : col + 3 * hidden] = from_g[
-                    skip : skip + height, i * hidden : (i + 1) * hidden
-                ]
-
-    @pl.when(part[0] == 0)
-    def _():
-        write(0, 0)
-
-    @pl.when(part[0] == 1)
-    def _():
-        write(2 * height - reach, reach - height)
-
-
-def weight_grads(part, rows, dab, hid, steps=4, per_step=2):
+            put_grads(out.at[n], rows, 2 * height * n + start, skip, dab, hid)
+
+    each_half(part[0], height, half)
+
+
+def weight_grads(part, rows, dab, hid, per_step=2):
     n_z, both, padded = rows.shape
-    height = (padded - PAD) // (2 * steps * per_step)
+    height = (padded - PAD) // (2 * BLOCKS)
     count, cols = dab.shape[0], dab.shape[1] + hid.shape[1]
     return pl.pallas_call(
         grads_kernel,
         grid_spec=pltpu.PrefetchScalarGridSpec(
             num_scalar_prefetch=1,
-            grid=(steps,),
+            grid=(BLOCKS // per_step,),
             in_specs=[
                 pl.BlockSpec((n_z, both, 2 * height * per_step), lambda i, part: (0, 0, i)),
                 pl.BlockSpec(dab.shape, lambda i, part: (0, 0)),
@@ -188,7 +210,7 @@
             ],
             out_specs=pl.BlockSpec((per_step, height, cols), lambda i, part: (i, 0, 0)),
         ),
-        out_shape=jax.ShapeDtypeStruct((steps * per_step, height, cols), jnp.bfloat16),
+        out_shape=jax.ShapeDtypeStruct((BLOCKS, height, cols), jnp.bfloat16),
         compiler_params=pltpu.CompilerParams(vmem_limit_bytes=VMEM_LIMIT),
         cost_estimate=pl.CostEstimate(
             flops=count * (padded - PAD) * cols, bytes_accessed=9_000_000, transcendentals=0
@@ -297,9 +319,9 @@
     return here[..., :cols], second, jnp.stack([first, there[..., :cols]])
 
 
-def reduce_weights(rows, dab, hid):
+def reduce_weights(send, rows, dab, hid):
     core = lax.axis_index("core")
-    got = lax.ppermute(weight_grads(1 - core, rows, dab, hid), "core", SWAP)
+    got = lax.ppermute(send, "core", SWAP)
     keep = weight_grads(core, rows, dab, hid)
     send_a, send_b = core_sum(keep, got, (1, 3))
     own_a, own_b = core_sum(keep, got, (0, 2))
@@ -344,8 +366,9 @@
     )
 
     rows = rows.reshape(n_z, 2 * tok, width + PAD)
-    back, dab, hid = forward(jnp.stack(experts).astype(jnp.int32), rows, weights)
-    grads = reduce_weights(rows, dab, hid)
+    scalars = jnp.stack([*experts, 1 - lax.axis_index("core")]).astype(jnp.int32)
+    back, dab, hid, send_grads = forward(scalars, rows, weights)
+    grads = reduce_weights(send_grads, rows, dab, hid)
     input_grad = lax.psum_scatter(back, "z", scatter_dimension=0, tiled=True)
     return (
         input_grad,

time: 194 us -> 190 us (0.979)
  Pallas kernels: 32.4 us -> 27.7 us
    pallas_call x2 -> x1, Pallas kernels: 11.9 us -> 5.91 us  [weight_grads(): pl.pallas_call(grads_kernel, grid_spec=pltpu.PrefetchScalarGridSpec(num_s...]
where the time goes in v5:
time: 190 us; the launch traced here: 189 us
  waiting for transfers between devices  92.5 us (49%)
  starting transfers between devices  31.4 us (17%)
  Pallas kernels  27.7 us (15%)
  other arithmetic  17.5 us (9%)
  between operations  14.4 us (8%)
  local copies, waits for them, and re-layouts  5.32 us (3%)
    ppermute x1, waiting for transfers between devices, partner_weights(): mine = lax.ppermute(half, 'yl', SWAP)  42.6 us
    all_gather x1, waiting for transfers between devices, local(): rows = lax.all_gather(send, 'z', axis=0, tiled=True)  23.8 us
    ppermute x4, starting transfers between devices, pair_sum(): last = lax.ppermute(add(second, got[1]), axes, step2)  12.9 us
    pallas_call x1, Pallas kernels, forward(): pl.pallas_call(forward_kernel, out_shape=(jax.ShapeDtypeStruct((count, wi...  11.8 us
    ppermute x4, starting transfers between devices, pair_sum(): got = lax.ppermute(send, axes, step1)  10.9 us
    pallas_call x2, Pallas kernels, core_sum(): pl.pallas_call(split_kernel, grid_spec=pltpu.PrefetchScalarGridSpec(num_s...  10.1 us
    ppermute x4, waiting for transfers between devices, pair_sum(): last = lax.ppermute(add(second, got[1]), axes, step2)  9.78 us
    ppermute x4, waiting for transfers between devices, pair_sum(): got = lax.ppermute(send, axes, step1)  7.86 us
  transfers between devices with their start and end apart: 13, of which 12 were waited for; matrix products, arithmetic and copies ran while one was open for 10% of the time, Pallas kernels for 8%

profile of v5, /device:TPU:6, one launch (start us, length us, event | category | flops | bytes accessed | tf_op | source)
XLA Modules:
  0.0 188.8 jit_solution(14676500619081955969)
XLA Ops:
  7.2 0.7 convert_element_type.126
  7.9 0.7 broadcast_compare_fusion
  8.6 0.8 convert_reduce_fusion
  9.3 1.8 maximum_maximum_fusion
  11.2 3.1 %fusion.4 = bf16[2560,384]{1,0:T(8,128)(2,1)} fusion(s32[]{:T(128)S(6)} %select_n.108, bf16[2,2560,128]{2,1,0:T(8,128)(2,1)} %bitcast.76, bf16[2,2560,128]{2,1,0:T(8,128)(2,1)} %bitcast.77, bf16[2,2560,128]{2,1,0:T(8,128)(2,1)} %bitcast.78), kind=kLoop, calls=%fused_computation.9 | loop fusion | flops 5898240 | bytes 5898244 | tf_op jit(solution)/shard_map/jit(dynamic_index_in_dim)/squeeze | solution.py:279
  14.3 3.6 %collective-permute-start = (bf16[2560,384]{1,0:T(8,128)(2,1)}, bf16[2560,384]{1,0:T(8,128)(2,1)}, u32[]{:S(2)}, u32[]{:S(2)}) collective-permute-start(bf16[2560,384]{1,0:T(8,128)(2,1)} %fusion.4), channel_id=1, source_target_pairs={{0,16},{16,0},{1,17},{17,1},{2,18},{18,2},{3,19},{19,3},{4,20},{20... | collective-permute-start | bytes 5898248 | tf_op jit(solution)/shard_map/ppermute | solution.py:338
  17.9 0.6 pad_add_fusion.scalars
  18.5 42.6 %collective-permute-done = bf16[2560,384]{1,0:T(8,128)(2,1)} collective-permute-done((bf16[2560,384]{1,0:T(8,128)(2,1)}, bf16[2560,384]{1,0:T(8,128)(2,1)}, u32[]{:S(2)}, u32[]{:S(2)}) %collective-permute-start) | collective-permute-done | bytes 1966112 | tf_op jit(solution)/shard_map/ppermute | solution.py:338
  61.2 1.9 %collective-permute-start.1 = (bf16[2560,384]{1,0:T(8,128)(2,1)}, bf16[2560,384]{1,0:T(8,128)(2,1)S(1)}, u32[]{:S(2)}, u32[]{:S(2)}) collective-permute-start(bf16[2560,384]{1,0:T(8,128)(2,1)} %collective-permute-done), channel_id=1, source_target_pairs={{0,32},{32,0},{1,33},{33,1},{2,34},{34,2},{3,35},{35,3},{4,36},{36... | collective-permute-start | bytes 5898248 | tf_op jit(solution)/shard_map/ppermute | solution.py:339
  63.1 1.2 bitcast_dynamic-update-slice_fusion.2
  64.3 1.3 bitcast_dynamic-update-slice_fusion.1
  65.6 1.6 collective-permute-done.1
  67.2 1.9 %broadcast_select_fusion = (bf16[2560,384]{1,0:T(8,128)(2,1)S(1)}, bf16[2560,384]{1,0:T(8,128)(2,1)S(1)}) fusion(bf16[2560,384]{1,0:T(8,128)(2,1)S(1)} %collective-permute-done.1, bf16[2560,384]{1,0:T(8,128)(2,1)} %collective-permute-done, pred[]{:T(512)S(6)} %eq.39), kind=kLoop, calls=%fused_computation.10 | loop fusion | flops 1966080 | bytes 7864321 | tf_op jit(solution)/shard_map/jit(_where)/select_n | solution.py:341
  69.2 1.8 fusion.1
  71.0 0.1 copy-done.2
  71.0 1.3 bitcast_dynamic-update-slice_fusion
  72.3 1.2 fusion.5.weights
  73.6 23.8 %all-gather.2.cloned.1.call-done = bf16[512,5248]{1,0:T(8,128)(2,1)} async-done(((bf16[32,5248]{1,0:T(8,128)(2,1)}), bf16[512,5248]{1,0:T(8,128)(2,1)}) %all-gather.2.cloned.1.call-update) | async-done | bytes 5373968 | tf_op jit(solution)/shard_map/all_gather | solution.py:359
  97.3 11.8 %shard_map.111 = (bf16[256,5120]{1,0:T(8,128)(2,1)}, bf16[256,512]{1,0:T(8,128)(2,1)}, bf16[256,256]{1,0:T(8,128)(2,1)}, bf16[8,320,768]{2,1,0:T(8,128)(2,1)}) custom-call(s32[3]{0:T(128)} %pad_add_fusion.scalars, bf16[16,32,5248]{2,1,0:T(8,128)(2,1)} %bitcast.74, bf16[5120,768]{1,0:T(8,128)(2,1)} %fusion.5.weights), custom_call_target="tpu_custom_call" | custom-call | flops 4697620480 | bytes 20000000 | tf_op jit(solution)/shard_map/pallas_call | solution.py:161
  109.1 1.9 %collective-permute-start.2 = (bf16[8,320,768]{2,1,0:T(8,128)(2,1)}, bf16[8,320,768]{2,1,0:T(8,128)(2,1)}, u32[]{:S(2)}, u32[]{:S(2)}) collective-permute-start(bf16[8,320,768]{2,1,0:T(8,128)(2,1)} %get-tuple-element.15), channel_id=1, source_target_pairs={{0,32},{32,0},{1,33},{33,1},{2,34},{34,2},{3,35},{35,3},{4,36},{36... | collective-permute-start | bytes 11796488 | tf_op jit(solution)/shard_map/ppermute | solution.py:324
  111.2 0.7 stack.101.place
  111.8 5.9 %shard_map.112.keep_a.keep_b = bf16[8,320,768]{2,1,0:T(8,128)(2,1)} custom-call(s32[1]{0:T(128)} %bitcast.19.part, bf16[16,32,5248]{2,1,0:T(8,128)(2,1)} %bitcast.75, bf16[256,512]{1,0:T(8,128)(2,1)} %get-tuple-element.13.dab, bf16[256,256]{1,0:T(8,128)(2,1)} %get-tuple-element.14.hid), custom_call_target="tpu_custom_call" | custom-call | flops 1006632960 | bytes 9000000 | tf_op jit(solution)/shard_map/pallas_call | solution.py:201
  117.7 0.4 collective-permute-done.2.got_a.got_b
  118.1 5.1 %shard_map.114 = (bf16[2,2,160,768]{3,2,1,0:T(8,128)(2,1)}, bf16[2,4,160,384]{3,2,1,0:T(8,128)(2,1)}) custom-call(s32[12]{0:T(128)} %stack.101.place, bf16[8,320,768]{2,1,0:T(8,128)(2,1)} %shard_map.112.keep_a.keep_b, bf16[8,320,768]{2,1,0:T(8,128)(2,1)} %collective-permute-done.2.got_a.got_b, bf16[8,320,768]{2,1,0:T(8,128)(2,1)} %shard_map.112.keep_a.keep_b, ...), custom_call_target="tpu_custom_call" | custom-call | bytes 6000000 | tf_op jit(solution)/shard_map/pallas_call | solution.py:246
  123.2 3.4 %collective-permute-start.7 = (bf16[2,4,160,384]{3,2,1,0:T(8,128)(2,1)}, bf16[2,4,160,384]{3,2,1,0:T(8,128)(2,1)S(1)}, u32[]{:S(2)}, u32[]{:S(2)}) collective-permute-start(bf16[2,4,160,384]{3,2,1,0:T(8,128)(2,1)} %get-tuple-element.19), channel_id=1, source_target_pairs={{0,16},{32,304},{16,0},{48,288},{256,272},{288,48},{272,256},{304,... | collective-permute-start | bytes 2949128 | tf_op jit(solution)/shard_map/ppermute | solution.py:299
  126.6 2.9 %collective-permute-start.3 = (bf16[2,2,160,768]{3,2,1,0:T(8,128)(2,1)}, bf16[2,2,160,768]{3,2,1,0:T(8,128)(2,1)S(1)}, u32[]{:S(2)}, u32[]{:S(2)}) collective-permute-start(bf16[2,2,160,768]{3,2,1,0:T(8,128)(2,1)} %get-tuple-element.17), channel_id=1, source_target_pairs={{0,64},{32,224},{64,0},{96,160},{128,192},{160,96},{192,128},{224,... | collective-permute-start | bytes 2949128 | tf_op jit(solution)/shard_map/ppermute | solution.py:299
  129.5 0.7 stack.92.place
  130.2 5.0 %shard_map.113 = (bf16[2,2,160,768]{3,2,1,0:T(8,128)(2,1)}, bf16[2,4,160,384]{3,2,1,0:T(8,128)(2,1)}) custom-call(s32[12]{0:T(128)} %stack.92.place, bf16[8,320,768]{2,1,0:T(8,128)(2,1)} %shard_map.112.keep_a.keep_b, bf16[8,320,768]{2,1,0:T(8,128)(2,1)} %collective-permute-done.2.got_a.got_b, bf16[8,320,768]{2,1,0:T(8,128)(2,1)} %shard_map.112.keep_a.keep_b, ...), custom_call_target="tpu_custom_call" | custom-call | bytes 6000000 | tf_op jit(solution)/shard_map/pallas_call | solution.py:246
  135.2 4.2 %collective-permute-done.7 = bf16[2,4,160,384]{3,2,1,0:T(8,128)(2,1)S(1)} collective-permute-done((bf16[2,4,160,384]{3,2,1,0:T(8,128)(2,1)}, bf16[2,4,160,384]{3,2,1,0:T(8,128)(2,1)S(1)}, u32[]{:S(2)}, u32[]{:S(2)}) %collective-permute-start.7) | collective-permute-done | bytes 983072 | tf_op jit(solution)/shard_map/ppermute | solution.py:299
  139.4 1.2 fusion.9
  140.6 4.6 %collective-permute-start.8 = (bf16[4,160,384]{2,1,0:T(8,128)(2,1)S(1)}, bf16[4,160,384]{2,1,0:T(8,128)(2,1)}, u32[]{:S(2)}, u32[]{:S(2)}) collective-permute-start(bf16[4,160,384]{2,1,0:T(8,128)(2,1)S(1)} %fusion.9), channel_id=1, source_target_pairs={{0,272},{32,48},{16,256},{48,32},{256,16},{288,304},{272,0},{304,2... | collective-permute-start | bytes 1474568 | tf_op jit(solution)/shard_map/ppermute | solution.py:300
  145.3 1.2 fusion.8
  146.5 2.6 %collective-permute-start.4 = (bf16[2,160,768]{2,1,0:T(8,128)(2,1)S(1)}, bf16[2,160,768]{2,1,0:T(8,128)(2,1)S(1)}, u32[]{:S(2)}, u32[]{:S(2)}) collective-permute-start(bf16[2,160,768]{2,1,0:T(8,128)(2,1)S(1)} %fusion.8), channel_id=1, source_target_pairs={{0,192},{32,96},{64,128},{96,32},{128,64},{160,224},{192,0},{224,1... | collective-permute-start | bytes 1474568 | tf_op jit(solution)/shard_map/ppermute | solution.py:300
  149.1 3.5 %collective-permute-done.8 = bf16[4,160,384]{2,1,0:T(8,128)(2,1)} collective-permute-done((bf16[4,160,384]{2,1,0:T(8,128)(2,1)S(1)}, bf16[4,160,384]{2,1,0:T(8,128)(2,1)}, u32[]{:S(2)}, u32[]{:S(2)}) %collective-permute-start.8) | collective-permute-done | bytes 491552 | tf_op jit(solution)/shard_map/ppermute | solution.py:300
  152.7 1.4 fusion.6
  154.1 2.8 %collective-permute-start.9 = (bf16[2,160,384]{2,1,0:T(8,128)(2,1)S(1)}, bf16[2,160,384]{2,1,0:T(8,128)(2,1)S(1)}, u32[]{:S(2)}, u32[]{:S(2)}) collective-permute-start(bf16[2,160,384]{2,1,0:T(8,128)(2,1)S(1)} %pad_maximum_fusion.2), channel_id=1, source_target_pairs={{0,64},{32,224},{64,0},{96,160},{128,192},{160,96},{192,128},{224,... | collective-permute-start | bytes 737288 | tf_op jit(solution)/shard_map/ppermute | solution.py:299
  156.9 1.5 collective-permute-done.4
  158.4 0.2 fusion.7
  158.7 1.9 %collective-permute-start.5 = (bf16[2,160,384]{2,1,0:T(8,128)(2,1)S(1)}, bf16[2,160,384]{2,1,0:T(8,128)(2,1)S(1)}, u32[]{:S(2)}, u32[]{:S(2)}) collective-permute-start(bf16[2,160,384]{2,1,0:T(8,128)(2,1)S(1)} %pad_maximum_fusion.1), channel_id=1, source_target_pairs={{0,16},{32,304},{16,0},{48,288},{256,272},{288,48},{272,256},{304,... | collective-permute-start | bytes 737288 | tf_op jit(solution)/shard_map/ppermute | solution.py:299
  160.6 1.6 collective-permute-done.9
  162.3 2.5 %collective-permute-start.10 = (bf16[160,384]{1,0:T(8,128)(2,1)S(1)}, bf16[160,384]{1,0:T(8,128)(2,1)S(1)}, u32[]{:S(2)}, u32[]{:S(2)}) collective-permute-start(bf16[160,384]{1,0:T(8,128)(2,1)S(1)} %fusion.14), channel_id=1, source_target_pairs={{0,192},{32,96},{64,128},{96,32},{128,64},{160,224},{192,0},{224,1... | collective-permute-start | bytes 368648 | tf_op jit(solution)/shard_map/ppermute | solution.py:300
  164.7 2.1 %collective-permute-done.5 = bf16[2,160,384]{2,1,0:T(8,128)(2,1)S(1)} collective-permute-done((bf16[2,160,384]{2,1,0:T(8,128)(2,1)S(1)}, bf16[2,160,384]{2,1,0:T(8,128)(2,1)S(1)}, u32[]{:S(2)}, u32[]{:S(2)}) %collective-permute-start.5) | collective-permute-done | bytes 245792 | tf_op jit(solution)/shard_map/ppermute | solution.py:299
  166.9 3.2 %collective-permute-start.6 = (bf16[160,384]{1,0:T(8,128)(2,1)S(1)}, bf16[160,384]{1,0:T(8,128)(2,1)S(1)}, u32[]{:S(2)}, u32[]{:S(2)}) collective-permute-start(bf16[160,384]{1,0:T(8,128)(2,1)S(1)} %fusion.10), channel_id=1, source_target_pairs={{0,272},{32,48},{16,256},{48,32},{256,16},{288,304},{272,0},{304,2... | collective-permute-start | bytes 368648 | tf_op jit(solution)/shard_map/ppermute | solution.py:300
  170.0 0.2 collective-permute-done.10
  170.2 0.1 fusion.13
  170.3 4.5 %collective-permute-done.6 = bf16[160,384]{1,0:T(8,128)(2,1)S(1)} collective-permute-done((bf16[160,384]{1,0:T(8,128)(2,1)S(1)}, bf16[160,384]{1,0:T(8,128)(2,1)S(1)}, u32[]{:S(2)}, u32[]{:S(2)}) %collective-permute-start.6) | collective-permute-done | bytes 122912 | tf_op jit(solution)/shard_map/ppermute | solution.py:300
  174.9 0.7 fusion.19
  175.6 6.3 %reduce-scatter.2.cloned.1.call-done = bf16[16,5120]{1,0:T(8,128)(2,1)} async-done(((bf16[256,5120]{1,0:T(8,128)(2,1)}), bf16[16,5120]{1,0:T(8,128)(2,1)}) %reduce-scatter.2.cloned.1.call-update) | async-done | bytes 163856 | tf_op jit(solution)/shard_map/reduce_scatter | solution.py:372
  (22 shorter events, 0.5 us)
Async XLA Ops:
  7.2 90.2 %all-gather.2.cloned.1.call-start = ((), (), s32[]{:S(2)}) async-start(), calls=%async_computation.1 | async-start | bytes 5709824 | tf_op jit(solution)/shard_map/all_gather | solution.py:359
  11.1 170.9 %reduce-scatter.2.cloned.1.call-start = ((), (), s32[]{:S(2)}) async-start(), calls=%async_computation.2 | async-start | bytes 2785280 | tf_op jit(solution)/shard_map/reduce_scatter | solution.py:372
  11.1 52.0 %copy-start = (bf16[1,5120,128]{2,1,0:T(8,128)(2,1)S(1)}, bf16[1,5120,128]{2,1,0:T(8,128)(2,1)}, u32[]{:S(2)}) copy-start(bf16[1,5120,128]{2,1,0:T(8,128)(2,1)} %param.13) | copy-start | bytes 3932164
  14.3 50.1 %copy-start.1 = (bf16[1,5120,128]{2,1,0:T(8,128)(2,1)S(1)}, bf16[1,5120,128]{2,1,0:T(8,128)(2,1)}, u32[]{:S(2)}) copy-start(bf16[1,5120,128]{2,1,0:T(8,128)(2,1)} %param.14) | copy-start | bytes 3932164
  14.3 46.9 %collective-permute-start = (bf16[2560,384]{1,0:T(8,128)(2,1)}, bf16[2560,384]{1,0:T(8,128)(2,1)}, u32[]{:S(2)}, u32[]{:S(2)}) collective-permute-start(bf16[2560,384]{1,0:T(8,128)(2,1)} %fusion.4), channel_id=1, source_target_pairs={{0,16},{16,0},{1,17},{17,1},{2,18},{18,2},{3,19},{19,3},{4,20},{20... | collective-permute-start | bytes 5898248 | tf_op jit(solution)/shard_map/ppermute | solution.py:338
  61.2 6.1 %collective-permute-start.1 = (bf16[2560,384]{1,0:T(8,128)(2,1)}, bf16[2560,384]{1,0:T(8,128)(2,1)S(1)}, u32[]{:S(2)}, u32[]{:S(2)}) collective-permute-start(bf16[2560,384]{1,0:T(8,128)(2,1)} %collective-permute-done), channel_id=1, source_target_pairs={{0,32},{32,0},{1,33},{33,1},{2,34},{34,2},{3,35},{35,3},{4,36},{36... | collective-permute-start | bytes 5898248 | tf_op jit(solution)/shard_map/ppermute | solution.py:339
  69.2 1.9 copy-start.2
  109.1 9.0 %collective-permute-start.2 = (bf16[8,320,768]{2,1,0:T(8,128)(2,1)}, bf16[8,320,768]{2,1,0:T(8,128)(2,1)}, u32[]{:S(2)}, u32[]{:S(2)}) collective-permute-start(bf16[8,320,768]{2,1,0:T(8,128)(2,1)} %get-tuple-element.15), channel_id=1, source_target_pairs={{0,32},{32,0},{1,33},{33,1},{2,34},{34,2},{3,35},{35,3},{4,36},{36... | collective-permute-start | bytes 11796488 | tf_op jit(solution)/shard_map/ppermute | solution.py:324
  123.2 16.2 %collective-permute-start.7 = (bf16[2,4,160,384]{3,2,1,0:T(8,128)(2,1)}, bf16[2,4,160,384]{3,2,1,0:T(8,128)(2,1)S(1)}, u32[]{:S(2)}, u32[]{:S(2)}) collective-permute-start(bf16[2,4,160,384]{3,2,1,0:T(8,128)(2,1)} %get-tuple-element.19), channel_id=1, source_target_pairs={{0,16},{32,304},{16,0},{48,288},{256,272},{288,48},{272,256},{304,... | collective-permute-start | bytes 2949128 | tf_op jit(solution)/shard_map/ppermute | solution.py:299
  126.6 18.7 %collective-permute-start.3 = (bf16[2,2,160,768]{3,2,1,0:T(8,128)(2,1)}, bf16[2,2,160,768]{3,2,1,0:T(8,128)(2,1)S(1)}, u32[]{:S(2)}, u32[]{:S(2)}) collective-permute-start(bf16[2,2,160,768]{3,2,1,0:T(8,128)(2,1)} %get-tuple-element.17), channel_id=1, source_target_pairs={{0,64},{32,224},{64,0},{96,160},{128,192},{160,96},{192,128},{224,... | collective-permute-start | bytes 2949128 | tf_op jit(solution)/shard_map/ppermute | solution.py:299
  139.4 19.0 %copy-start.3 = (bf16[2,2,160,768]{3,2,1,0:T(8,128)(2,1)S(1)}, bf16[2,2,160,768]{3,2,1,0:T(8,128)(2,1)}, u32[]{:S(2)}) copy-start(bf16[2,2,160,768]{3,2,1,0:T(8,128)(2,1)} %get-tuple-element.16) | copy-start | bytes 2949124
  140.6 12.0 %collective-permute-start.8 = (bf16[4,160,384]{2,1,0:T(8,128)(2,1)S(1)}, bf16[4,160,384]{2,1,0:T(8,128)(2,1)}, u32[]{:S(2)}, u32[]{:S(2)}) collective-permute-start(bf16[4,160,384]{2,1,0:T(8,128)(2,1)S(1)} %fusion.9), channel_id=1, source_target_pairs={{0,272},{32,48},{16,256},{48,32},{256,16},{288,304},{272,0},{304,2... | collective-permute-start | bytes 1474568 | tf_op jit(solution)/shard_map/ppermute | solution.py:300
  146.5 11.9 %collective-permute-start.4 = (bf16[2,160,768]{2,1,0:T(8,128)(2,1)S(1)}, bf16[2,160,768]{2,1,0:T(8,128)(2,1)S(1)}, u32[]{:S(2)}, u32[]{:S(2)}) collective-permute-start(bf16[2,160,768]{2,1,0:T(8,128)(2,1)S(1)} %fusion.8), channel_id=1, source_target_pairs={{0,192},{32,96},{64,128},{96,32},{128,64},{160,224},{192,0},{224,1... | collective-permute-start | bytes 1474568 | tf_op jit(solution)/shard_map/ppermute | solution.py:300
  154.1 8.1 %collective-permute-start.9 = (bf16[2,160,384]{2,1,0:T(8,128)(2,1)S(1)}, bf16[2,160,384]{2,1,0:T(8,128)(2,1)S(1)}, u32[]{:S(2)}, u32[]{:S(2)}) collective-permute-start(bf16[2,160,384]{2,1,0:T(8,128)(2,1)S(1)} %pad_maximum_fusion.2), channel_id=1, source_target_pairs={{0,64},{32,224},{64,0},{96,160},{128,192},{160,96},{192,128},{224,... | collective-permute-start | bytes 737288 | tf_op jit(solution)/shard_map/ppermute | solution.py:299
  158.7 8.1 %collective-permute-start.5 = (bf16[2,160,384]{2,1,0:T(8,128)(2,1)S(1)}, bf16[2,160,384]{2,1,0:T(8,128)(2,1)S(1)}, u32[]{:S(2)}, u32[]{:S(2)}) collective-permute-start(bf16[2,160,384]{2,1,0:T(8,128)(2,1)S(1)} %pad_maximum_fusion.1), channel_id=1, source_target_pairs={{0,16},{32,304},{16,0},{48,288},{256,272},{288,48},{272,256},{304,... | collective-permute-start | bytes 737288 | tf_op jit(solution)/shard_map/ppermute | solution.py:299
  162.3 8.0 %collective-permute-start.10 = (bf16[160,384]{1,0:T(8,128)(2,1)S(1)}, bf16[160,384]{1,0:T(8,128)(2,1)S(1)}, u32[]{:S(2)}, u32[]{:S(2)}) collective-permute-start(bf16[160,384]{1,0:T(8,128)(2,1)S(1)} %fusion.14), channel_id=1, source_target_pairs={{0,192},{32,96},{64,128},{96,32},{128,64},{160,224},{192,0},{224,1... | collective-permute-start | bytes 368648 | tf_op jit(solution)/shard_map/ppermute | solution.py:300
  166.9 8.0 %collective-permute-start.6 = (bf16[160,384]{1,0:T(8,128)(2,1)S(1)}, bf16[160,384]{1,0:T(8,128)(2,1)S(1)}, u32[]{:S(2)}, u32[]{:S(2)}) collective-permute-start(bf16[160,384]{1,0:T(8,128)(2,1)S(1)} %fusion.10), channel_id=1, source_target_pairs={{0,272},{32,48},{16,256},{48,32},{256,16},{288,304},{272,0},{304,2... | collective-permute-start | bytes 368648 | tf_op jit(solution)/shard_map/ppermute | solution.py:300
Sparse Core Ops, SparseCore 0:
  11.2 86.0 all-gather.1
  111.2 70.7 reduce-scatter.1

commit v6 on v5

--- a/solution.py
+++ b/solution.py
@@ -19,10 +19,14 @@
     return block.reshape(-1, block.shape[-1])
 
 
-def dot_rows(block, other):
+def dot_f32(block, other):
     return lax.dot_general(
         flat(block), other, (((0,), (0,)), ((), ())), preferred_element_type=jnp.float32
-    ).astype(jnp.bfloat16)
+    )
+
+
+def dot_rows(block, other):
+    return dot_f32(block, other).astype(jnp.bfloat16)
 
 
 def put_grads(out, rows, at, skip, dab, hid):
@@ -59,14 +63,15 @@
 
 
 def forward_kernel(
-    scalars, rows, weights, back, dab, hid, send, rows_v, turned, w_v, back_v, send_v, total, sems
+    scalars, rows, weights, back, dab, hid, swap, rows_v, w_v, back_v, acts_v, total, sems
 ):
     n_z, both, _ = rows_v.shape
     chunk = w_v.shape[1]
     tok = both // 2
-    hidden, bf16 = hid.shape[1] // 2, jnp.bfloat16
+    hidden = hid.shape[1] // 2
     width = CHUNKS * chunk
-    blocks, height, _ = send_v.shape
+    blocks, reach = swap.shape[0] - 1, swap.shape[-1]
+    step = width // blocks
 
     def columns(k):
         return pl.ds(pl.multiple_of(k * chunk, 128), chunk)
@@ -81,9 +86,11 @@
     def back_copy(k):
         return pltpu.make_async_copy(back_v.at[k], back.at[:, columns(k)], sems.at[2, k])
 
-    def send_copy(n):
-        return pltpu.make_async_copy(send_v.at[n], send.at[n], sems.at[3, n])
-
+    def swap_copy(n):
+        at = pl.ds(pl.multiple_of(n * step + scalars[2] * (step - reach), 128), reach)
+        return pltpu.make_async_copy(rows_v.at[:, :, at], swap.at[n], sems.at[3, n])
+
+    acts_copy = pltpu.make_async_copy(acts_v, swap.at[blocks], sems.at[3, blocks])
     last = pl.ds(width, PAD)
     route_copy = pltpu.make_async_copy(rows.at[:, :, last], rows_v.at[:, :, last], sems.at[4, 0])
 
@@ -97,8 +104,6 @@
         weight_copy(k).wait()
         at = slice(k * chunk, (k + 1) * chunk)
         x_rows, g_rows = flat(rows_v[:, :tok, at]), flat(rows_v[:, tok:, at])
-        turned[0, at, :] = x_rows.T
-        turned[1, at, :] = g_rows.T
         from_x = jnp.dot(x_rows, w_v[k, :, : 4 * hidden], preferred_element_type=jnp.float32)
         from_g = jnp.dot(g_rows, w_v[k, :, 4 * hidden :], preferred_element_type=jnp.float32)
         if k == 0:
@@ -108,6 +113,8 @@
             total[:, : 4 * hidden] += from_x
             total[:, 4 * hidden :] += from_g
     route_copy.wait()
+    for n in range(blocks):
+        swap_copy(n).start()
 
     live_rows = flat(rows_v[:, :tok, width:]).astype(jnp.float32)
     gate_rows = flat(rows_v[:, tok:, width:]).astype(jnp.float32)
@@ -129,6 +136,13 @@
             hid.dtype
         )
 
+    edge = 3 * hidden
+    acts = jnp.concatenate(
+        [dab[:, :edge], jnp.concatenate([dab[:, edge:], hid[...]], axis=1)], axis=0
+    )
+    acts_v[...] = acts.reshape(acts_v.shape)
+    acts_copy.start()
+
     for k in range(CHUNKS):
         back_v[k] = lax.dot_general(
             dab[...],
@@ -138,23 +152,18 @@
         ).astype(back_v.dtype)
         back_copy(k).start()
 
-    for n in range(blocks):
-        at = pl.ds(pl.multiple_of((2 * n + scalars[2]) * height, 64), height)
-        from_x = jnp.dot(turned[0, at, :], dab[...], preferred_element_type=jnp.float32)
-        from_g = jnp.dot(turned[1, at, :], hid[...], preferred_element_type=jnp.float32)
-        fill_grads(send_v.at[n], from_x.astype(bf16), from_g.astype(bf16), 0, hidden)
-        send_copy(n).start()
     for k in range(CHUNKS):
         back_copy(k).wait()
     for n in range(blocks):
-        send_copy(n).wait()
+        swap_copy(n).wait()
+    acts_copy.wait()
 
 
 def forward(scalars, rows, weights):
     n_z, both, padded = rows.shape
     width, cols = weights.shape
     hidden, chunk, count = cols // 6, width // CHUNKS, n_z * both // 2
-    height = width // (2 * BLOCKS)
+    reach = -(-width // (2 * BLOCKS) // 128) * 128
     bf16 = jnp.bfloat16
     vmem = pl.BlockSpec(memory_space=pltpu.VMEM)
     hbm = pl.BlockSpec(memory_space=pl.ANY)
@@ -164,22 +173,21 @@
             jax.ShapeDtypeStruct((count, width), bf16),
             jax.ShapeDtypeStruct((count, 4 * hidden), bf16),
             jax.ShapeDtypeStruct((count, 2 * hidden), bf16),
-            jax.ShapeDtypeStruct((BLOCKS, height, cols), bf16),
+            jax.ShapeDtypeStruct((BLOCKS + 1, n_z, both, reach), bf16),
         ),
         in_specs=[pl.BlockSpec(memory_space=pltpu.SMEM), hbm, hbm],
         out_specs=(hbm, vmem, vmem, hbm),
         scratch_shapes=[
             pltpu.VMEM((n_z, both, padded), bf16),
-            pltpu.VMEM((2, width, count), bf16),
             pltpu.VMEM((CHUNKS, chunk, cols), bf16),
             pltpu.VMEM((CHUNKS, count, chunk), bf16),
-            pltpu.VMEM((BLOCKS, height, cols), bf16),
+            pltpu.VMEM((n_z, both, reach), bf16),
             pltpu.VMEM((count, cols), jnp.float32),
-            pltpu.SemaphoreType.DMA((5, BLOCKS)),
+            pltpu.SemaphoreType.DMA((5, BLOCKS + 1)),
         ],
         compiler_params=pltpu.CompilerParams(vmem_limit_bytes=VMEM_LIMIT),
         cost_estimate=pl.CostEstimate(
-            flops=2 * count * width * 14 * hidden, bytes_accessed=20_000_000, transcendentals=0
+            flops=2 * count * width * 10 * hidden, bytes_accessed=20_000_000, transcendentals=0
         ),
     )(scalars, rows, weights)
 
@@ -218,15 +226,59 @@
     )(jnp.reshape(part, (1,)).astype(jnp.int32), rows, dab, hid)
 
 
-def split_kernel(place, keep_a, got_a, keep_b, got_b, out_a, out_b):
-    out_a[...] = add(keep_a[...], got_a[...])[None]
-    out_b[...] = add(keep_b[...], got_b[...])[None]
+def other_kernel(place, keep_a, keep_b, got_a, got_b, acts, out_a, out_b, dab, hid):
+    tok, hidden = got_a.shape[2] // 2, hid.shape[1] // 2
+    count, cut, reach = dab.shape[0], keep_a.shape[1], got_a.shape[3]
+    edge = 3 * hidden
+    step = pl.program_id(0)
+
+    @pl.when(step == 0)
+    def _():
+        rows = flat(acts[0])
+        dab[:, :edge] = rows[:count]
+        dab[:, edge:] = rows[count:, :hidden]
+        hid[...] = rows[count:, hidden:]
+
+    def dots(block, at, slices):
+        columns = slice(at, at + 2 * hidden)
+        pairs = pl.ds(pl.multiple_of(slices[0] * 2 * hidden, 128), slices[1] * 2 * hidden)
+        ones = pl.ds(pl.multiple_of(slices[0] * hidden, 128), slices[1] * hidden)
+        return dot_f32(block[:, :tok, columns], dab[:, pairs]), dot_f32(
+            block[:, tok:, columns], hid[:, ones]
+        )
+
+    def put(start):
+        from_x, from_g = dots(got_a[0], 0, (0, 2))
+        rows = slice(start, start + cut)
+        for i in range(2):
+            col = 3 * i * hidden
+            for at, part in (
+                (col, from_x[rows, 2 * i * hidden : 2 * (i + 1) * hidden]),
+                (col + 2 * hidden, from_g[rows, i * hidden : (i + 1) * hidden]),
+            ):
+                to = slice(at, at + part.shape[1])
+                out_a[0, 0, :, to] = (keep_a[0, :, to].astype(jnp.float32) + part).astype(out_a.dtype)
+        first = reach - 2 * hidden
+        rows = slice(start + cut - first, start + 2 * cut - first)
+        for m in range(2):
+            from_x, from_g = dots(got_b[m], first, (place[8 + step], 1))
+            for at, part in ((0, from_x[rows]), (2 * hidden, from_g[rows])):
+                to = slice(at, at + part.shape[1])
+                out_b[0, m, :, to] = (keep_b[m, :, to].astype(jnp.float32) + part).astype(out_b.dtype)
+
+    @pl.when(place[12] == 0)
+    def _():
+        put(0)
+
+    @pl.when(place[12] == 1)
+    def _():
+        put(reach - 2 * cut)
 
 
 def core_sum(keep, got, slots):
     x, core, yh = lax.axis_index("x"), lax.axis_index("core"), lax.axis_index("yh")
     blocks, part, cols = keep.shape
-    n_x, half, cut = blocks // 2, cols // 2, part // 2
+    n_x, half, cut, width = blocks // 2, cols // 2, part // 2, blocks * part
     up = (x + core) % 2 == 0
     after, before = (x + 1) % 4, (x + 3) % 4
     a_slots = [x, jnp.where(up, after, before), jnp.where(up, before, after), (x + 2) % 4]
@@ -234,7 +286,7 @@
     b_slots = [(yh, 0), (1 - far, 1), (far, 1), (1 - yh, 0)]
     place = [h * n_x + a_slots[s] for s in slots for h in range(2)]
     place += [h * 2 + m for h, _ in [b_slots[s] for s in slots] for m in range(2)]
-    place += [c for _, c in [b_slots[s] for s in slots] for m in range(2)]
+    place += [c for _, c in [b_slots[s] for s in slots] for m in range(2)] + [core]
     place = jnp.stack([jnp.asarray(v, jnp.int32) for v in place])
 
     in_a = pl.BlockSpec((1, cut, cols), lambda j, p: (p[j], 0, 0))
@@ -243,15 +295,27 @@
     def out(j, p):
         return (j // 2, j % 2, 0, 0)
 
+    _, n_z, both, reach = got.shape
+    count, hidden = n_z * both // 2, cols // 6
     return pl.pallas_call(
-        split_kernel,
+        other_kernel,
         grid_spec=pltpu.PrefetchScalarGridSpec(
             num_scalar_prefetch=1,
             grid=(4,),
-            in_specs=[in_a, in_a, in_b, in_b],
+            in_specs=[
+                in_a,
+                in_b,
+                pl.BlockSpec((1, n_z, both, reach), lambda j, p: (p[j], 0, 0, 0)),
+                pl.BlockSpec((2, n_z, both, reach), lambda j, p: (p[4 + j], 0, 0, 0)),
+                pl.BlockSpec((1, n_z, both, reach), lambda j, p: (blocks, 0, 0, 0)),
+            ],
             out_specs=[
                 pl.BlockSpec((1, 1, cut, cols), out),
                 pl.BlockSpec((1, 2, cut, half), out),
+            ],
+            scratch_shapes=[
+                pltpu.VMEM((count, 4 * hidden), keep.dtype),
+                pltpu.VMEM((count, 2 * hidden), keep.dtype),
             ],
         ),
         out_shape=[
@@ -259,8 +323,10 @@
             jax.ShapeDtypeStruct((2, n_x, cut, half), keep.dtype),
         ],
         compiler_params=pltpu.CompilerParams(vmem_limit_bytes=VMEM_LIMIT),
-        cost_estimate=pl.CostEstimate(flops=0, bytes_accessed=6_000_000, transcendentals=0),
-    )(place, keep, got, keep, got)
+        cost_estimate=pl.CostEstimate(
+            flops=count * width * cols, bytes_accessed=9_000_000, transcendentals=0
+        ),
+    )(place, keep, keep, got, got, got)
 
 
 def route_columns(expert_index, slot, gate):
@@ -319,9 +385,9 @@
     return here[..., :cols], second, jnp.stack([first, there[..., :cols]])
 
 
-def reduce_weights(send, rows, dab, hid):
+def reduce_weights(swap, rows, dab, hid):
     core = lax.axis_index("core")
-    got = lax.ppermute(send, "core", SWAP)
+    got = lax.ppermute(swap, "core", SWAP)
     keep = weight_grads(core, rows, dab, hid)
     send_a, send_b = core_sum(keep, got, (1, 3))
     own_a, own_b = core_sum(keep, got, (0, 2))
@@ -367,8 +433,8 @@
 
     rows = rows.reshape(n_z, 2 * tok, width + PAD)
     scalars = jnp.stack([*experts, 1 - lax.axis_index("core")]).astype(jnp.int32)
-    back, dab, hid, send_grads = forward(scalars, rows, weights)
-    grads = reduce_weights(send_grads, rows, dab, hid)
+    back, dab, hid, swap = forward(scalars, rows, weights)
+    grads = reduce_weights(swap, rows, dab, hid)
     input_grad = lax.psum_scatter(back, "z", scatter_dimension=0, tiled=True)
     return (
         input_grad,

time: 190 us -> 189 us (level)
  waiting for transfers between devices: 92.5 us -> 87.3 us
  Pallas kernels: 27.7 us -> 29.9 us
    reduce_scatter x1, waiting for transfers between devices: 6.33 us -> 3.09 us  [local(): input_grad = lax.psum_scatter(back, 'z', scatter_dimension=0, tiled=True)]
    pallas_call x2, Pallas kernels: 10.1 us -> 13.3 us  [core_sum(): pl.pallas_call(other_kernel, grid_spec=pltpu.PrefetchScalarGridSpec(num_s...]
    unnamed x11 -> x13, local copies, waits for them, and re-layouts: 3.88 us -> 5.54 us
  transfers between devices with their start and end apart: 13 -> 13, of which waited for: 12 -> 11; matrix products, arithmetic and copies ran while one was open for 10% -> 10% of each run, Pallas kernels for 8% -> 10%
where the time goes in v6:
time: 189 us; the launch traced here: 187 us
  waiting for transfers between devices  87.3 us (46%)
  starting transfers between devices  31.3 us (17%)
  Pallas kernels  29.9 us (16%)
  other arithmetic  17.5 us (9%)
  between operations  14.4 us (8%)
  local copies, waits for them, and re-layouts  6.99 us (4%)
    ppermute x1, waiting for transfers between devices, partner_weights(): mine = lax.ppermute(half, 'yl', SWAP)  42.6 us
    all_gather x1, waiting for transfers between devices, local(): rows = lax.all_gather(send, 'z', axis=0, tiled=True)  23.8 us
    pallas_call x2, Pallas kernels, core_sum(): pl.pallas_call(other_kernel, grid_spec=pltpu.PrefetchScalarGridSpec(num_s...  13.3 us
    ppermute x4, starting transfers between devices, pair_sum(): last = lax.ppermute(add(second, got[1]), axes, step2)  12.9 us
    ppermute x4, starting transfers between devices, pair_sum(): got = lax.ppermute(send, axes, step1)  10.9 us
    pallas_call x1, Pallas kernels, forward(): pl.pallas_call(forward_kernel, out_shape=(jax.ShapeDtypeStruct((count, wi...  10.7 us
    ppermute x4, waiting for transfers between devices, pair_sum(): last = lax.ppermute(add(second, got[1]), axes, step2)  9.79 us
    ppermute x4, waiting for transfers between devices, pair_sum(): got = lax.ppermute(send, axes, step1)  6.29 us
  transfers between devices with their start and end apart: 13, of which 11 were waited for; matrix products, arithmetic and copies ran while one was open for 10% of the time, Pallas kernels for 10%

profile of v6, /device:TPU:6, one launch (start us, length us, event | category | flops | bytes accessed | tf_op | source)
XLA Modules:
  0.0 187.5 jit_solution(13108935994403535627)
XLA Ops:
  7.2 0.7 convert_element_type.126
  7.9 0.7 broadcast_compare_fusion
  8.6 0.8 convert_reduce_fusion
  9.3 1.8 maximum_maximum_fusion
  11.2 3.1 %fusion.4 = bf16[2560,384]{1,0:T(8,128)(2,1)} fusion(s32[]{:T(128)S(6)} %select_n.108, bf16[2,2560,128]{2,1,0:T(8,128)(2,1)} %bitcast.76, bf16[2,2560,128]{2,1,0:T(8,128)(2,1)} %bitcast.77, bf16[2,2560,128]{2,1,0:T(8,128)(2,1)} %bitcast.78), kind=kLoop, calls=%fused_computation.9 | loop fusion | flops 5898240 | bytes 5898244 | tf_op jit(solution)/shard_map/jit(dynamic_index_in_dim)/squeeze | solution.py:345
  14.3 3.6 %collective-permute-start = (bf16[2560,384]{1,0:T(8,128)(2,1)}, bf16[2560,384]{1,0:T(8,128)(2,1)}, u32[]{:S(2)}, u32[]{:S(2)}) collective-permute-start(bf16[2560,384]{1,0:T(8,128)(2,1)} %fusion.4), channel_id=1, source_target_pairs={{0,16},{16,0},{1,17},{17,1},{2,18},{18,2},{3,19},{19,3},{4,20},{20... | collective-permute-start | bytes 5898248 | tf_op jit(solution)/shard_map/ppermute | solution.py:404
  18.0 0.6 pad_add_fusion.scalars
  18.6 42.6 %collective-permute-done = bf16[2560,384]{1,0:T(8,128)(2,1)} collective-permute-done((bf16[2560,384]{1,0:T(8,128)(2,1)}, bf16[2560,384]{1,0:T(8,128)(2,1)}, u32[]{:S(2)}, u32[]{:S(2)}) %collective-permute-start) | collective-permute-done | bytes 1966112 | tf_op jit(solution)/shard_map/ppermute | solution.py:404
  61.2 1.9 %collective-permute-start.1 = (bf16[2560,384]{1,0:T(8,128)(2,1)}, bf16[2560,384]{1,0:T(8,128)(2,1)S(1)}, u32[]{:S(2)}, u32[]{:S(2)}) collective-permute-start(bf16[2560,384]{1,0:T(8,128)(2,1)} %collective-permute-done), channel_id=1, source_target_pairs={{0,32},{32,0},{1,33},{33,1},{2,34},{34,2},{3,35},{35,3},{4,36},{36... | collective-permute-start | bytes 5898248 | tf_op jit(solution)/shard_map/ppermute | solution.py:405
  63.1 1.2 bitcast_dynamic-update-slice_fusion.2
  64.3 1.2 bitcast_dynamic-update-slice_fusion.1
  65.6 1.7 collective-permute-done.1
  67.3 1.9 %broadcast_select_fusion = (bf16[2560,384]{1,0:T(8,128)(2,1)S(1)}, bf16[2560,384]{1,0:T(8,128)(2,1)S(1)}) fusion(bf16[2560,384]{1,0:T(8,128)(2,1)S(1)} %collective-permute-done.1, bf16[2560,384]{1,0:T(8,128)(2,1)} %collective-permute-done, pred[]{:T(512)S(6)} %eq.39), kind=kLoop, calls=%fused_computation.10 | loop fusion | flops 1966080 | bytes 7864321 | tf_op jit(solution)/shard_map/jit(_where)/select_n | solution.py:407
  69.2 1.8 fusion.1
  71.0 0.1 copy-done.3
  71.1 1.2 bitcast_dynamic-update-slice_fusion
  72.3 1.3 fusion.5.weights
  73.6 23.8 %all-gather.2.cloned.1.call-done = bf16[512,5248]{1,0:T(8,128)(2,1)} async-done(((bf16[32,5248]{1,0:T(8,128)(2,1)}), bf16[512,5248]{1,0:T(8,128)(2,1)}) %all-gather.2.cloned.1.call-update) | async-done | bytes 5373968 | tf_op jit(solution)/shard_map/all_gather | solution.py:425
  97.4 10.7 %shard_map.111 = (bf16[256,5120]{1,0:T(8,128)(2,1)}, bf16[256,512]{1,0:T(8,128)(2,1)}, bf16[256,256]{1,0:T(8,128)(2,1)}, bf16[9,16,32,384]{3,2,1,0:T(8,128)(2,1)}) custom-call(s32[3]{0:T(128)} %pad_add_fusion.scalars, bf16[16,32,5248]{2,1,0:T(8,128)(2,1)} %bitcast.74, bf16[5120,768]{1,0:T(8,128)(2,1)} %fusion.5.weights), custom_call_target="tpu_custom_call" | custom-call | flops 3355443200 | bytes 20000000 | tf_op jit(solution)/shard_map/pallas_call | solution.py:170
  108.0 1.9 %collective-permute-start.2 = (bf16[9,16,32,384]{3,2,1,0:T(8,128)(2,1)}, bf16[9,16,32,384]{3,2,1,0:T(8,128)(2,1)S(1)}, u32[]{:S(2)}, u32[]{:S(2)}) collective-permute-start(bf16[9,16,32,384]{3,2,1,0:T(8,128)(2,1)} %get-tuple-element.15), channel_id=1, source_target_pairs={{0,32},{32,0},{1,33},{33,1},{2,34},{34,2},{3,35},{35,3},{4,36},{36... | collective-permute-start | bytes 10616840 | tf_op jit(solution)/shard_map/ppermute | solution.py:390
  110.1 0.7 stack.106.place
  110.7 5.9 %shard_map.112.keep_a.keep_b = bf16[8,320,768]{2,1,0:T(8,128)(2,1)} custom-call(s32[1]{0:T(128)} %bitcast.19.part, bf16[16,32,5248]{2,1,0:T(8,128)(2,1)} %bitcast.75, bf16[256,512]{1,0:T(8,128)(2,1)} %get-tuple-element.13.dab, bf16[256,256]{1,0:T(8,128)(2,1)} %get-tuple-element.14.hid), custom_call_target="tpu_custom_call" | custom-call | flops 1006632960 | bytes 9000000 | tf_op jit(solution)/shard_map/pallas_call | solution.py:209
  116.7 1.8 copy-done
  118.5 6.7 %shard_map.114 = (bf16[2,2,160,768]{3,2,1,0:T(8,128)(2,1)}, bf16[2,4,160,384]{3,2,1,0:T(8,128)(2,1)}) custom-call(s32[13]{0:T(128)} %stack.106.place, bf16[8,320,768]{2,1,0:T(8,128)(2,1)} %shard_map.112.keep_a.keep_b, bf16[8,320,768]{2,1,0:T(8,128)(2,1)} %shard_map.112.keep_a.keep_b, bf16[9,16,32,384]{3,2,1,0:T(8,128)(2,1)} %copy-done, ...), custom_call_target="tpu_custom_call" | custom-call | flops 503316480 | bytes 9000000 | tf_op jit(solution)/shard_map/pallas_call | solution.py:300
  125.1 3.4 %collective-permute-start.7 = (bf16[2,4,160,384]{3,2,1,0:T(8,128)(2,1)}, bf16[2,4,160,384]{3,2,1,0:T(8,128)(2,1)S(1)}, u32[]{:S(2)}, u32[]{:S(2)}) collective-permute-start(bf16[2,4,160,384]{3,2,1,0:T(8,128)(2,1)} %get-tuple-element.19), channel_id=1, source_target_pairs={{0,16},{32,304},{16,0},{48,288},{256,272},{288,48},{272,256},{304,... | collective-permute-start | bytes 2949128 | tf_op jit(solution)/shard_map/ppermute | solution.py:365
  128.5 2.9 %collective-permute-start.3 = (bf16[2,2,160,768]{3,2,1,0:T(8,128)(2,1)}, bf16[2,2,160,768]{3,2,1,0:T(8,128)(2,1)S(1)}, u32[]{:S(2)}, u32[]{:S(2)}) collective-permute-start(bf16[2,2,160,768]{3,2,1,0:T(8,128)(2,1)} %get-tuple-element.17), channel_id=1, source_target_pairs={{0,64},{32,224},{64,0},{96,160},{128,192},{160,96},{192,128},{224,... | collective-permute-start | bytes 2949128 | tf_op jit(solution)/shard_map/ppermute | solution.py:365
  131.4 0.7 stack.97.place
  132.1 6.6 %shard_map.113 = (bf16[2,2,160,768]{3,2,1,0:T(8,128)(2,1)}, bf16[2,4,160,384]{3,2,1,0:T(8,128)(2,1)}) custom-call(s32[13]{0:T(128)} %stack.97.place, bf16[8,320,768]{2,1,0:T(8,128)(2,1)} %shard_map.112.keep_a.keep_b, bf16[8,320,768]{2,1,0:T(8,128)(2,1)} %shard_map.112.keep_a.keep_b, bf16[9,16,32,384]{3,2,1,0:T(8,128)(2,1)} %copy-done, ...), custom_call_target="tpu_custom_call" | custom-call | flops 503316480 | bytes 9000000 | tf_op jit(solution)/shard_map/pallas_call | solution.py:300
  138.7 2.6 %collective-permute-done.7 = bf16[2,4,160,384]{3,2,1,0:T(8,128)(2,1)S(1)} collective-permute-done((bf16[2,4,160,384]{3,2,1,0:T(8,128)(2,1)}, bf16[2,4,160,384]{3,2,1,0:T(8,128)(2,1)S(1)}, u32[]{:S(2)}, u32[]{:S(2)}) %collective-permute-start.7) | collective-permute-done | bytes 983072 | tf_op jit(solution)/shard_map/ppermute | solution.py:365
  141.3 1.2 fusion.9
  142.5 4.6 %collective-permute-start.8 = (bf16[4,160,384]{2,1,0:T(8,128)(2,1)S(1)}, bf16[4,160,384]{2,1,0:T(8,128)(2,1)}, u32[]{:S(2)}, u32[]{:S(2)}) collective-permute-start(bf16[4,160,384]{2,1,0:T(8,128)(2,1)S(1)} %fusion.9), channel_id=1, source_target_pairs={{0,272},{32,48},{16,256},{48,32},{256,16},{288,304},{272,0},{304,2... | collective-permute-start | bytes 1474568 | tf_op jit(solution)/shard_map/ppermute | solution.py:366
  147.2 1.2 fusion.8
  148.4 2.7 %collective-permute-start.4 = (bf16[2,160,768]{2,1,0:T(8,128)(2,1)S(1)}, bf16[2,160,768]{2,1,0:T(8,128)(2,1)S(1)}, u32[]{:S(2)}, u32[]{:S(2)}) collective-permute-start(bf16[2,160,768]{2,1,0:T(8,128)(2,1)S(1)} %fusion.8), channel_id=1, source_target_pairs={{0,192},{32,96},{64,128},{96,32},{128,64},{160,224},{192,0},{224,1... | collective-permute-start | bytes 1474568 | tf_op jit(solution)/shard_map/ppermute | solution.py:366
  151.1 3.5 %collective-permute-done.8 = bf16[4,160,384]{2,1,0:T(8,128)(2,1)} collective-permute-done((bf16[4,160,384]{2,1,0:T(8,128)(2,1)S(1)}, bf16[4,160,384]{2,1,0:T(8,128)(2,1)}, u32[]{:S(2)}, u32[]{:S(2)}) %collective-permute-start.8) | collective-permute-done | bytes 491552 | tf_op jit(solution)/shard_map/ppermute | solution.py:366
  154.6 1.4 fusion.6
  156.1 2.8 %collective-permute-start.9 = (bf16[2,160,384]{2,1,0:T(8,128)(2,1)S(1)}, bf16[2,160,384]{2,1,0:T(8,128)(2,1)S(1)}, u32[]{:S(2)}, u32[]{:S(2)}) collective-permute-start(bf16[2,160,384]{2,1,0:T(8,128)(2,1)S(1)} %pad_maximum_fusion.2), channel_id=1, source_target_pairs={{0,64},{32,224},{64,0},{96,160},{128,192},{160,96},{192,128},{224,... | collective-permute-start | bytes 737288 | tf_op jit(solution)/shard_map/ppermute | solution.py:365
  158.8 1.5 collective-permute-done.4
  160.3 0.2 fusion.7
  160.6 1.9 %collective-permute-start.5 = (bf16[2,160,384]{2,1,0:T(8,128)(2,1)S(1)}, bf16[2,160,384]{2,1,0:T(8,128)(2,1)S(1)}, u32[]{:S(2)}, u32[]{:S(2)}) collective-permute-start(bf16[2,160,384]{2,1,0:T(8,128)(2,1)S(1)} %pad_maximum_fusion.1), channel_id=1, source_target_pairs={{0,16},{32,304},{16,0},{48,288},{256,272},{288,48},{272,256},{304,... | collective-permute-start | bytes 737288 | tf_op jit(solution)/shard_map/ppermute | solution.py:365
  162.6 1.6 collective-permute-done.9
  164.2 2.4 %collective-permute-start.10 = (bf16[160,384]{1,0:T(8,128)(2,1)S(1)}, bf16[160,384]{1,0:T(8,128)(2,1)S(1)}, u32[]{:S(2)}, u32[]{:S(2)}) collective-permute-start(bf16[160,384]{1,0:T(8,128)(2,1)S(1)} %fusion.14), channel_id=1, source_target_pairs={{0,192},{32,96},{64,128},{96,32},{128,64},{160,224},{192,0},{224,1... | collective-permute-start | bytes 368648 | tf_op jit(solution)/shard_map/ppermute | solution.py:366
  166.6 2.1 %collective-permute-done.5 = bf16[2,160,384]{2,1,0:T(8,128)(2,1)S(1)} collective-permute-done((bf16[2,160,384]{2,1,0:T(8,128)(2,1)S(1)}, bf16[2,160,384]{2,1,0:T(8,128)(2,1)S(1)}, u32[]{:S(2)}, u32[]{:S(2)}) %collective-permute-start.5) | collective-permute-done | bytes 245792 | tf_op jit(solution)/shard_map/ppermute | solution.py:365
  168.8 3.2 %collective-permute-start.6 = (bf16[160,384]{1,0:T(8,128)(2,1)S(1)}, bf16[160,384]{1,0:T(8,128)(2,1)S(1)}, u32[]{:S(2)}, u32[]{:S(2)}) collective-permute-start(bf16[160,384]{1,0:T(8,128)(2,1)S(1)} %fusion.10), channel_id=1, source_target_pairs={{0,272},{32,48},{16,256},{48,32},{256,16},{288,304},{272,0},{304,2... | collective-permute-start | bytes 368648 | tf_op jit(solution)/shard_map/ppermute | solution.py:366
  171.9 0.2 collective-permute-done.10
  172.2 0.1 fusion.13
  172.2 4.5 %collective-permute-done.6 = bf16[160,384]{1,0:T(8,128)(2,1)S(1)} collective-permute-done((bf16[160,384]{1,0:T(8,128)(2,1)S(1)}, bf16[160,384]{1,0:T(8,128)(2,1)S(1)}, u32[]{:S(2)}, u32[]{:S(2)}) %collective-permute-start.6) | collective-permute-done | bytes 122912 | tf_op jit(solution)/shard_map/ppermute | solution.py:366
  176.8 0.7 fusion.19
  177.5 3.1 %reduce-scatter.2.cloned.1.call-done = bf16[16,5120]{1,0:T(8,128)(2,1)} async-done(((bf16[256,5120]{1,0:T(8,128)(2,1)}), bf16[16,5120]{1,0:T(8,128)(2,1)}) %reduce-scatter.2.cloned.1.call-update) | async-done | bytes 163856 | tf_op jit(solution)/shard_map/reduce_scatter | solution.py:438
  (24 shorter events, 0.5 us)
Async XLA Ops:
  7.2 90.2 %all-gather.2.cloned.1.call-start = ((), (), s32[]{:S(2)}) async-start(), calls=%async_computation.1 | async-start | bytes 5709824 | tf_op jit(solution)/shard_map/all_gather | solution.py:425
  11.1 169.5 %reduce-scatter.2.cloned.1.call-start = ((), (), s32[]{:S(2)}) async-start(), calls=%async_computation.2 | async-start | bytes 2785280 | tf_op jit(solution)/shard_map/reduce_scatter | solution.py:438
  11.2 52.0 %copy-start.1 = (bf16[1,5120,128]{2,1,0:T(8,128)(2,1)S(1)}, bf16[1,5120,128]{2,1,0:T(8,128)(2,1)}, u32[]{:S(2)}) copy-start(bf16[1,5120,128]{2,1,0:T(8,128)(2,1)} %param.13) | copy-start | bytes 3932164
  14.3 50.0 %copy-start.2 = (bf16[1,5120,128]{2,1,0:T(8,128)(2,1)S(1)}, bf16[1,5120,128]{2,1,0:T(8,128)(2,1)}, u32[]{:S(2)}) copy-start(bf16[1,5120,128]{2,1,0:T(8,128)(2,1)} %param.14) | copy-start | bytes 3932164
  14.3 46.9 %collective-permute-start = (bf16[2560,384]{1,0:T(8,128)(2,1)}, bf16[2560,384]{1,0:T(8,128)(2,1)}, u32[]{:S(2)}, u32[]{:S(2)}) collective-permute-start(bf16[2560,384]{1,0:T(8,128)(2,1)} %fusion.4), channel_id=1, source_target_pairs={{0,16},{16,0},{1,17},{17,1},{2,18},{18,2},{3,19},{19,3},{4,20},{20... | collective-permute-start | bytes 5898248 | tf_op jit(solution)/shard_map/ppermute | solution.py:404
  61.2 6.1 %collective-permute-start.1 = (bf16[2560,384]{1,0:T(8,128)(2,1)}, bf16[2560,384]{1,0:T(8,128)(2,1)S(1)}, u32[]{:S(2)}, u32[]{:S(2)}) collective-permute-start(bf16[2560,384]{1,0:T(8,128)(2,1)} %collective-permute-done), channel_id=1, source_target_pairs={{0,32},{32,0},{1,33},{33,1},{2,34},{34,2},{3,35},{35,3},{4,36},{36... | collective-permute-start | bytes 5898248 | tf_op jit(solution)/shard_map/ppermute | solution.py:405
  69.2 1.9 copy-start.3
  108.0 8.7 %collective-permute-start.2 = (bf16[9,16,32,384]{3,2,1,0:T(8,128)(2,1)}, bf16[9,16,32,384]{3,2,1,0:T(8,128)(2,1)S(1)}, u32[]{:S(2)}, u32[]{:S(2)}) collective-permute-start(bf16[9,16,32,384]{3,2,1,0:T(8,128)(2,1)} %get-tuple-element.15), channel_id=1, source_target_pairs={{0,32},{32,0},{1,33},{33,1},{2,34},{34,2},{3,35},{35,3},{4,36},{36... | collective-permute-start | bytes 10616840 | tf_op jit(solution)/shard_map/ppermute | solution.py:390
  116.7 1.8 copy-start
  125.1 16.2 %collective-permute-start.7 = (bf16[2,4,160,384]{3,2,1,0:T(8,128)(2,1)}, bf16[2,4,160,384]{3,2,1,0:T(8,128)(2,1)S(1)}, u32[]{:S(2)}, u32[]{:S(2)}) collective-permute-start(bf16[2,4,160,384]{3,2,1,0:T(8,128)(2,1)} %get-tuple-element.19), channel_id=1, source_target_pairs={{0,16},{32,304},{16,0},{48,288},{256,272},{288,48},{272,256},{304,... | collective-permute-start | bytes 2949128 | tf_op jit(solution)/shard_map/ppermute | solution.py:365
  128.5 18.7 %collective-permute-start.3 = (bf16[2,2,160,768]{3,2,1,0:T(8,128)(2,1)}, bf16[2,2,160,768]{3,2,1,0:T(8,128)(2,1)S(1)}, u32[]{:S(2)}, u32[]{:S(2)}) collective-permute-start(bf16[2,2,160,768]{3,2,1,0:T(8,128)(2,1)} %get-tuple-element.17), channel_id=1, source_target_pairs={{0,64},{32,224},{64,0},{96,160},{128,192},{160,96},{192,128},{224,... | collective-permute-start | bytes 2949128 | tf_op jit(solution)/shard_map/ppermute | solution.py:365
  141.3 19.0 %copy-start.4 = (bf16[2,2,160,768]{3,2,1,0:T(8,128)(2,1)S(1)}, bf16[2,2,160,768]{3,2,1,0:T(8,128)(2,1)}, u32[]{:S(2)}) copy-start(bf16[2,2,160,768]{3,2,1,0:T(8,128)(2,1)} %get-tuple-element.16) | copy-start | bytes 2949124
  142.5 12.0 %collective-permute-start.8 = (bf16[4,160,384]{2,1,0:T(8,128)(2,1)S(1)}, bf16[4,160,384]{2,1,0:T(8,128)(2,1)}, u32[]{:S(2)}, u32[]{:S(2)}) collective-permute-start(bf16[4,160,384]{2,1,0:T(8,128)(2,1)S(1)} %fusion.9), channel_id=1, source_target_pairs={{0,272},{32,48},{16,256},{48,32},{256,16},{288,304},{272,0},{304,2... | collective-permute-start | bytes 1474568 | tf_op jit(solution)/shard_map/ppermute | solution.py:366
  148.4 11.9 %collective-permute-start.4 = (bf16[2,160,768]{2,1,0:T(8,128)(2,1)S(1)}, bf16[2,160,768]{2,1,0:T(8,128)(2,1)S(1)}, u32[]{:S(2)}, u32[]{:S(2)}) collective-permute-start(bf16[2,160,768]{2,1,0:T(8,128)(2,1)S(1)} %fusion.8), channel_id=1, source_target_pairs={{0,192},{32,96},{64,128},{96,32},{128,64},{160,224},{192,0},{224,1... | collective-permute-start | bytes 1474568 | tf_op jit(solution)/shard_map/ppermute | solution.py:366
  156.1 8.1 %collective-permute-start.9 = (bf16[2,160,384]{2,1,0:T(8,128)(2,1)S(1)}, bf16[2,160,384]{2,1,0:T(8,128)(2,1)S(1)}, u32[]{:S(2)}, u32[]{:S(2)}) collective-permute-start(bf16[2,160,384]{2,1,0:T(8,128)(2,1)S(1)} %pad_maximum_fusion.2), channel_id=1, source_target_pairs={{0,64},{32,224},{64,0},{96,160},{128,192},{160,96},{192,128},{224,... | collective-permute-start | bytes 737288 | tf_op jit(solution)/shard_map/ppermute | solution.py:365
  160.6 8.1 %collective-permute-start.5 = (bf16[2,160,384]{2,1,0:T(8,128)(2,1)S(1)}, bf16[2,160,384]{2,1,0:T(8,128)(2,1)S(1)}, u32[]{:S(2)}, u32[]{:S(2)}) collective-permute-start(bf16[2,160,384]{2,1,0:T(8,128)(2,1)S(1)} %pad_maximum_fusion.1), channel_id=1, source_target_pairs={{0,16},{32,304},{16,0},{48,288},{256,272},{288,48},{272,256},{304,... | collective-permute-start | bytes 737288 | tf_op jit(solution)/shard_map/ppermute | solution.py:365
  164.2 8.0 %collective-permute-start.10 = (bf16[160,384]{1,0:T(8,128)(2,1)S(1)}, bf16[160,384]{1,0:T(8,128)(2,1)S(1)}, u32[]{:S(2)}, u32[]{:S(2)}) collective-permute-start(bf16[160,384]{1,0:T(8,128)(2,1)S(1)} %fusion.14), channel_id=1, source_target_pairs={{0,192},{32,96},{64,128},{96,32},{128,64},{160,224},{192,0},{224,1... | collective-permute-start | bytes 368648 | tf_op jit(solution)/shard_map/ppermute | solution.py:366
  168.8 8.0 %collective-permute-start.6 = (bf16[160,384]{1,0:T(8,128)(2,1)S(1)}, bf16[160,384]{1,0:T(8,128)(2,1)S(1)}, u32[]{:S(2)}, u32[]{:S(2)}) collective-permute-start(bf16[160,384]{1,0:T(8,128)(2,1)S(1)} %fusion.10), channel_id=1, source_target_pairs={{0,272},{32,48},{16,256},{48,32},{256,16},{288,304},{272,0},{304,2... | collective-permute-start | bytes 368648 | tf_op jit(solution)/shard_map/ppermute | solution.py:366
Sparse Core Ops, SparseCore 0:
  11.2 86.0 all-gather.1
  110.1 70.4 reduce-scatter.1

commit v7 on v6

--- a/solution.py
+++ b/solution.py
@@ -9,9 +9,10 @@
 WINDOW_EXPERTS = 4
 SPLIT = 8
 PAD = 128
-CHUNKS = 5
+CHUNKS = 10
 BLOCKS = 8
 VMEM_LIMIT = 60 * 1024 * 1024
+VMEM_SMALL = 24 * 1024 * 1024
 SWAP = [(0, 1), (1, 0)]
 
 
@@ -183,7 +184,7 @@
             pltpu.VMEM((CHUNKS, count, chunk), bf16),
             pltpu.VMEM((n_z, both, reach), bf16),
             pltpu.VMEM((count, cols), jnp.float32),
-            pltpu.SemaphoreType.DMA((5, BLOCKS + 1)),
+            pltpu.SemaphoreType.DMA((5, CHUNKS + BLOCKS)),
         ],
         compiler_params=pltpu.CompilerParams(vmem_limit_bytes=VMEM_LIMIT),
         cost_estimate=pl.CostEstimate(
@@ -219,7 +220,7 @@
             out_specs=pl.BlockSpec((per_step, height, cols), lambda i, part: (i, 0, 0)),
         ),
         out_shape=jax.ShapeDtypeStruct((BLOCKS, height, cols), jnp.bfloat16),
-        compiler_params=pltpu.CompilerParams(vmem_limit_bytes=VMEM_LIMIT),
+        compiler_params=pltpu.CompilerParams(vmem_limit_bytes=VMEM_SMALL),
         cost_estimate=pl.CostEstimate(
             flops=count * (padded - PAD) * cols, bytes_accessed=9_000_000, transcendentals=0
         ),
@@ -322,19 +323,47 @@
             jax.ShapeDtypeStruct((2, 2, cut, cols), keep.dtype),
             jax.ShapeDtypeStruct((2, n_x, cut, half), keep.dtype),
         ],
-        compiler_params=pltpu.CompilerParams(vmem_limit_bytes=VMEM_LIMIT),
+        compiler_params=pltpu.CompilerParams(vmem_limit_bytes=VMEM_SMALL),
         cost_estimate=pl.CostEstimate(
             flops=count * width * cols, bytes_accessed=9_000_000, transcendentals=0
         ),
     )(place, keep, keep, got, got, got)
 
 
-def route_columns(expert_index, slot, gate):
-    experts = jnp.arange(PAD, dtype=jnp.int32)
-    hit = (expert_index[:, :, None] == experts) & (slot >= 0)[:, :, None]
-    live = jnp.sum(hit.astype(jnp.float32), axis=1)
-    weight = jnp.sum(jnp.where(hit, gate[:, :, None].astype(jnp.float32), 0.0), axis=1)
-    return live.astype(jnp.bfloat16), weight.astype(jnp.bfloat16)
+def pack_kernel(expert_index, slot, gate, tokens, out_grad, out):
+    tok, width = tokens.shape
+    out[:tok, :width] = tokens[...]
+    out[tok:, :width] = out_grad[...]
+    square = (tok, tok)
+    eye = lax.broadcasted_iota(jnp.int32, square, 0) == lax.broadcasted_iota(jnp.int32, square, 1)
+
+    def column(row):
+        spread = jnp.broadcast_to(row.astype(jnp.float32), square)
+        return jnp.sum(jnp.where(eye, spread, 0.0), axis=1, keepdims=True)
+
+    lanes = lax.broadcasted_iota(jnp.int32, (tok, PAD), 1).astype(jnp.float32)
+    live, weight = jnp.zeros((tok, PAD), jnp.float32), jnp.zeros((tok, PAD), jnp.float32)
+    gates = gate[...].astype(jnp.float32)
+    for r in range(expert_index.shape[0]):
+        row = slice(r, r + 1)
+        hit = (lanes == column(expert_index[row])) & (column(slot[row]) >= 0)
+        live += jnp.where(hit, 1.0, 0.0)
+        weight += jnp.where(hit, column(gates[row]), 0.0)
+    out[:tok, width:] = live.astype(out.dtype)
+    out[tok:, width:] = weight.astype(out.dtype)
+
+
+def pack(tokens, out_grad, expert_index, slot, gate):
+    tok, width = tokens.shape
+    vmem = pl.BlockSpec(memory_space=pltpu.VMEM)
+    return pl.pallas_call(
+        pack_kernel,
+        out_shape=jax.ShapeDtypeStruct((2 * tok, width + PAD), tokens.dtype),
+        in_specs=[vmem] * 5,
+        out_specs=vmem,
+        compiler_params=pltpu.CompilerParams(vmem_limit_bytes=VMEM_LIMIT),
+        cost_estimate=pl.CostEstimate(flops=0, bytes_accessed=700_000, transcendentals=0),
+    )(expert_index.T, slot.T, gate.T, tokens, out_grad)
 
 
 def add(*terms):
@@ -414,14 +443,7 @@
     yl, z = lax.axis_index("yl"), lax.axis_index("z")
     experts = [(row * n_z + z) // SPLIT for row in (yl, 1 - yl)]
 
-    live, weight = route_columns(expert_index, slot, gate)
-    send = jnp.concatenate(
-        [
-            jnp.concatenate([tokens, live], axis=1),
-            jnp.concatenate([out_grad, weight], axis=1),
-        ],
-        axis=0,
-    )
+    send = pack(tokens, out_grad, expert_index, slot, gate)
     rows = lax.all_gather(send, "z", axis=0, tiled=True)
 
     own = jnp.concatenate([w_gate[0], w_up[0], w_down[0]], axis=1)

time: 189 us -> 187 us (0.989)
  Pallas kernels: 29.9 us -> 21.5 us
  waiting for transfers between devices: 87.3 us -> 93 us
  local copies, waits for them, and re-layouts: 6.99 us -> 11.6 us
  other arithmetic: 17.5 us -> 14.8 us
    pallas_call x2, Pallas kernels: 13.3 us -> 6.63 us  [core_sum(): pl.pallas_call(other_kernel, grid_spec=pltpu.PrefetchScalarGridSpec(num_s...]
    unnamed x13 -> x25, local copies, waits for them, and re-layouts: 5.54 us -> 11.3 us
    pallas_call x1, Pallas kernels: 5.94 us -> 2.5 us  [weight_grads(): pl.pallas_call(grads_kernel, grid_spec=pltpu.PrefetchScalarGridSpec(num_s...]
    reduce_scatter x1, waiting for transfers between devices: 3.09 us -> 6.36 us  [local(): input_grad = lax.psum_scatter(back, 'z', scatter_dimension=0, tiled=True)]
  transfers between devices with their start and end apart: 13 -> 13, of which waited for: 11 -> 10; matrix products, arithmetic and copies ran while one was open for 10% -> 10% of each run, Pallas kernels for 10% -> 5%
where the time goes in v7:
time: 187 us
  waiting for transfers between devices  93 us (50%)
  starting transfers between devices  31.2 us (17%)
  Pallas kernels  21.5 us (11%)
  other arithmetic  14.8 us (8%)
  between operations  14.5 us (8%)
  local copies, waits for them, and re-layouts  11.6 us (6%)
    ppermute x1, waiting for transfers between devices, partner_weights(): mine = lax.ppermute(half, 'yl', SWAP)  42.6 us
    all_gather x1, waiting for transfers between devices, local(): rows = lax.all_gather(send, 'z', axis=0, tiled=True)  24.7 us
    ppermute x4, starting transfers between devices, pair_sum(): last = lax.ppermute(add(second, got[1]), axes, step2)  12.6 us
    unnamed x25, local copies, waits for them, and re-layouts  11.3 us
    ppermute x4, starting transfers between devices, pair_sum(): got = lax.ppermute(send, axes, step1)  11 us
    pallas_call x1, Pallas kernels, forward(): pl.pallas_call(forward_kernel, out_shape=(jax.ShapeDtypeStruct((count, wi...  10.5 us
    ppermute x4, waiting for transfers between devices, pair_sum(): last = lax.ppermute(add(second, got[1]), axes, step2)  10 us
    ppermute x4, waiting for transfers between devices, pair_sum(): got = lax.ppermute(send, axes, step1)  7.63 us
  transfers between devices with their start and end apart: 13, of which 10 were waited for; matrix products, arithmetic and copies ran while one was open for 10% of the time, Pallas kernels for 5%

profile of v7, /device:TPU:6, one launch (start us, length us, event | category | flops | bytes accessed | tf_op | source)
XLA Modules:
  0.0 186.6 jit_solution(6394440262725140250)
XLA Ops:
  7.2 1.9 %shard_map.111 = bf16[32,5248]{1,0:T(8,128)(2,1)} custom-call(s32[2,16]{1,0:T(2,128)} %bitcast.82, s32[2,16]{1,0:T(2,128)} %bitcast.83, bf16[2,16]{1,0:T(2,128)(2,1)} %bitcast.84, bf16[16,5120]{1,0:T(8,128)(2,1)} %tokens.1, bf16[16,5120]{1,0:T(8,128)(2,1)} %out_grad.1), custom_call_target="tpu_custom_call" | custom-call | bytes 700000 | tf_op jit(solution)/shard_map/pallas_call | solution.py:359
  9.2 3.1 %fusion.4 = bf16[2560,384]{1,0:T(8,128)(2,1)} fusion(s32[]{:T(128)S(6)} %select_n.103, bf16[2,2560,128]{2,1,0:T(8,128)(2,1)} %bitcast.79, bf16[2,2560,128]{2,1,0:T(8,128)(2,1)} %bitcast.80, bf16[2,2560,128]{2,1,0:T(8,128)(2,1)} %bitcast.81), kind=kLoop, calls=%fused_computation.9 | loop fusion | flops 5898240 | bytes 5898244 | tf_op jit(solution)/shard_map/jit(dynamic_index_in_dim)/squeeze | solution.py:374
  12.3 3.6 %collective-permute-start = (bf16[2560,384]{1,0:T(8,128)(2,1)}, bf16[2560,384]{1,0:T(8,128)(2,1)}, u32[]{:S(2)}, u32[]{:S(2)}) collective-permute-start(bf16[2560,384]{1,0:T(8,128)(2,1)} %fusion.4), channel_id=1, source_target_pairs={{0,16},{16,0},{1,17},{17,1},{2,18},{18,2},{3,19},{19,3},{4,20},{20... | collective-permute-start | bytes 5898248 | tf_op jit(solution)/shard_map/ppermute | solution.py:433
  16.0 0.6 pad_add_fusion.scalars
  16.6 42.6 %collective-permute-done = bf16[2560,384]{1,0:T(8,128)(2,1)} collective-permute-done((bf16[2560,384]{1,0:T(8,128)(2,1)}, bf16[2560,384]{1,0:T(8,128)(2,1)}, u32[]{:S(2)}, u32[]{:S(2)}) %collective-permute-start) | collective-permute-done | bytes 1966112 | tf_op jit(solution)/shard_map/ppermute | solution.py:433
  59.2 1.9 %collective-permute-start.1 = (bf16[2560,384]{1,0:T(8,128)(2,1)}, bf16[2560,384]{1,0:T(8,128)(2,1)S(1)}, u32[]{:S(2)}, u32[]{:S(2)}) collective-permute-start(bf16[2560,384]{1,0:T(8,128)(2,1)} %collective-permute-done), channel_id=1, source_target_pairs={{0,32},{32,0},{1,33},{33,1},{2,34},{34,2},{3,35},{35,3},{4,36},{36... | collective-permute-start | bytes 5898248 | tf_op jit(solution)/shard_map/ppermute | solution.py:434
  61.1 1.2 bitcast_dynamic-update-slice_fusion.2
  62.4 1.3 bitcast_dynamic-update-slice_fusion.1
  63.6 1.6 collective-permute-done.1
  65.3 1.9 %broadcast_select_fusion = (bf16[2560,384]{1,0:T(8,128)(2,1)S(1)}, bf16[2560,384]{1,0:T(8,128)(2,1)S(1)}) fusion(bf16[2560,384]{1,0:T(8,128)(2,1)S(1)} %collective-permute-done.1, bf16[2560,384]{1,0:T(8,128)(2,1)} %collective-permute-done, pred[]{:T(512)S(6)} %eq.23), kind=kLoop, calls=%fused_computation.10 | loop fusion | flops 1966080 | bytes 7864321 | tf_op jit(solution)/shard_map/jit(_where)/select_n | solution.py:436
  67.2 1.7 fusion.1
  68.9 0.1 copy-done.10
  69.0 1.3 bitcast_dynamic-update-slice_fusion
  70.3 1.2 fusion.5.weights
  71.5 24.7 %all-gather.2.cloned.1.call-done = bf16[512,5248]{1,0:T(8,128)(2,1)} async-done(((bf16[32,5248]{1,0:T(8,128)(2,1)}), bf16[512,5248]{1,0:T(8,128)(2,1)}) %all-gather.2.cloned.1.call-update) | async-done | bytes 5373968 | tf_op jit(solution)/shard_map/all_gather | solution.py:447
  96.2 10.5 %shard_map.112 = (bf16[256,5120]{1,0:T(8,128)(2,1)}, bf16[256,512]{1,0:T(8,128)(2,1)}, bf16[256,256]{1,0:T(8,128)(2,1)}, bf16[9,16,32,384]{3,2,1,0:T(8,128)(2,1)}) custom-call(s32[3]{0:T(128)} %pad_add_fusion.scalars, bf16[16,32,5248]{2,1,0:T(8,128)(2,1)} %bitcast.77, bf16[5120,768]{1,0:T(8,128)(2,1)} %fusion.5.weights), custom_call_target="tpu_custom_call" | custom-call | flops 3355443200 | bytes 20000000 | tf_op jit(solution)/shard_map/pallas_call | solution.py:171
  106.8 1.9 %collective-permute-start.2 = (bf16[9,16,32,384]{3,2,1,0:T(8,128)(2,1)}, bf16[9,16,32,384]{3,2,1,0:T(8,128)(2,1)S(1)}, u32[]{:S(2)}, u32[]{:S(2)}) collective-permute-start(bf16[9,16,32,384]{3,2,1,0:T(8,128)(2,1)} %get-tuple-element.15), channel_id=1, source_target_pairs={{0,32},{32,0},{1,33},{33,1},{2,34},{34,2},{3,35},{35,3},{4,36},{36... | collective-permute-start | bytes 10616840 | tf_op jit(solution)/shard_map/ppermute | solution.py:419
  108.8 0.1 stack.106.place
  108.9 2.5 %copy-done.2 = bf16[512,5248]{1,0:T(8,128)(2,1)S(1)} copy-done((bf16[512,5248]{1,0:T(8,128)(2,1)S(1)}, bf16[512,5248]{1,0:T(8,128)(2,1)}, u32[]{:S(2)}) %copy-start.2) | copy-done | bytes 5373976
  111.4 0.9 copy-done.6
  112.4 0.9 copy-done.7
  113.3 2.5 %shard_map.113.keep_a.keep_b = bf16[8,320,768]{2,1,0:T(8,128)(2,1)S(1)} custom-call(s32[1]{0:T(128)} %bitcast.22.part, bf16[16,32,5248]{2,1,0:T(8,128)(2,1)S(1)} %bitcast.78, bf16[256,512]{1,0:T(8,128)(2,1)S(1)} %copy-done.6, bf16[256,256]{1,0:T(8,128)(2,1)S(1)} %copy-done.7), custom_call_target="tpu_custom_call" | custom-call | flops 1006632960 | bytes 9000000 | tf_op jit(solution)/shard_map/pallas_call | solution.py:210
  115.8 3.9 %shard_map.115 = (bf16[2,2,160,768]{3,2,1,0:T(8,128)(2,1)}, bf16[2,4,160,384]{3,2,1,0:T(8,128)(2,1)}) custom-call(s32[13]{0:T(128)S(1)} %stack.106.place, bf16[8,320,768]{2,1,0:T(8,128)(2,1)S(1)} %shard_map.113.keep_a.keep_b, bf16[8,320,768]{2,1,0:T(8,128)(2,1)S(1)} %shard_map.113.keep_a.keep_b, ...), custom_call_target="tpu_custom_call" | custom-call | flops 503316480 | bytes 9000000 | tf_op jit(solution)/shard_map/pallas_call | solution.py:301
  119.7 3.4 %collective-permute-start.7 = (bf16[2,4,160,384]{3,2,1,0:T(8,128)(2,1)}, bf16[2,4,160,384]{3,2,1,0:T(8,128)(2,1)}, u32[]{:S(2)}, u32[]{:S(2)}) collective-permute-start(bf16[2,4,160,384]{3,2,1,0:T(8,128)(2,1)} %get-tuple-element.19), channel_id=1, source_target_pairs={{0,16},{32,304},{16,0},{48,288},{256,272},{288,48},{272,256},{304,... | collective-permute-start | bytes 2949128 | tf_op jit(solution)/shard_map/ppermute | solution.py:394
  123.1 3.0 %collective-permute-start.3 = (bf16[2,2,160,768]{3,2,1,0:T(8,128)(2,1)}, bf16[2,2,160,768]{3,2,1,0:T(8,128)(2,1)}, u32[]{:S(2)}, u32[]{:S(2)}) collective-permute-start(bf16[2,2,160,768]{3,2,1,0:T(8,128)(2,1)} %get-tuple-element.17), channel_id=1, source_target_pairs={{0,64},{32,224},{64,0},{96,160},{128,192},{160,96},{192,128},{224,... | collective-permute-start | bytes 2949128 | tf_op jit(solution)/shard_map/ppermute | solution.py:394
  126.1 0.1 stack.97.place
  126.2 2.1 %copy-done.1 = bf16[8,320,768]{2,1,0:T(8,128)(2,1)S(1)} copy-done((bf16[8,320,768]{2,1,0:T(8,128)(2,1)S(1)}, bf16[8,320,768]{2,1,0:T(8,128)(2,1)}, u32[]{:S(2)}) %copy-start.1) | copy-done | bytes 3932184
  128.3 2.7 %shard_map.114 = (bf16[2,2,160,768]{3,2,1,0:T(8,128)(2,1)S(1)}, bf16[2,4,160,384]{3,2,1,0:T(8,128)(2,1)S(1)}) custom-call(s32[13]{0:T(128)S(1)} %stack.97.place, bf16[8,320,768]{2,1,0:T(8,128)(2,1)S(1)} %copy-done.1, bf16[8,320,768]{2,1,0:T(8,128)(2,1)S(1)} %copy-done.1, bf16[9,16,32,384]{3,2,1,0:T(8,128)(2,1)S(1)} %collective-permute-done.2.got_a.got_b.acts, ...), custom_call_target="tpu_custom_call" | custom-call | flops 503316480 | bytes 9000000 | tf_op jit(solution)/shard_map/pallas_call | solution.py:301
  131.1 0.9 copy-done.3
  132.0 4.0 %collective-permute-done.7 = bf16[2,4,160,384]{3,2,1,0:T(8,128)(2,1)} collective-permute-done((bf16[2,4,160,384]{3,2,1,0:T(8,128)(2,1)}, bf16[2,4,160,384]{3,2,1,0:T(8,128)(2,1)}, u32[]{:S(2)}, u32[]{:S(2)}) %collective-permute-start.7) | collective-permute-done | bytes 983072 | tf_op jit(solution)/shard_map/ppermute | solution.py:394
  136.0 1.2 fusion.9
  137.2 4.6 %collective-permute-start.8 = (bf16[4,160,384]{2,1,0:T(8,128)(2,1)S(1)}, bf16[4,160,384]{2,1,0:T(8,128)(2,1)S(1)}, u32[]{:S(2)}, u32[]{:S(2)}) collective-permute-start(bf16[4,160,384]{2,1,0:T(8,128)(2,1)S(1)} %fusion.9), channel_id=1, source_target_pairs={{0,272},{32,48},{16,256},{48,32},{256,16},{288,304},{272,0},{304,2... | collective-permute-start | bytes 1474568 | tf_op jit(solution)/shard_map/ppermute | solution.py:395
  141.9 1.3 fusion.8
  143.2 2.6 %collective-permute-start.4 = (bf16[2,160,768]{2,1,0:T(8,128)(2,1)S(1)}, bf16[2,160,768]{2,1,0:T(8,128)(2,1)S(1)}, u32[]{:S(2)}, u32[]{:S(2)}) collective-permute-start(bf16[2,160,768]{2,1,0:T(8,128)(2,1)S(1)} %fusion.8), channel_id=1, source_target_pairs={{0,192},{32,96},{64,128},{96,32},{128,64},{160,224},{192,0},{224,1... | collective-permute-start | bytes 1474568 | tf_op jit(solution)/shard_map/ppermute | solution.py:395
  145.9 3.3 %collective-permute-done.8 = bf16[4,160,384]{2,1,0:T(8,128)(2,1)S(1)} collective-permute-done((bf16[4,160,384]{2,1,0:T(8,128)(2,1)S(1)}, bf16[4,160,384]{2,1,0:T(8,128)(2,1)S(1)}, u32[]{:S(2)}, u32[]{:S(2)}) %collective-permute-start.8) | collective-permute-done | bytes 491552 | tf_op jit(solution)/shard_map/ppermute | solution.py:395
  149.2 1.4 fusion.6
  150.7 2.7 %collective-permute-start.9 = (bf16[2,160,384]{2,1,0:T(8,128)(2,1)S(1)}, bf16[2,160,384]{2,1,0:T(8,128)(2,1)S(1)}, u32[]{:S(2)}, u32[]{:S(2)}) collective-permute-start(bf16[2,160,384]{2,1,0:T(8,128)(2,1)S(1)} %pad_maximum_fusion.2), channel_id=1, source_target_pairs={{0,64},{32,224},{64,0},{96,160},{128,192},{160,96},{192,128},{224,... | collective-permute-start | bytes 737288 | tf_op jit(solution)/shard_map/ppermute | solution.py:394
  153.4 1.8 collective-permute-done.4
  155.2 1.2 fusion.7
  156.5 1.9 %collective-permute-start.5 = (bf16[2,160,384]{2,1,0:T(8,128)(2,1)S(1)}, bf16[2,160,384]{2,1,0:T(8,128)(2,1)S(1)}, u32[]{:S(2)}, u32[]{:S(2)}) collective-permute-start(bf16[2,160,384]{2,1,0:T(8,128)(2,1)S(1)} %pad_maximum_fusion.1), channel_id=1, source_target_pairs={{0,16},{32,304},{16,0},{48,288},{256,272},{288,48},{272,256},{304,... | collective-permute-start | bytes 737288 | tf_op jit(solution)/shard_map/ppermute | solution.py:394
  158.4 0.3 collective-permute-done.9
  158.8 2.5 %collective-permute-start.10 = (bf16[160,384]{1,0:T(8,128)(2,1)S(1)}, bf16[160,384]{1,0:T(8,128)(2,1)S(1)}, u32[]{:S(2)}, u32[]{:S(2)}) collective-permute-start(bf16[160,384]{1,0:T(8,128)(2,1)S(1)} %fusion.14), channel_id=1, source_target_pairs={{0,192},{32,96},{64,128},{96,32},{128,64},{160,224},{192,0},{224,1... | collective-permute-start | bytes 368648 | tf_op jit(solution)/shard_map/ppermute | solution.py:395
  161.2 3.4 %collective-permute-done.5 = bf16[2,160,384]{2,1,0:T(8,128)(2,1)S(1)} collective-permute-done((bf16[2,160,384]{2,1,0:T(8,128)(2,1)S(1)}, bf16[2,160,384]{2,1,0:T(8,128)(2,1)S(1)}, u32[]{:S(2)}, u32[]{:S(2)}) %collective-permute-start.5) | collective-permute-done | bytes 245792 | tf_op jit(solution)/shard_map/ppermute | solution.py:394
  164.6 2.9 %collective-permute-start.6 = (bf16[160,384]{1,0:T(8,128)(2,1)S(1)}, bf16[160,384]{1,0:T(8,128)(2,1)S(1)}, u32[]{:S(2)}, u32[]{:S(2)}) collective-permute-start(bf16[160,384]{1,0:T(8,128)(2,1)S(1)} %fusion.10), channel_id=1, source_target_pairs={{0,272},{32,48},{16,256},{48,32},{256,16},{288,304},{272,0},{304,2... | collective-permute-start | bytes 368648 | tf_op jit(solution)/shard_map/ppermute | solution.py:395
  167.6 0.1 fusion.13
  167.7 5.0 %collective-permute-done.6 = bf16[160,384]{1,0:T(8,128)(2,1)S(1)} collective-permute-done((bf16[160,384]{1,0:T(8,128)(2,1)S(1)}, bf16[160,384]{1,0:T(8,128)(2,1)S(1)}, u32[]{:S(2)}, u32[]{:S(2)}) %collective-permute-start.6) | collective-permute-done | bytes 122912 | tf_op jit(solution)/shard_map/ppermute | solution.py:395
  172.7 0.7 fusion.19
  173.4 6.4 %reduce-scatter.2.cloned.1.call-done = bf16[16,5120]{1,0:T(8,128)(2,1)} async-done(((bf16[256,5120]{1,0:T(8,128)(2,1)}), bf16[16,5120]{1,0:T(8,128)(2,1)}) %reduce-scatter.2.cloned.1.call-update) | async-done | bytes 163856 | tf_op jit(solution)/shard_map/reduce_scatter | solution.py:460
  (33 shorter events, 0.5 us)
Async XLA Ops:
  7.2 89.0 %all-gather.2.cloned.1.call-start = ((), (), s32[]{:S(2)}) async-start(), calls=%async_computation.1 | async-start | bytes 5709824 | tf_op jit(solution)/shard_map/all_gather | solution.py:447
  9.1 170.7 %reduce-scatter.2.cloned.1.call-start = ((), (), s32[]{:S(2)}) async-start(), calls=%async_computation.2 | async-start | bytes 2785280 | tf_op jit(solution)/shard_map/reduce_scatter | solution.py:460
  9.2 52.0 %copy-start.8 = (bf16[1,5120,128]{2,1,0:T(8,128)(2,1)S(1)}, bf16[1,5120,128]{2,1,0:T(8,128)(2,1)}, u32[]{:S(2)}) copy-start(bf16[1,5120,128]{2,1,0:T(8,128)(2,1)} %param.13) | copy-start | bytes 3932164
  12.3 50.0 %copy-start.9 = (bf16[1,5120,128]{2,1,0:T(8,128)(2,1)S(1)}, bf16[1,5120,128]{2,1,0:T(8,128)(2,1)}, u32[]{:S(2)}) copy-start(bf16[1,5120,128]{2,1,0:T(8,128)(2,1)} %param.14) | copy-start | bytes 3932164
  12.3 46.9 %collective-permute-start = (bf16[2560,384]{1,0:T(8,128)(2,1)}, bf16[2560,384]{1,0:T(8,128)(2,1)}, u32[]{:S(2)}, u32[]{:S(2)}) collective-permute-start(bf16[2560,384]{1,0:T(8,128)(2,1)} %fusion.4), channel_id=1, source_target_pairs={{0,16},{16,0},{1,17},{17,1},{2,18},{18,2},{3,19},{19,3},{4,20},{20... | collective-permute-start | bytes 5898248 | tf_op jit(solution)/shard_map/ppermute | solution.py:433
  59.2 6.1 %collective-permute-start.1 = (bf16[2560,384]{1,0:T(8,128)(2,1)}, bf16[2560,384]{1,0:T(8,128)(2,1)S(1)}, u32[]{:S(2)}, u32[]{:S(2)}) collective-permute-start(bf16[2560,384]{1,0:T(8,128)(2,1)} %collective-permute-done), channel_id=1, source_target_pairs={{0,32},{32,0},{1,33},{33,1},{2,34},{34,2},{3,35},{35,3},{4,36},{36... | collective-permute-start | bytes 5898248 | tf_op jit(solution)/shard_map/ppermute | solution.py:434
  67.2 1.9 copy-start.10
  106.8 9.0 %collective-permute-start.2 = (bf16[9,16,32,384]{3,2,1,0:T(8,128)(2,1)}, bf16[9,16,32,384]{3,2,1,0:T(8,128)(2,1)S(1)}, u32[]{:S(2)}, u32[]{:S(2)}) collective-permute-start(bf16[9,16,32,384]{3,2,1,0:T(8,128)(2,1)} %get-tuple-element.15), channel_id=1, source_target_pairs={{0,32},{32,0},{1,33},{33,1},{2,34},{34,2},{3,35},{35,3},{4,36},{36... | collective-permute-start | bytes 10616840 | tf_op jit(solution)/shard_map/ppermute | solution.py:419
  108.9 2.5 %copy-start.2 = (bf16[512,5248]{1,0:T(8,128)(2,1)S(1)}, bf16[512,5248]{1,0:T(8,128)(2,1)}, u32[]{:S(2)}) copy-start(bf16[512,5248]{1,0:T(8,128)(2,1)} %all-gather.2.cloned.1.call-done) | copy-start | bytes 16121860
  111.4 0.9 copy-start.6
  112.4 0.9 copy-start.7
  115.8 3.9 %copy-start = (bf16[8,320,768]{2,1,0:T(8,128)(2,1)}, bf16[8,320,768]{2,1,0:T(8,128)(2,1)S(1)}, u32[]{:S(2)}) copy-start(bf16[8,320,768]{2,1,0:T(8,128)(2,1)S(1)} %shard_map.113.keep_a.keep_b) | copy-start | bytes 11796484
  119.7 16.3 %collective-permute-start.7 = (bf16[2,4,160,384]{3,2,1,0:T(8,128)(2,1)}, bf16[2,4,160,384]{3,2,1,0:T(8,128)(2,1)}, u32[]{:S(2)}, u32[]{:S(2)}) collective-permute-start(bf16[2,4,160,384]{3,2,1,0:T(8,128)(2,1)} %get-tuple-element.19), channel_id=1, source_target_pairs={{0,16},{32,304},{16,0},{48,288},{256,272},{288,48},{272,256},{304,... | collective-permute-start | bytes 2949128 | tf_op jit(solution)/shard_map/ppermute | solution.py:394
  123.1 18.8 %collective-permute-start.3 = (bf16[2,2,160,768]{3,2,1,0:T(8,128)(2,1)}, bf16[2,2,160,768]{3,2,1,0:T(8,128)(2,1)}, u32[]{:S(2)}, u32[]{:S(2)}) collective-permute-start(bf16[2,2,160,768]{3,2,1,0:T(8,128)(2,1)} %get-tuple-element.17), channel_id=1, source_target_pairs={{0,64},{32,224},{64,0},{96,160},{128,192},{160,96},{192,128},{224,... | collective-permute-start | bytes 2949128 | tf_op jit(solution)/shard_map/ppermute | solution.py:394
  126.2 2.1 %copy-start.1 = (bf16[8,320,768]{2,1,0:T(8,128)(2,1)S(1)}, bf16[8,320,768]{2,1,0:T(8,128)(2,1)}, u32[]{:S(2)}) copy-start(bf16[8,320,768]{2,1,0:T(8,128)(2,1)} %copy-done) | copy-start | bytes 11796484
  131.1 1.0 copy-start.3
  132.0 4.0 %copy-start.5 = (bf16[2,4,160,384]{3,2,1,0:T(8,128)(2,1)}, bf16[2,4,160,384]{3,2,1,0:T(8,128)(2,1)S(1)}, u32[]{:S(2)}) copy-start(bf16[2,4,160,384]{3,2,1,0:T(8,128)(2,1)S(1)} %get-tuple-element.18) | copy-start | bytes 2949124
  136.0 19.2 %copy-start.4 = (bf16[2,2,160,768]{3,2,1,0:T(8,128)(2,1)S(1)}, bf16[2,2,160,768]{3,2,1,0:T(8,128)(2,1)}, u32[]{:S(2)}) copy-start(bf16[2,2,160,768]{3,2,1,0:T(8,128)(2,1)} %copy-done.3) | copy-start | bytes 2949124
  137.2 11.9 %collective-permute-start.8 = (bf16[4,160,384]{2,1,0:T(8,128)(2,1)S(1)}, bf16[4,160,384]{2,1,0:T(8,128)(2,1)S(1)}, u32[]{:S(2)}, u32[]{:S(2)}) collective-permute-start(bf16[4,160,384]{2,1,0:T(8,128)(2,1)S(1)} %fusion.9), channel_id=1, source_target_pairs={{0,272},{32,48},{16,256},{48,32},{256,16},{288,304},{272,0},{304,2... | collective-permute-start | bytes 1474568 | tf_op jit(solution)/shard_map/ppermute | solution.py:395
  143.2 11.9 %collective-permute-start.4 = (bf16[2,160,768]{2,1,0:T(8,128)(2,1)S(1)}, bf16[2,160,768]{2,1,0:T(8,128)(2,1)S(1)}, u32[]{:S(2)}, u32[]{:S(2)}) collective-permute-start(bf16[2,160,768]{2,1,0:T(8,128)(2,1)S(1)} %fusion.8), channel_id=1, source_target_pairs={{0,192},{32,96},{64,128},{96,32},{128,64},{160,224},{192,0},{224,1... | collective-permute-start | bytes 1474568 | tf_op jit(solution)/shard_map/ppermute | solution.py:395
  150.7 8.1 %collective-permute-start.9 = (bf16[2,160,384]{2,1,0:T(8,128)(2,1)S(1)}, bf16[2,160,384]{2,1,0:T(8,128)(2,1)S(1)}, u32[]{:S(2)}, u32[]{:S(2)}) collective-permute-start(bf16[2,160,384]{2,1,0:T(8,128)(2,1)S(1)} %pad_maximum_fusion.2), channel_id=1, source_target_pairs={{0,64},{32,224},{64,0},{96,160},{128,192},{160,96},{192,128},{224,... | collective-permute-start | bytes 737288 | tf_op jit(solution)/shard_map/ppermute | solution.py:394
  156.5 8.1 %collective-permute-start.5 = (bf16[2,160,384]{2,1,0:T(8,128)(2,1)S(1)}, bf16[2,160,384]{2,1,0:T(8,128)(2,1)S(1)}, u32[]{:S(2)}, u32[]{:S(2)}) collective-permute-start(bf16[2,160,384]{2,1,0:T(8,128)(2,1)S(1)} %pad_maximum_fusion.1), channel_id=1, source_target_pairs={{0,16},{32,304},{16,0},{48,288},{256,272},{288,48},{272,256},{304,... | collective-permute-start | bytes 737288 | tf_op jit(solution)/shard_map/ppermute | solution.py:394
  158.8 8.8 %collective-permute-start.10 = (bf16[160,384]{1,0:T(8,128)(2,1)S(1)}, bf16[160,384]{1,0:T(8,128)(2,1)S(1)}, u32[]{:S(2)}, u32[]{:S(2)}) collective-permute-start(bf16[160,384]{1,0:T(8,128)(2,1)S(1)} %fusion.14), channel_id=1, source_target_pairs={{0,192},{32,96},{64,128},{96,32},{128,64},{160,224},{192,0},{224,1... | collective-permute-start | bytes 368648 | tf_op jit(solution)/shard_map/ppermute | solution.py:395
  164.6 8.0 %collective-permute-start.6 = (bf16[160,384]{1,0:T(8,128)(2,1)S(1)}, bf16[160,384]{1,0:T(8,128)(2,1)S(1)}, u32[]{:S(2)}, u32[]{:S(2)}) collective-permute-start(bf16[160,384]{1,0:T(8,128)(2,1)S(1)} %fusion.10), channel_id=1, source_target_pairs={{0,272},{32,48},{16,256},{48,32},{256,16},{288,304},{272,0},{304,2... | collective-permute-start | bytes 368648 | tf_op jit(solution)/shard_map/ppermute | solution.py:395
Sparse Core Ops, SparseCore 0:
  10.1 86.0 all-gather.1
  108.8 70.8 reduce-scatter.1

commit v8 on v7

--- a/solution.py
+++ b/solution.py
@@ -78,8 +78,9 @@
         return pl.ds(pl.multiple_of(k * chunk, 128), chunk)
 
     def row_copy(k):
-        at = columns(k)
-        return pltpu.make_async_copy(rows.at[:, :, at], rows_v.at[:, :, at], sems.at[0, k])
+        half, at = divmod(k * chunk, width // 2)
+        source = rows.at[:, half * both : (half + 1) * both, at : at + chunk]
+        return pltpu.make_async_copy(source, rows_v.at[:, :, columns(k)], sems.at[0, k])
 
     def weight_copy(k):
         return pltpu.make_async_copy(weights.at[columns(k), :], w_v.at[k], sems.at[1, k])
@@ -92,8 +93,9 @@
         return pltpu.make_async_copy(rows_v.at[:, :, at], swap.at[n], sems.at[3, n])
 
     acts_copy = pltpu.make_async_copy(acts_v, swap.at[blocks], sems.at[3, blocks])
-    last = pl.ds(width, PAD)
-    route_copy = pltpu.make_async_copy(rows.at[:, :, last], rows_v.at[:, :, last], sems.at[4, 0])
+    route_copy = pltpu.make_async_copy(
+        rows.at[:, :both, width // 2 :], rows_v.at[:, :, width:], sems.at[4, 0]
+    )
 
     for k in range(CHUNKS):
         row_copy(k).start()
@@ -161,7 +163,7 @@
 
 
 def forward(scalars, rows, weights):
-    n_z, both, padded = rows.shape
+    n_z, both = rows.shape[0], rows.shape[1] // 2
     width, cols = weights.shape
     hidden, chunk, count = cols // 6, width // CHUNKS, n_z * both // 2
     reach = -(-width // (2 * BLOCKS) // 128) * 128
@@ -179,7 +181,7 @@
         in_specs=[pl.BlockSpec(memory_space=pltpu.SMEM), hbm, hbm],
         out_specs=(hbm, vmem, vmem, hbm),
         scratch_shapes=[
-            pltpu.VMEM((n_z, both, padded), bf16),
+            pltpu.VMEM((n_z, both, width + PAD), bf16),
             pltpu.VMEM((CHUNKS, chunk, cols), bf16),
             pltpu.VMEM((CHUNKS, count, chunk), bf16),
             pltpu.VMEM((n_z, both, reach), bf16),
@@ -204,16 +206,20 @@
 
 
 def weight_grads(part, rows, dab, hid, per_step=2):
-    n_z, both, padded = rows.shape
-    height = (padded - PAD) // (2 * BLOCKS)
+    n_z, both = rows.shape[0], rows.shape[1] // 2
+    width = 2 * (rows.shape[2] - PAD)
+    height, steps = width // (2 * BLOCKS), BLOCKS // per_step
     count, cols = dab.shape[0], dab.shape[1] + hid.shape[1]
     return pl.pallas_call(
         grads_kernel,
         grid_spec=pltpu.PrefetchScalarGridSpec(
             num_scalar_prefetch=1,
-            grid=(BLOCKS // per_step,),
+            grid=(steps,),
             in_specs=[
-                pl.BlockSpec((n_z, both, 2 * height * per_step), lambda i, part: (0, 0, i)),
+                pl.BlockSpec(
+                    (n_z, both, 2 * height * per_step),
+                    lambda i, part: (0, i // (steps // 2), i % (steps // 2)),
+                ),
                 pl.BlockSpec(dab.shape, lambda i, part: (0, 0)),
                 pl.BlockSpec(hid.shape, lambda i, part: (0, 0)),
             ],
@@ -222,7 +228,7 @@
         out_shape=jax.ShapeDtypeStruct((BLOCKS, height, cols), jnp.bfloat16),
         compiler_params=pltpu.CompilerParams(vmem_limit_bytes=VMEM_SMALL),
         cost_estimate=pl.CostEstimate(
-            flops=count * (padded - PAD) * cols, bytes_accessed=9_000_000, transcendentals=0
+            flops=count * width * cols, bytes_accessed=9_000_000, transcendentals=0
         ),
     )(jnp.reshape(part, (1,)).astype(jnp.int32), rows, dab, hid)
 
@@ -332,8 +338,11 @@
 
 def pack_kernel(expert_index, slot, gate, tokens, out_grad, out):
     tok, width = tokens.shape
-    out[:tok, :width] = tokens[...]
-    out[tok:, :width] = out_grad[...]
+    half = width // 2
+    for i in range(2):
+        columns = slice(i * half, (i + 1) * half)
+        out[2 * i * tok : (2 * i + 1) * tok, :half] = tokens[:, columns]
+        out[(2 * i + 1) * tok : 2 * (i + 1) * tok, :half] = out_grad[:, columns]
     square = (tok, tok)
     eye = lax.broadcasted_iota(jnp.int32, square, 0) == lax.broadcasted_iota(jnp.int32, square, 1)
 
@@ -349,8 +358,9 @@
         hit = (lanes == column(expert_index[row])) & (column(slot[row]) >= 0)
         live += jnp.where(hit, 1.0, 0.0)
         weight += jnp.where(hit, column(gates[row]), 0.0)
-    out[:tok, width:] = live.astype(out.dtype)
-    out[tok:, width:] = weight.astype(out.dtype)
+    out[:tok, half:] = live.astype(out.dtype)
+    out[tok : 2 * tok, half:] = weight.astype(out.dtype)
+    out[2 * tok :, half:] = jnp.zeros((2 * tok, PAD), out.dtype)
 
 
 def pack(tokens, out_grad, expert_index, slot, gate):
@@ -358,7 +368,7 @@
     vmem = pl.BlockSpec(memory_space=pltpu.VMEM)
     return pl.pallas_call(
         pack_kernel,
-        out_shape=jax.ShapeDtypeStruct((2 * tok, width + PAD), tokens.dtype),
+        out_shape=jax.ShapeDtypeStruct((4 * tok, width // 2 + PAD), tokens.dtype),
         in_specs=[vmem] * 5,
         out_specs=vmem,
         compiler_params=pltpu.CompilerParams(vmem_limit_bytes=VMEM_LIMIT),
@@ -453,7 +463,7 @@
         [own[:, :pairs], partner[:, :pairs], own[:, pairs:], partner[:, pairs:]], axis=1
     )
 
-    rows = rows.reshape(n_z, 2 * tok, width + PAD)
+    rows = rows.reshape(n_z, 4 * tok, -1)
     scalars = jnp.stack([*experts, 1 - lax.axis_index("core")]).astype(jnp.int32)
     back, dab, hid, swap = forward(scalars, rows, weights)
     grads = reduce_weights(swap, rows, dab, hid)

time: 187 us -> 188 us (level)
  no operation moved by 1% of the time
where the time goes in v8:
time: 188 us; the launch traced here: 187 us
  waiting for transfers between devices  93.3 us (50%)
  starting transfers between devices  31.1 us (17%)
  Pallas kernels  21.6 us (11%)
  other arithmetic  14.8 us (8%)
  between operations  14.5 us (8%)
  local copies, waits for them, and re-layouts  11.6 us (6%)
    ppermute x1, waiting for transfers between devices, partner_weights(): mine = lax.ppermute(half, 'yl', SWAP)  42.6 us
    all_gather x1, waiting for transfers between devices, local(): rows = lax.all_gather(send, 'z', axis=0, tiled=True)  25.5 us
    ppermute x4, starting transfers between devices, pair_sum(): last = lax.ppermute(add(second, got[1]), axes, step2)  12.5 us
    unnamed x25, local copies, waits for them, and re-layouts  11.4 us
    ppermute x4, starting transfers between devices, pair_sum(): got = lax.ppermute(send, axes, step1)  11.1 us
    pallas_call x1, Pallas kernels, forward(): pl.pallas_call(forward_kernel, out_shape=(jax.ShapeDtypeStruct((count, wi...  10.6 us
    ppermute x4, waiting for transfers between devices, pair_sum(): last = lax.ppermute(add(second, got[1]), axes, step2)  10.2 us
    ppermute x4, waiting for transfers between devices, pair_sum(): got = lax.ppermute(send, axes, step1)  7.61 us
  transfers between devices with their start and end apart: 13, of which 10 were waited for; matrix products, arithmetic and copies ran while one was open for 10% of the time, Pallas kernels for 5%

profile of v8, /device:TPU:6, one launch (start us, length us, event | category | flops | bytes accessed | tf_op | source)
XLA Modules:
  0.0 186.9 jit_solution(13110400023880791112)
XLA Ops:
  7.2 1.9 %shard_map.111 = bf16[64,2688]{1,0:T(8,128)(2,1)} custom-call(s32[2,16]{1,0:T(2,128)} %bitcast.82, s32[2,16]{1,0:T(2,128)} %bitcast.83, bf16[2,16]{1,0:T(2,128)(2,1)} %bitcast.84, bf16[16,5120]{1,0:T(8,128)(2,1)} %tokens.1, bf16[16,5120]{1,0:T(8,128)(2,1)} %out_grad.1), custom_call_target="tpu_custom_call" | custom-call | bytes 700000 | tf_op jit(solution)/shard_map/pallas_call | solution.py:369
  9.2 3.1 %fusion.4 = bf16[2560,384]{1,0:T(8,128)(2,1)} fusion(s32[]{:T(128)S(6)} %select_n.103, bf16[2,2560,128]{2,1,0:T(8,128)(2,1)} %bitcast.79, bf16[2,2560,128]{2,1,0:T(8,128)(2,1)} %bitcast.80, bf16[2,2560,128]{2,1,0:T(8,128)(2,1)} %bitcast.81), kind=kLoop, calls=%fused_computation.9 | loop fusion | flops 5898240 | bytes 5898244 | tf_op jit(solution)/shard_map/jit(dynamic_index_in_dim)/squeeze | solution.py:384
  12.3 3.6 %collective-permute-start = (bf16[2560,384]{1,0:T(8,128)(2,1)}, bf16[2560,384]{1,0:T(8,128)(2,1)}, u32[]{:S(2)}, u32[]{:S(2)}) collective-permute-start(bf16[2560,384]{1,0:T(8,128)(2,1)} %fusion.4), channel_id=1, source_target_pairs={{0,16},{16,0},{1,17},{17,1},{2,18},{18,2},{3,19},{19,3},{4,20},{20... | collective-permute-start | bytes 5898248 | tf_op jit(solution)/shard_map/ppermute | solution.py:443
  16.0 0.6 pad_add_fusion.scalars
  16.6 42.6 %collective-permute-done = bf16[2560,384]{1,0:T(8,128)(2,1)} collective-permute-done((bf16[2560,384]{1,0:T(8,128)(2,1)}, bf16[2560,384]{1,0:T(8,128)(2,1)}, u32[]{:S(2)}, u32[]{:S(2)}) %collective-permute-start) | collective-permute-done | bytes 1966112 | tf_op jit(solution)/shard_map/ppermute | solution.py:443
  59.2 1.9 %collective-permute-start.1 = (bf16[2560,384]{1,0:T(8,128)(2,1)}, bf16[2560,384]{1,0:T(8,128)(2,1)S(1)}, u32[]{:S(2)}, u32[]{:S(2)}) collective-permute-start(bf16[2560,384]{1,0:T(8,128)(2,1)} %collective-permute-done), channel_id=1, source_target_pairs={{0,32},{32,0},{1,33},{33,1},{2,34},{34,2},{3,35},{35,3},{4,36},{36... | collective-permute-start | bytes 5898248 | tf_op jit(solution)/shard_map/ppermute | solution.py:444
  61.1 1.2 bitcast_dynamic-update-slice_fusion.2
  62.4 1.3 bitcast_dynamic-update-slice_fusion.1
  63.6 1.6 collective-permute-done.1
  65.3 1.9 %broadcast_select_fusion = (bf16[2560,384]{1,0:T(8,128)(2,1)S(1)}, bf16[2560,384]{1,0:T(8,128)(2,1)S(1)}) fusion(bf16[2560,384]{1,0:T(8,128)(2,1)S(1)} %collective-permute-done.1, bf16[2560,384]{1,0:T(8,128)(2,1)} %collective-permute-done, pred[]{:T(512)S(6)} %eq.23), kind=kLoop, calls=%fused_computation.10 | loop fusion | flops 1966080 | bytes 7864321 | tf_op jit(solution)/shard_map/jit(_where)/select_n | solution.py:446
  67.2 1.7 fusion.1
  69.0 0.1 copy-done.10
  69.0 1.3 bitcast_dynamic-update-slice_fusion
  70.3 1.2 fusion.5.weights
  71.5 25.5 %all-gather.2.cloned.1.call-done = bf16[1024,2688]{1,0:T(8,128)(2,1)} async-done(((bf16[64,2688]{1,0:T(8,128)(2,1)}), bf16[1024,2688]{1,0:T(8,128)(2,1)}) %all-gather.2.cloned.1.call-update) | async-done | bytes 5505040 | tf_op jit(solution)/shard_map/all_gather | solution.py:457
  97.0 10.6 %shard_map.112 = (bf16[256,5120]{1,0:T(8,128)(2,1)}, bf16[256,512]{1,0:T(8,128)(2,1)}, bf16[256,256]{1,0:T(8,128)(2,1)}, bf16[9,16,32,384]{3,2,1,0:T(8,128)(2,1)}) custom-call(s32[3]{0:T(128)} %pad_add_fusion.scalars, bf16[16,64,2688]{2,1,0:T(8,128)(2,1)} %bitcast.77, bf16[5120,768]{1,0:T(8,128)(2,1)} %fusion.5.weights), custom_call_target="tpu_custom_call" | custom-call | flops 3355443200 | bytes 20000000 | tf_op jit(solution)/shard_map/pallas_call | solution.py:173
  107.6 1.9 %collective-permute-start.2 = (bf16[9,16,32,384]{3,2,1,0:T(8,128)(2,1)}, bf16[9,16,32,384]{3,2,1,0:T(8,128)(2,1)S(1)}, u32[]{:S(2)}, u32[]{:S(2)}) collective-permute-start(bf16[9,16,32,384]{3,2,1,0:T(8,128)(2,1)} %get-tuple-element.15), channel_id=1, source_target_pairs={{0,32},{32,0},{1,33},{33,1},{2,34},{34,2},{3,35},{35,3},{4,36},{36... | collective-permute-start | bytes 10616840 | tf_op jit(solution)/shard_map/ppermute | solution.py:429
  109.7 0.1 stack.106.place
  109.8 2.6 %copy-done.2 = bf16[1024,2688]{1,0:T(8,128)(2,1)S(1)} copy-done((bf16[1024,2688]{1,0:T(8,128)(2,1)S(1)}, bf16[1024,2688]{1,0:T(8,128)(2,1)}, u32[]{:S(2)}) %copy-start.2) | copy-done | bytes 5505048
  112.3 0.9 copy-done.6
  113.3 0.9 copy-done.7
  114.2 2.5 %shard_map.113.keep_a.keep_b = bf16[8,320,768]{2,1,0:T(8,128)(2,1)S(1)} custom-call(s32[1]{0:T(128)} %bitcast.22.part, bf16[16,64,2688]{2,1,0:T(8,128)(2,1)S(1)} %bitcast.78, bf16[256,512]{1,0:T(8,128)(2,1)S(1)} %copy-done.6, bf16[256,256]{1,0:T(8,128)(2,1)S(1)} %copy-done.7), custom_call_target="tpu_custom_call" | custom-call | flops 1006632960 | bytes 9000000 | tf_op jit(solution)/shard_map/pallas_call | solution.py:213
  116.7 3.9 %shard_map.115 = (bf16[2,2,160,768]{3,2,1,0:T(8,128)(2,1)}, bf16[2,4,160,384]{3,2,1,0:T(8,128)(2,1)}) custom-call(s32[13]{0:T(128)S(1)} %stack.106.place, bf16[8,320,768]{2,1,0:T(8,128)(2,1)S(1)} %shard_map.113.keep_a.keep_b, bf16[8,320,768]{2,1,0:T(8,128)(2,1)S(1)} %shard_map.113.keep_a.keep_b, ...), custom_call_target="tpu_custom_call" | custom-call | flops 503316480 | bytes 9000000 | tf_op jit(solution)/shard_map/pallas_call | solution.py:307
  120.6 3.4 %collective-permute-start.7 = (bf16[2,4,160,384]{3,2,1,0:T(8,128)(2,1)}, bf16[2,4,160,384]{3,2,1,0:T(8,128)(2,1)}, u32[]{:S(2)}, u32[]{:S(2)}) collective-permute-start(bf16[2,4,160,384]{3,2,1,0:T(8,128)(2,1)} %get-tuple-element.19), channel_id=1, source_target_pairs={{0,16},{32,304},{16,0},{48,288},{256,272},{288,48},{272,256},{304,... | collective-permute-start | bytes 2949128 | tf_op jit(solution)/shard_map/ppermute | solution.py:404
  124.0 2.8 %collective-permute-start.3 = (bf16[2,2,160,768]{3,2,1,0:T(8,128)(2,1)}, bf16[2,2,160,768]{3,2,1,0:T(8,128)(2,1)}, u32[]{:S(2)}, u32[]{:S(2)}) collective-permute-start(bf16[2,2,160,768]{3,2,1,0:T(8,128)(2,1)} %get-tuple-element.17), channel_id=1, source_target_pairs={{0,64},{32,224},{64,0},{96,160},{128,192},{160,96},{192,128},{224,... | collective-permute-start | bytes 2949128 | tf_op jit(solution)/shard_map/ppermute | solution.py:404
  126.8 0.1 stack.97.place
  126.9 2.1 %copy-done.1 = bf16[8,320,768]{2,1,0:T(8,128)(2,1)S(1)} copy-done((bf16[8,320,768]{2,1,0:T(8,128)(2,1)S(1)}, bf16[8,320,768]{2,1,0:T(8,128)(2,1)}, u32[]{:S(2)}) %copy-start.1) | copy-done | bytes 3932184
  129.1 2.7 %shard_map.114 = (bf16[2,2,160,768]{3,2,1,0:T(8,128)(2,1)S(1)}, bf16[2,4,160,384]{3,2,1,0:T(8,128)(2,1)S(1)}) custom-call(s32[13]{0:T(128)S(1)} %stack.97.place, bf16[8,320,768]{2,1,0:T(8,128)(2,1)S(1)} %copy-done.1, bf16[8,320,768]{2,1,0:T(8,128)(2,1)S(1)} %copy-done.1, bf16[9,16,32,384]{3,2,1,0:T(8,128)(2,1)S(1)} %collective-permute-done.2.got_a.got_b.acts, ...), custom_call_target="tpu_custom_call" | custom-call | flops 503316480 | bytes 9000000 | tf_op jit(solution)/shard_map/pallas_call | solution.py:307
  131.8 0.9 copy-done.3
  132.8 4.2 %collective-permute-done.7 = bf16[2,4,160,384]{3,2,1,0:T(8,128)(2,1)} collective-permute-done((bf16[2,4,160,384]{3,2,1,0:T(8,128)(2,1)}, bf16[2,4,160,384]{3,2,1,0:T(8,128)(2,1)}, u32[]{:S(2)}, u32[]{:S(2)}) %collective-permute-start.7) | collective-permute-done | bytes 983072 | tf_op jit(solution)/shard_map/ppermute | solution.py:404
  136.9 1.2 fusion.9
  138.2 4.7 %collective-permute-start.8 = (bf16[4,160,384]{2,1,0:T(8,128)(2,1)S(1)}, bf16[4,160,384]{2,1,0:T(8,128)(2,1)S(1)}, u32[]{:S(2)}, u32[]{:S(2)}) collective-permute-start(bf16[4,160,384]{2,1,0:T(8,128)(2,1)S(1)} %fusion.9), channel_id=1, source_target_pairs={{0,272},{32,48},{16,256},{48,32},{256,16},{288,304},{272,0},{304,2... | collective-permute-start | bytes 1474568 | tf_op jit(solution)/shard_map/ppermute | solution.py:405
  142.9 1.3 fusion.8
  144.2 2.5 %collective-permute-start.4 = (bf16[2,160,768]{2,1,0:T(8,128)(2,1)S(1)}, bf16[2,160,768]{2,1,0:T(8,128)(2,1)S(1)}, u32[]{:S(2)}, u32[]{:S(2)}) collective-permute-start(bf16[2,160,768]{2,1,0:T(8,128)(2,1)S(1)} %fusion.8), channel_id=1, source_target_pairs={{0,192},{32,96},{64,128},{96,32},{128,64},{160,224},{192,0},{224,1... | collective-permute-start | bytes 1474568 | tf_op jit(solution)/shard_map/ppermute | solution.py:405
  146.6 3.5 %collective-permute-done.8 = bf16[4,160,384]{2,1,0:T(8,128)(2,1)S(1)} collective-permute-done((bf16[4,160,384]{2,1,0:T(8,128)(2,1)S(1)}, bf16[4,160,384]{2,1,0:T(8,128)(2,1)S(1)}, u32[]{:S(2)}, u32[]{:S(2)}) %collective-permute-start.8) | collective-permute-done | bytes 491552 | tf_op jit(solution)/shard_map/ppermute | solution.py:405
  150.1 1.4 fusion.6
  151.6 2.8 %collective-permute-start.9 = (bf16[2,160,384]{2,1,0:T(8,128)(2,1)S(1)}, bf16[2,160,384]{2,1,0:T(8,128)(2,1)S(1)}, u32[]{:S(2)}, u32[]{:S(2)}) collective-permute-start(bf16[2,160,384]{2,1,0:T(8,128)(2,1)S(1)} %pad_maximum_fusion.2), channel_id=1, source_target_pairs={{0,64},{32,224},{64,0},{96,160},{128,192},{160,96},{192,128},{224,... | collective-permute-start | bytes 737288 | tf_op jit(solution)/shard_map/ppermute | solution.py:404
  154.4 1.8 collective-permute-done.4
  156.1 1.2 fusion.7
  157.5 2.1 %collective-permute-start.5 = (bf16[2,160,384]{2,1,0:T(8,128)(2,1)S(1)}, bf16[2,160,384]{2,1,0:T(8,128)(2,1)S(1)}, u32[]{:S(2)}, u32[]{:S(2)}) collective-permute-start(bf16[2,160,384]{2,1,0:T(8,128)(2,1)S(1)} %pad_maximum_fusion.1), channel_id=1, source_target_pairs={{0,16},{32,304},{16,0},{48,288},{256,272},{288,48},{272,256},{304,... | collective-permute-start | bytes 737288 | tf_op jit(solution)/shard_map/ppermute | solution.py:404
  159.6 0.1 collective-permute-done.9
  159.7 2.5 %collective-permute-start.10 = (bf16[160,384]{1,0:T(8,128)(2,1)S(1)}, bf16[160,384]{1,0:T(8,128)(2,1)S(1)}, u32[]{:S(2)}, u32[]{:S(2)}) collective-permute-start(bf16[160,384]{1,0:T(8,128)(2,1)S(1)} %fusion.14), channel_id=1, source_target_pairs={{0,192},{32,96},{64,128},{96,32},{128,64},{160,224},{192,0},{224,1... | collective-permute-start | bytes 368648 | tf_op jit(solution)/shard_map/ppermute | solution.py:405
  162.2 3.4 %collective-permute-done.5 = bf16[2,160,384]{2,1,0:T(8,128)(2,1)S(1)} collective-permute-done((bf16[2,160,384]{2,1,0:T(8,128)(2,1)S(1)}, bf16[2,160,384]{2,1,0:T(8,128)(2,1)S(1)}, u32[]{:S(2)}, u32[]{:S(2)}) %collective-permute-start.5) | collective-permute-done | bytes 245792 | tf_op jit(solution)/shard_map/ppermute | solution.py:404
  165.6 2.9 %collective-permute-start.6 = (bf16[160,384]{1,0:T(8,128)(2,1)S(1)}, bf16[160,384]{1,0:T(8,128)(2,1)S(1)}, u32[]{:S(2)}, u32[]{:S(2)}) collective-permute-start(bf16[160,384]{1,0:T(8,128)(2,1)S(1)} %fusion.10), channel_id=1, source_target_pairs={{0,272},{32,48},{16,256},{48,32},{256,16},{288,304},{272,0},{304,2... | collective-permute-start | bytes 368648 | tf_op jit(solution)/shard_map/ppermute | solution.py:405
  168.5 0.1 fusion.13
  168.6 5.0 %collective-permute-done.6 = bf16[160,384]{1,0:T(8,128)(2,1)S(1)} collective-permute-done((bf16[160,384]{1,0:T(8,128)(2,1)S(1)}, bf16[160,384]{1,0:T(8,128)(2,1)S(1)}, u32[]{:S(2)}, u32[]{:S(2)}) %collective-permute-start.6) | collective-permute-done | bytes 122912 | tf_op jit(solution)/shard_map/ppermute | solution.py:405
  173.6 0.7 fusion.19
  174.3 5.7 %reduce-scatter.2.cloned.1.call-done = bf16[16,5120]{1,0:T(8,128)(2,1)} async-done(((bf16[256,5120]{1,0:T(8,128)(2,1)}), bf16[16,5120]{1,0:T(8,128)(2,1)}) %reduce-scatter.2.cloned.1.call-update) | async-done | bytes 163856 | tf_op jit(solution)/shard_map/reduce_scatter | solution.py:470
  (33 shorter events, 0.5 us)
Async XLA Ops:
  7.2 89.9 %all-gather.2.cloned.1.call-start = ((), (), s32[]{:S(2)}) async-start(), calls=%async_computation.1 | async-start | bytes 5849088 | tf_op jit(solution)/shard_map/all_gather | solution.py:457
  9.1 170.9 %reduce-scatter.2.cloned.1.call-start = ((), (), s32[]{:S(2)}) async-start(), calls=%async_computation.2 | async-start | bytes 2785280 | tf_op jit(solution)/shard_map/reduce_scatter | solution.py:470
  9.2 52.0 %copy-start.8 = (bf16[1,5120,128]{2,1,0:T(8,128)(2,1)S(1)}, bf16[1,5120,128]{2,1,0:T(8,128)(2,1)}, u32[]{:S(2)}) copy-start(bf16[1,5120,128]{2,1,0:T(8,128)(2,1)} %param.13) | copy-start | bytes 3932164
  12.3 50.0 %copy-start.9 = (bf16[1,5120,128]{2,1,0:T(8,128)(2,1)S(1)}, bf16[1,5120,128]{2,1,0:T(8,128)(2,1)}, u32[]{:S(2)}) copy-start(bf16[1,5120,128]{2,1,0:T(8,128)(2,1)} %param.14) | copy-start | bytes 3932164
  12.3 46.9 %collective-permute-start = (bf16[2560,384]{1,0:T(8,128)(2,1)}, bf16[2560,384]{1,0:T(8,128)(2,1)}, u32[]{:S(2)}, u32[]{:S(2)}) collective-permute-start(bf16[2560,384]{1,0:T(8,128)(2,1)} %fusion.4), channel_id=1, source_target_pairs={{0,16},{16,0},{1,17},{17,1},{2,18},{18,2},{3,19},{19,3},{4,20},{20... | collective-permute-start | bytes 5898248 | tf_op jit(solution)/shard_map/ppermute | solution.py:443
  59.2 6.1 %collective-permute-start.1 = (bf16[2560,384]{1,0:T(8,128)(2,1)}, bf16[2560,384]{1,0:T(8,128)(2,1)S(1)}, u32[]{:S(2)}, u32[]{:S(2)}) collective-permute-start(bf16[2560,384]{1,0:T(8,128)(2,1)} %collective-permute-done), channel_id=1, source_target_pairs={{0,32},{32,0},{1,33},{33,1},{2,34},{34,2},{3,35},{35,3},{4,36},{36... | collective-permute-start | bytes 5898248 | tf_op jit(solution)/shard_map/ppermute | solution.py:444
  67.2 1.8 copy-start.10
  107.6 9.1 %collective-permute-start.2 = (bf16[9,16,32,384]{3,2,1,0:T(8,128)(2,1)}, bf16[9,16,32,384]{3,2,1,0:T(8,128)(2,1)S(1)}, u32[]{:S(2)}, u32[]{:S(2)}) collective-permute-start(bf16[9,16,32,384]{3,2,1,0:T(8,128)(2,1)} %get-tuple-element.15), channel_id=1, source_target_pairs={{0,32},{32,0},{1,33},{33,1},{2,34},{34,2},{3,35},{35,3},{4,36},{36... | collective-permute-start | bytes 10616840 | tf_op jit(solution)/shard_map/ppermute | solution.py:429
  109.8 2.6 %copy-start.2 = (bf16[1024,2688]{1,0:T(8,128)(2,1)S(1)}, bf16[1024,2688]{1,0:T(8,128)(2,1)}, u32[]{:S(2)}) copy-start(bf16[1024,2688]{1,0:T(8,128)(2,1)} %all-gather.2.cloned.1.call-done) | copy-start | bytes 16515076
  112.3 0.9 copy-start.6
  113.3 0.9 copy-start.7
  116.7 3.9 %copy-start = (bf16[8,320,768]{2,1,0:T(8,128)(2,1)}, bf16[8,320,768]{2,1,0:T(8,128)(2,1)S(1)}, u32[]{:S(2)}) copy-start(bf16[8,320,768]{2,1,0:T(8,128)(2,1)S(1)} %shard_map.113.keep_a.keep_b) | copy-start | bytes 11796484
  120.6 16.3 %collective-permute-start.7 = (bf16[2,4,160,384]{3,2,1,0:T(8,128)(2,1)}, bf16[2,4,160,384]{3,2,1,0:T(8,128)(2,1)}, u32[]{:S(2)}, u32[]{:S(2)}) collective-permute-start(bf16[2,4,160,384]{3,2,1,0:T(8,128)(2,1)} %get-tuple-element.19), channel_id=1, source_target_pairs={{0,16},{32,304},{16,0},{48,288},{256,272},{288,48},{272,256},{304,... | collective-permute-start | bytes 2949128 | tf_op jit(solution)/shard_map/ppermute | solution.py:404
  124.0 18.8 %collective-permute-start.3 = (bf16[2,2,160,768]{3,2,1,0:T(8,128)(2,1)}, bf16[2,2,160,768]{3,2,1,0:T(8,128)(2,1)}, u32[]{:S(2)}, u32[]{:S(2)}) collective-permute-start(bf16[2,2,160,768]{3,2,1,0:T(8,128)(2,1)} %get-tuple-element.17), channel_id=1, source_target_pairs={{0,64},{32,224},{64,0},{96,160},{128,192},{160,96},{192,128},{224,... | collective-permute-start | bytes 2949128 | tf_op jit(solution)/shard_map/ppermute | solution.py:404
  126.9 2.1 %copy-start.1 = (bf16[8,320,768]{2,1,0:T(8,128)(2,1)S(1)}, bf16[8,320,768]{2,1,0:T(8,128)(2,1)}, u32[]{:S(2)}) copy-start(bf16[8,320,768]{2,1,0:T(8,128)(2,1)} %copy-done) | copy-start | bytes 11796484
  131.8 1.0 copy-start.3
  132.8 4.2 %copy-start.5 = (bf16[2,4,160,384]{3,2,1,0:T(8,128)(2,1)}, bf16[2,4,160,384]{3,2,1,0:T(8,128)(2,1)S(1)}, u32[]{:S(2)}) copy-start(bf16[2,4,160,384]{3,2,1,0:T(8,128)(2,1)S(1)} %get-tuple-element.18) | copy-start | bytes 2949124
  136.9 19.2 %copy-start.4 = (bf16[2,2,160,768]{3,2,1,0:T(8,128)(2,1)S(1)}, bf16[2,2,160,768]{3,2,1,0:T(8,128)(2,1)}, u32[]{:S(2)}) copy-start(bf16[2,2,160,768]{3,2,1,0:T(8,128)(2,1)} %copy-done.3) | copy-start | bytes 2949124
  138.2 11.9 %collective-permute-start.8 = (bf16[4,160,384]{2,1,0:T(8,128)(2,1)S(1)}, bf16[4,160,384]{2,1,0:T(8,128)(2,1)S(1)}, u32[]{:S(2)}, u32[]{:S(2)}) collective-permute-start(bf16[4,160,384]{2,1,0:T(8,128)(2,1)S(1)} %fusion.9), channel_id=1, source_target_pairs={{0,272},{32,48},{16,256},{48,32},{256,16},{288,304},{272,0},{304,2... | collective-permute-start | bytes 1474568 | tf_op jit(solution)/shard_map/ppermute | solution.py:405
  144.2 11.9 %collective-permute-start.4 = (bf16[2,160,768]{2,1,0:T(8,128)(2,1)S(1)}, bf16[2,160,768]{2,1,0:T(8,128)(2,1)S(1)}, u32[]{:S(2)}, u32[]{:S(2)}) collective-permute-start(bf16[2,160,768]{2,1,0:T(8,128)(2,1)S(1)} %fusion.8), channel_id=1, source_target_pairs={{0,192},{32,96},{64,128},{96,32},{128,64},{160,224},{192,0},{224,1... | collective-permute-start | bytes 1474568 | tf_op jit(solution)/shard_map/ppermute | solution.py:405
  151.6 8.1 %collective-permute-start.9 = (bf16[2,160,384]{2,1,0:T(8,128)(2,1)S(1)}, bf16[2,160,384]{2,1,0:T(8,128)(2,1)S(1)}, u32[]{:S(2)}, u32[]{:S(2)}) collective-permute-start(bf16[2,160,384]{2,1,0:T(8,128)(2,1)S(1)} %pad_maximum_fusion.2), channel_id=1, source_target_pairs={{0,64},{32,224},{64,0},{96,160},{128,192},{160,96},{192,128},{224,... | collective-permute-start | bytes 737288 | tf_op jit(solution)/shard_map/ppermute | solution.py:404
  157.5 8.1 %collective-permute-start.5 = (bf16[2,160,384]{2,1,0:T(8,128)(2,1)S(1)}, bf16[2,160,384]{2,1,0:T(8,128)(2,1)S(1)}, u32[]{:S(2)}, u32[]{:S(2)}) collective-permute-start(bf16[2,160,384]{2,1,0:T(8,128)(2,1)S(1)} %pad_maximum_fusion.1), channel_id=1, source_target_pairs={{0,16},{32,304},{16,0},{48,288},{256,272},{288,48},{272,256},{304,... | collective-permute-start | bytes 737288 | tf_op jit(solution)/shard_map/ppermute | solution.py:404
  159.7 8.8 %collective-permute-start.10 = (bf16[160,384]{1,0:T(8,128)(2,1)S(1)}, bf16[160,384]{1,0:T(8,128)(2,1)S(1)}, u32[]{:S(2)}, u32[]{:S(2)}) collective-permute-start(bf16[160,384]{1,0:T(8,128)(2,1)S(1)} %fusion.14), channel_id=1, source_target_pairs={{0,192},{32,96},{64,128},{96,32},{128,64},{160,224},{192,0},{224,1... | collective-permute-start | bytes 368648 | tf_op jit(solution)/shard_map/ppermute | solution.py:405
  165.6 8.0 %collective-permute-start.6 = (bf16[160,384]{1,0:T(8,128)(2,1)S(1)}, bf16[160,384]{1,0:T(8,128)(2,1)S(1)}, u32[]{:S(2)}, u32[]{:S(2)}) collective-permute-start(bf16[160,384]{1,0:T(8,128)(2,1)S(1)} %fusion.10), channel_id=1, source_target_pairs={{0,272},{32,48},{16,256},{48,32},{256,16},{288,304},{272,0},{304,2... | collective-permute-start | bytes 368648 | tf_op jit(solution)/shard_map/ppermute | solution.py:405
Sparse Core Ops, SparseCore 0:
  10.1 86.9 all-gather.1
  109.7 70.2 reduce-scatter.1

commit v9 on v7

--- a/solution.py
+++ b/solution.py
@@ -96,8 +96,8 @@
     route_copy = pltpu.make_async_copy(rows.at[:, :, last], rows_v.at[:, :, last], sems.at[4, 0])
 
     for k in range(CHUNKS):
+        weight_copy(k).start()
         row_copy(k).start()
-        weight_copy(k).start()
     route_copy.start()
 
     for k in range(CHUNKS):

time: 187 us -> 187 us (level)
  no operation moved by 1% of the time
where the time goes in v9:
time: 187 us; the launch traced here: 186 us
  waiting for transfers between devices  92.5 us (49%)
  starting transfers between devices  31.2 us (17%)
  Pallas kernels  21.5 us (11%)
  other arithmetic  14.8 us (8%)
  between operations  14.5 us (8%)
  local copies, waits for them, and re-layouts  11.6 us (6%)
    ppermute x1, waiting for transfers between devices, partner_weights(): mine = lax.ppermute(half, 'yl', SWAP)  42.6 us
    all_gather x1, waiting for transfers between devices, local(): rows = lax.all_gather(send, 'z', axis=0, tiled=True)  24.7 us
    ppermute x4, starting transfers between devices, pair_sum(): last = lax.ppermute(add(second, got[1]), axes, step2)  12.7 us
    unnamed x25, local copies, waits for them, and re-layouts  11.3 us
    ppermute x4, starting transfers between devices, pair_sum(): got = lax.ppermute(send, axes, step1)  11 us
    pallas_call x1, Pallas kernels, forward(): pl.pallas_call(forward_kernel, out_shape=(jax.ShapeDtypeStruct((count, wi...  10.5 us
    ppermute x4, waiting for transfers between devices, pair_sum(): last = lax.ppermute(add(second, got[1]), axes, step2)  10.1 us
    ppermute x4, waiting for transfers between devices, pair_sum(): got = lax.ppermute(send, axes, step1)  7.61 us
  transfers between devices with their start and end apart: 13, of which 10 were waited for; matrix products, arithmetic and copies ran while one was open for 10% of the time, Pallas kernels for 5%

profile of v9, /device:TPU:6, one launch (start us, length us, event | category | flops | bytes accessed | tf_op | source)
XLA Modules:
  0.0 186.0 jit_solution(4747973111494530753)
XLA Ops:
  7.2 1.9 %shard_map.111 = bf16[32,5248]{1,0:T(8,128)(2,1)} custom-call(s32[2,16]{1,0:T(2,128)} %bitcast.82, s32[2,16]{1,0:T(2,128)} %bitcast.83, bf16[2,16]{1,0:T(2,128)(2,1)} %bitcast.84, bf16[16,5120]{1,0:T(8,128)(2,1)} %tokens.1, bf16[16,5120]{1,0:T(8,128)(2,1)} %out_grad.1), custom_call_target="tpu_custom_call" | custom-call | bytes 700000 | tf_op jit(solution)/shard_map/pallas_call | solution.py:359
  9.2 3.1 %fusion.4 = bf16[2560,384]{1,0:T(8,128)(2,1)} fusion(s32[]{:T(128)S(6)} %select_n.103, bf16[2,2560,128]{2,1,0:T(8,128)(2,1)} %bitcast.79, bf16[2,2560,128]{2,1,0:T(8,128)(2,1)} %bitcast.80, bf16[2,2560,128]{2,1,0:T(8,128)(2,1)} %bitcast.81), kind=kLoop, calls=%fused_computation.9 | loop fusion | flops 5898240 | bytes 5898244 | tf_op jit(solution)/shard_map/jit(dynamic_index_in_dim)/squeeze | solution.py:374
  12.3 3.6 %collective-permute-start = (bf16[2560,384]{1,0:T(8,128)(2,1)}, bf16[2560,384]{1,0:T(8,128)(2,1)}, u32[]{:S(2)}, u32[]{:S(2)}) collective-permute-start(bf16[2560,384]{1,0:T(8,128)(2,1)} %fusion.4), channel_id=1, source_target_pairs={{0,16},{16,0},{1,17},{17,1},{2,18},{18,2},{3,19},{19,3},{4,20},{20... | collective-permute-start | bytes 5898248 | tf_op jit(solution)/shard_map/ppermute | solution.py:433
  16.0 0.6 pad_add_fusion.scalars
  16.6 42.6 %collective-permute-done = bf16[2560,384]{1,0:T(8,128)(2,1)} collective-permute-done((bf16[2560,384]{1,0:T(8,128)(2,1)}, bf16[2560,384]{1,0:T(8,128)(2,1)}, u32[]{:S(2)}, u32[]{:S(2)}) %collective-permute-start) | collective-permute-done | bytes 1966112 | tf_op jit(solution)/shard_map/ppermute | solution.py:433
  59.2 1.9 %collective-permute-start.1 = (bf16[2560,384]{1,0:T(8,128)(2,1)}, bf16[2560,384]{1,0:T(8,128)(2,1)S(1)}, u32[]{:S(2)}, u32[]{:S(2)}) collective-permute-start(bf16[2560,384]{1,0:T(8,128)(2,1)} %collective-permute-done), channel_id=1, source_target_pairs={{0,32},{32,0},{1,33},{33,1},{2,34},{34,2},{3,35},{35,3},{4,36},{36... | collective-permute-start | bytes 5898248 | tf_op jit(solution)/shard_map/ppermute | solution.py:434
  61.1 1.2 bitcast_dynamic-update-slice_fusion.2
  62.4 1.3 bitcast_dynamic-update-slice_fusion.1
  63.6 1.6 collective-permute-done.1
  65.3 1.9 %broadcast_select_fusion = (bf16[2560,384]{1,0:T(8,128)(2,1)S(1)}, bf16[2560,384]{1,0:T(8,128)(2,1)S(1)}) fusion(bf16[2560,384]{1,0:T(8,128)(2,1)S(1)} %collective-permute-done.1, bf16[2560,384]{1,0:T(8,128)(2,1)} %collective-permute-done, pred[]{:T(512)S(6)} %eq.23), kind=kLoop, calls=%fused_computation.10 | loop fusion | flops 1966080 | bytes 7864321 | tf_op jit(solution)/shard_map/jit(_where)/select_n | solution.py:436
  67.2 1.7 fusion.1
  68.9 0.1 copy-done.10
  69.0 1.3 bitcast_dynamic-update-slice_fusion
  70.3 1.2 fusion.5.weights
  71.5 24.7 %all-gather.2.cloned.1.call-done = bf16[512,5248]{1,0:T(8,128)(2,1)} async-done(((bf16[32,5248]{1,0:T(8,128)(2,1)}), bf16[512,5248]{1,0:T(8,128)(2,1)}) %all-gather.2.cloned.1.call-update) | async-done | bytes 5373968 | tf_op jit(solution)/shard_map/all_gather | solution.py:447
  96.2 10.5 %shard_map.112 = (bf16[256,5120]{1,0:T(8,128)(2,1)}, bf16[256,512]{1,0:T(8,128)(2,1)}, bf16[256,256]{1,0:T(8,128)(2,1)}, bf16[9,16,32,384]{3,2,1,0:T(8,128)(2,1)}) custom-call(s32[3]{0:T(128)} %pad_add_fusion.scalars, bf16[16,32,5248]{2,1,0:T(8,128)(2,1)} %bitcast.77, bf16[5120,768]{1,0:T(8,128)(2,1)} %fusion.5.weights), custom_call_target="tpu_custom_call" | custom-call | flops 3355443200 | bytes 20000000 | tf_op jit(solution)/shard_map/pallas_call | solution.py:171
  106.7 1.9 %collective-permute-start.2 = (bf16[9,16,32,384]{3,2,1,0:T(8,128)(2,1)}, bf16[9,16,32,384]{3,2,1,0:T(8,128)(2,1)S(1)}, u32[]{:S(2)}, u32[]{:S(2)}) collective-permute-start(bf16[9,16,32,384]{3,2,1,0:T(8,128)(2,1)} %get-tuple-element.15), channel_id=1, source_target_pairs={{0,32},{32,0},{1,33},{33,1},{2,34},{34,2},{3,35},{35,3},{4,36},{36... | collective-permute-start | bytes 10616840 | tf_op jit(solution)/shard_map/ppermute | solution.py:419
  108.8 0.1 stack.106.place
  108.9 2.5 %copy-done.2 = bf16[512,5248]{1,0:T(8,128)(2,1)S(1)} copy-done((bf16[512,5248]{1,0:T(8,128)(2,1)S(1)}, bf16[512,5248]{1,0:T(8,128)(2,1)}, u32[]{:S(2)}) %copy-start.2) | copy-done | bytes 5373976
  111.4 0.9 copy-done.6
  112.4 0.9 copy-done.7
  113.3 2.5 %shard_map.113.keep_a.keep_b = bf16[8,320,768]{2,1,0:T(8,128)(2,1)S(1)} custom-call(s32[1]{0:T(128)} %bitcast.22.part, bf16[16,32,5248]{2,1,0:T(8,128)(2,1)S(1)} %bitcast.78, bf16[256,512]{1,0:T(8,128)(2,1)S(1)} %copy-done.6, bf16[256,256]{1,0:T(8,128)(2,1)S(1)} %copy-done.7), custom_call_target="tpu_custom_call" | custom-call | flops 1006632960 | bytes 9000000 | tf_op jit(solution)/shard_map/pallas_call | solution.py:210
  115.8 3.9 %shard_map.115 = (bf16[2,2,160,768]{3,2,1,0:T(8,128)(2,1)}, bf16[2,4,160,384]{3,2,1,0:T(8,128)(2,1)}) custom-call(s32[13]{0:T(128)S(1)} %stack.106.place, bf16[8,320,768]{2,1,0:T(8,128)(2,1)S(1)} %shard_map.113.keep_a.keep_b, bf16[8,320,768]{2,1,0:T(8,128)(2,1)S(1)} %shard_map.113.keep_a.keep_b, ...), custom_call_target="tpu_custom_call" | custom-call | flops 503316480 | bytes 9000000 | tf_op jit(solution)/shard_map/pallas_call | solution.py:301
  119.7 3.4 %collective-permute-start.7 = (bf16[2,4,160,384]{3,2,1,0:T(8,128)(2,1)}, bf16[2,4,160,384]{3,2,1,0:T(8,128)(2,1)}, u32[]{:S(2)}, u32[]{:S(2)}) collective-permute-start(bf16[2,4,160,384]{3,2,1,0:T(8,128)(2,1)} %get-tuple-element.19), channel_id=1, source_target_pairs={{0,16},{32,304},{16,0},{48,288},{256,272},{288,48},{272,256},{304,... | collective-permute-start | bytes 2949128 | tf_op jit(solution)/shard_map/ppermute | solution.py:394
  123.1 3.0 %collective-permute-start.3 = (bf16[2,2,160,768]{3,2,1,0:T(8,128)(2,1)}, bf16[2,2,160,768]{3,2,1,0:T(8,128)(2,1)}, u32[]{:S(2)}, u32[]{:S(2)}) collective-permute-start(bf16[2,2,160,768]{3,2,1,0:T(8,128)(2,1)} %get-tuple-element.17), channel_id=1, source_target_pairs={{0,64},{32,224},{64,0},{96,160},{128,192},{160,96},{192,128},{224,... | collective-permute-start | bytes 2949128 | tf_op jit(solution)/shard_map/ppermute | solution.py:394
  126.1 0.1 stack.97.place
  126.2 2.1 %copy-done.1 = bf16[8,320,768]{2,1,0:T(8,128)(2,1)S(1)} copy-done((bf16[8,320,768]{2,1,0:T(8,128)(2,1)S(1)}, bf16[8,320,768]{2,1,0:T(8,128)(2,1)}, u32[]{:S(2)}) %copy-start.1) | copy-done | bytes 3932184
  128.3 2.7 %shard_map.114 = (bf16[2,2,160,768]{3,2,1,0:T(8,128)(2,1)S(1)}, bf16[2,4,160,384]{3,2,1,0:T(8,128)(2,1)S(1)}) custom-call(s32[13]{0:T(128)S(1)} %stack.97.place, bf16[8,320,768]{2,1,0:T(8,128)(2,1)S(1)} %copy-done.1, bf16[8,320,768]{2,1,0:T(8,128)(2,1)S(1)} %copy-done.1, bf16[9,16,32,384]{3,2,1,0:T(8,128)(2,1)S(1)} %collective-permute-done.2.got_a.got_b.acts, ...), custom_call_target="tpu_custom_call" | custom-call | flops 503316480 | bytes 9000000 | tf_op jit(solution)/shard_map/pallas_call | solution.py:301
  131.0 0.9 copy-done.3
  132.0 4.0 %collective-permute-done.7 = bf16[2,4,160,384]{3,2,1,0:T(8,128)(2,1)} collective-permute-done((bf16[2,4,160,384]{3,2,1,0:T(8,128)(2,1)}, bf16[2,4,160,384]{3,2,1,0:T(8,128)(2,1)}, u32[]{:S(2)}, u32[]{:S(2)}) %collective-permute-start.7) | collective-permute-done | bytes 983072 | tf_op jit(solution)/shard_map/ppermute | solution.py:394
  136.0 1.2 fusion.9
  137.2 4.7 %collective-permute-start.8 = (bf16[4,160,384]{2,1,0:T(8,128)(2,1)S(1)}, bf16[4,160,384]{2,1,0:T(8,128)(2,1)S(1)}, u32[]{:S(2)}, u32[]{:S(2)}) collective-permute-start(bf16[4,160,384]{2,1,0:T(8,128)(2,1)S(1)} %fusion.9), channel_id=1, source_target_pairs={{0,272},{32,48},{16,256},{48,32},{256,16},{288,304},{272,0},{304,2... | collective-permute-start | bytes 1474568 | tf_op jit(solution)/shard_map/ppermute | solution.py:395
  141.9 1.3 fusion.8
  143.2 2.6 %collective-permute-start.4 = (bf16[2,160,768]{2,1,0:T(8,128)(2,1)S(1)}, bf16[2,160,768]{2,1,0:T(8,128)(2,1)S(1)}, u32[]{:S(2)}, u32[]{:S(2)}) collective-permute-start(bf16[2,160,768]{2,1,0:T(8,128)(2,1)S(1)} %fusion.8), channel_id=1, source_target_pairs={{0,192},{32,96},{64,128},{96,32},{128,64},{160,224},{192,0},{224,1... | collective-permute-start | bytes 1474568 | tf_op jit(solution)/shard_map/ppermute | solution.py:395
  145.9 3.3 %collective-permute-done.8 = bf16[4,160,384]{2,1,0:T(8,128)(2,1)S(1)} collective-permute-done((bf16[4,160,384]{2,1,0:T(8,128)(2,1)S(1)}, bf16[4,160,384]{2,1,0:T(8,128)(2,1)S(1)}, u32[]{:S(2)}, u32[]{:S(2)}) %collective-permute-start.8) | collective-permute-done | bytes 491552 | tf_op jit(solution)/shard_map/ppermute | solution.py:395
  149.2 1.4 fusion.6
  150.6 2.7 %collective-permute-start.9 = (bf16[2,160,384]{2,1,0:T(8,128)(2,1)S(1)}, bf16[2,160,384]{2,1,0:T(8,128)(2,1)S(1)}, u32[]{:S(2)}, u32[]{:S(2)}) collective-permute-start(bf16[2,160,384]{2,1,0:T(8,128)(2,1)S(1)} %pad_maximum_fusion.2), channel_id=1, source_target_pairs={{0,64},{32,224},{64,0},{96,160},{128,192},{160,96},{192,128},{224,... | collective-permute-start | bytes 737288 | tf_op jit(solution)/shard_map/ppermute | solution.py:394
  153.4 1.8 collective-permute-done.4
  155.2 1.2 fusion.7
  156.5 1.9 %collective-permute-start.5 = (bf16[2,160,384]{2,1,0:T(8,128)(2,1)S(1)}, bf16[2,160,384]{2,1,0:T(8,128)(2,1)S(1)}, u32[]{:S(2)}, u32[]{:S(2)}) collective-permute-start(bf16[2,160,384]{2,1,0:T(8,128)(2,1)S(1)} %pad_maximum_fusion.1), channel_id=1, source_target_pairs={{0,16},{32,304},{16,0},{48,288},{256,272},{288,48},{272,256},{304,... | collective-permute-start | bytes 737288 | tf_op jit(solution)/shard_map/ppermute | solution.py:394
  158.4 0.3 collective-permute-done.9
  158.7 2.5 %collective-permute-start.10 = (bf16[160,384]{1,0:T(8,128)(2,1)S(1)}, bf16[160,384]{1,0:T(8,128)(2,1)S(1)}, u32[]{:S(2)}, u32[]{:S(2)}) collective-permute-start(bf16[160,384]{1,0:T(8,128)(2,1)S(1)} %fusion.14), channel_id=1, source_target_pairs={{0,192},{32,96},{64,128},{96,32},{128,64},{160,224},{192,0},{224,1... | collective-permute-start | bytes 368648 | tf_op jit(solution)/shard_map/ppermute | solution.py:395
  161.2 3.4 %collective-permute-done.5 = bf16[2,160,384]{2,1,0:T(8,128)(2,1)S(1)} collective-permute-done((bf16[2,160,384]{2,1,0:T(8,128)(2,1)S(1)}, bf16[2,160,384]{2,1,0:T(8,128)(2,1)S(1)}, u32[]{:S(2)}, u32[]{:S(2)}) %collective-permute-start.5) | collective-permute-done | bytes 245792 | tf_op jit(solution)/shard_map/ppermute | solution.py:394
  164.6 2.9 %collective-permute-start.6 = (bf16[160,384]{1,0:T(8,128)(2,1)S(1)}, bf16[160,384]{1,0:T(8,128)(2,1)S(1)}, u32[]{:S(2)}, u32[]{:S(2)}) collective-permute-start(bf16[160,384]{1,0:T(8,128)(2,1)S(1)} %fusion.10), channel_id=1, source_target_pairs={{0,272},{32,48},{16,256},{48,32},{256,16},{288,304},{272,0},{304,2... | collective-permute-start | bytes 368648 | tf_op jit(solution)/shard_map/ppermute | solution.py:395
  167.5 0.1 fusion.13
  167.6 5.0 %collective-permute-done.6 = bf16[160,384]{1,0:T(8,128)(2,1)S(1)} collective-permute-done((bf16[160,384]{1,0:T(8,128)(2,1)S(1)}, bf16[160,384]{1,0:T(8,128)(2,1)S(1)}, u32[]{:S(2)}, u32[]{:S(2)}) %collective-permute-start.6) | collective-permute-done | bytes 122912 | tf_op jit(solution)/shard_map/ppermute | solution.py:395
  172.7 0.7 fusion.19
  173.4 5.8 %reduce-scatter.2.cloned.1.call-done = bf16[16,5120]{1,0:T(8,128)(2,1)} async-done(((bf16[256,5120]{1,0:T(8,128)(2,1)}), bf16[16,5120]{1,0:T(8,128)(2,1)}) %reduce-scatter.2.cloned.1.call-update) | async-done | bytes 163856 | tf_op jit(solution)/shard_map/reduce_scatter | solution.py:460
  (33 shorter events, 0.5 us)
Async XLA Ops:
  7.2 89.0 %all-gather.2.cloned.1.call-start = ((), (), s32[]{:S(2)}) async-start(), calls=%async_computation.1 | async-start | bytes 5709824 | tf_op jit(solution)/shard_map/all_gather | solution.py:447
  9.1 170.1 %reduce-scatter.2.cloned.1.call-start = ((), (), s32[]{:S(2)}) async-start(), calls=%async_computation.2 | async-start | bytes 2785280 | tf_op jit(solution)/shard_map/reduce_scatter | solution.py:460
  9.2 52.0 %copy-start.8 = (bf16[1,5120,128]{2,1,0:T(8,128)(2,1)S(1)}, bf16[1,5120,128]{2,1,0:T(8,128)(2,1)}, u32[]{:S(2)}) copy-start(bf16[1,5120,128]{2,1,0:T(8,128)(2,1)} %param.13) | copy-start | bytes 3932164
  12.3 50.0 %copy-start.9 = (bf16[1,5120,128]{2,1,0:T(8,128)(2,1)S(1)}, bf16[1,5120,128]{2,1,0:T(8,128)(2,1)}, u32[]{:S(2)}) copy-start(bf16[1,5120,128]{2,1,0:T(8,128)(2,1)} %param.14) | copy-start | bytes 3932164
  12.3 46.9 %collective-permute-start = (bf16[2560,384]{1,0:T(8,128)(2,1)}, bf16[2560,384]{1,0:T(8,128)(2,1)}, u32[]{:S(2)}, u32[]{:S(2)}) collective-permute-start(bf16[2560,384]{1,0:T(8,128)(2,1)} %fusion.4), channel_id=1, source_target_pairs={{0,16},{16,0},{1,17},{17,1},{2,18},{18,2},{3,19},{19,3},{4,20},{20... | collective-permute-start | bytes 5898248 | tf_op jit(solution)/shard_map/ppermute | solution.py:433
  59.2 6.1 %collective-permute-start.1 = (bf16[2560,384]{1,0:T(8,128)(2,1)}, bf16[2560,384]{1,0:T(8,128)(2,1)S(1)}, u32[]{:S(2)}, u32[]{:S(2)}) collective-permute-start(bf16[2560,384]{1,0:T(8,128)(2,1)} %collective-permute-done), channel_id=1, source_target_pairs={{0,32},{32,0},{1,33},{33,1},{2,34},{34,2},{3,35},{35,3},{4,36},{36... | collective-permute-start | bytes 5898248 | tf_op jit(solution)/shard_map/ppermute | solution.py:434
  67.2 1.9 copy-start.10
  106.7 9.0 %collective-permute-start.2 = (bf16[9,16,32,384]{3,2,1,0:T(8,128)(2,1)}, bf16[9,16,32,384]{3,2,1,0:T(8,128)(2,1)S(1)}, u32[]{:S(2)}, u32[]{:S(2)}) collective-permute-start(bf16[9,16,32,384]{3,2,1,0:T(8,128)(2,1)} %get-tuple-element.15), channel_id=1, source_target_pairs={{0,32},{32,0},{1,33},{33,1},{2,34},{34,2},{3,35},{35,3},{4,36},{36... | collective-permute-start | bytes 10616840 | tf_op jit(solution)/shard_map/ppermute | solution.py:419
  108.9 2.5 %copy-start.2 = (bf16[512,5248]{1,0:T(8,128)(2,1)S(1)}, bf16[512,5248]{1,0:T(8,128)(2,1)}, u32[]{:S(2)}) copy-start(bf16[512,5248]{1,0:T(8,128)(2,1)} %all-gather.2.cloned.1.call-done) | copy-start | bytes 16121860
  111.4 0.9 copy-start.6
  112.3 0.9 copy-start.7
  115.8 3.9 %copy-start = (bf16[8,320,768]{2,1,0:T(8,128)(2,1)}, bf16[8,320,768]{2,1,0:T(8,128)(2,1)S(1)}, u32[]{:S(2)}) copy-start(bf16[8,320,768]{2,1,0:T(8,128)(2,1)S(1)} %shard_map.113.keep_a.keep_b) | copy-start | bytes 11796484
  119.7 16.3 %collective-permute-start.7 = (bf16[2,4,160,384]{3,2,1,0:T(8,128)(2,1)}, bf16[2,4,160,384]{3,2,1,0:T(8,128)(2,1)}, u32[]{:S(2)}, u32[]{:S(2)}) collective-permute-start(bf16[2,4,160,384]{3,2,1,0:T(8,128)(2,1)} %get-tuple-element.19), channel_id=1, source_target_pairs={{0,16},{32,304},{16,0},{48,288},{256,272},{288,48},{272,256},{304,... | collective-permute-start | bytes 2949128 | tf_op jit(solution)/shard_map/ppermute | solution.py:394
  123.1 18.8 %collective-permute-start.3 = (bf16[2,2,160,768]{3,2,1,0:T(8,128)(2,1)}, bf16[2,2,160,768]{3,2,1,0:T(8,128)(2,1)}, u32[]{:S(2)}, u32[]{:S(2)}) collective-permute-start(bf16[2,2,160,768]{3,2,1,0:T(8,128)(2,1)} %get-tuple-element.17), channel_id=1, source_target_pairs={{0,64},{32,224},{64,0},{96,160},{128,192},{160,96},{192,128},{224,... | collective-permute-start | bytes 2949128 | tf_op jit(solution)/shard_map/ppermute | solution.py:394
  126.1 2.1 %copy-start.1 = (bf16[8,320,768]{2,1,0:T(8,128)(2,1)S(1)}, bf16[8,320,768]{2,1,0:T(8,128)(2,1)}, u32[]{:S(2)}) copy-start(bf16[8,320,768]{2,1,0:T(8,128)(2,1)} %copy-done) | copy-start | bytes 11796484
  131.0 1.0 copy-start.3
  132.0 4.0 %copy-start.5 = (bf16[2,4,160,384]{3,2,1,0:T(8,128)(2,1)}, bf16[2,4,160,384]{3,2,1,0:T(8,128)(2,1)S(1)}, u32[]{:S(2)}) copy-start(bf16[2,4,160,384]{3,2,1,0:T(8,128)(2,1)S(1)} %get-tuple-element.18) | copy-start | bytes 2949124
  136.0 19.2 %copy-start.4 = (bf16[2,2,160,768]{3,2,1,0:T(8,128)(2,1)S(1)}, bf16[2,2,160,768]{3,2,1,0:T(8,128)(2,1)}, u32[]{:S(2)}) copy-start(bf16[2,2,160,768]{3,2,1,0:T(8,128)(2,1)} %copy-done.3) | copy-start | bytes 2949124
  137.2 11.9 %collective-permute-start.8 = (bf16[4,160,384]{2,1,0:T(8,128)(2,1)S(1)}, bf16[4,160,384]{2,1,0:T(8,128)(2,1)S(1)}, u32[]{:S(2)}, u32[]{:S(2)}) collective-permute-start(bf16[4,160,384]{2,1,0:T(8,128)(2,1)S(1)} %fusion.9), channel_id=1, source_target_pairs={{0,272},{32,48},{16,256},{48,32},{256,16},{288,304},{272,0},{304,2... | collective-permute-start | bytes 1474568 | tf_op jit(solution)/shard_map/ppermute | solution.py:395
  143.2 11.9 %collective-permute-start.4 = (bf16[2,160,768]{2,1,0:T(8,128)(2,1)S(1)}, bf16[2,160,768]{2,1,0:T(8,128)(2,1)S(1)}, u32[]{:S(2)}, u32[]{:S(2)}) collective-permute-start(bf16[2,160,768]{2,1,0:T(8,128)(2,1)S(1)} %fusion.8), channel_id=1, source_target_pairs={{0,192},{32,96},{64,128},{96,32},{128,64},{160,224},{192,0},{224,1... | collective-permute-start | bytes 1474568 | tf_op jit(solution)/shard_map/ppermute | solution.py:395
  150.6 8.1 %collective-permute-start.9 = (bf16[2,160,384]{2,1,0:T(8,128)(2,1)S(1)}, bf16[2,160,384]{2,1,0:T(8,128)(2,1)S(1)}, u32[]{:S(2)}, u32[]{:S(2)}) collective-permute-start(bf16[2,160,384]{2,1,0:T(8,128)(2,1)S(1)} %pad_maximum_fusion.2), channel_id=1, source_target_pairs={{0,64},{32,224},{64,0},{96,160},{128,192},{160,96},{192,128},{224,... | collective-permute-start | bytes 737288 | tf_op jit(solution)/shard_map/ppermute | solution.py:394
  156.5 8.1 %collective-permute-start.5 = (bf16[2,160,384]{2,1,0:T(8,128)(2,1)S(1)}, bf16[2,160,384]{2,1,0:T(8,128)(2,1)S(1)}, u32[]{:S(2)}, u32[]{:S(2)}) collective-permute-start(bf16[2,160,384]{2,1,0:T(8,128)(2,1)S(1)} %pad_maximum_fusion.1), channel_id=1, source_target_pairs={{0,16},{32,304},{16,0},{48,288},{256,272},{288,48},{272,256},{304,... | collective-permute-start | bytes 737288 | tf_op jit(solution)/shard_map/ppermute | solution.py:394
  158.7 8.8 %collective-permute-start.10 = (bf16[160,384]{1,0:T(8,128)(2,1)S(1)}, bf16[160,384]{1,0:T(8,128)(2,1)S(1)}, u32[]{:S(2)}, u32[]{:S(2)}) collective-permute-start(bf16[160,384]{1,0:T(8,128)(2,1)S(1)} %fusion.14), channel_id=1, source_target_pairs={{0,192},{32,96},{64,128},{96,32},{128,64},{160,224},{192,0},{224,1... | collective-permute-start | bytes 368648 | tf_op jit(solution)/shard_map/ppermute | solution.py:395
  164.6 8.0 %collective-permute-start.6 = (bf16[160,384]{1,0:T(8,128)(2,1)S(1)}, bf16[160,384]{1,0:T(8,128)(2,1)S(1)}, u32[]{:S(2)}, u32[]{:S(2)}) collective-permute-start(bf16[160,384]{1,0:T(8,128)(2,1)S(1)} %fusion.10), channel_id=1, source_target_pairs={{0,272},{32,48},{16,256},{48,32},{256,16},{288,304},{272,0},{304,2... | collective-permute-start | bytes 368648 | tf_op jit(solution)/shard_map/ppermute | solution.py:395
Sparse Core Ops, SparseCore 0:
  10.1 86.0 all-gather.1
  108.8 70.3 reduce-scatter.1
